TPU v7x, 1024 devices: a whole 4x8x16 slice. The times are simulated.
1024 devices in a mesh: group: 64 (over y, x, core), expert: 16 (over z).
Axes of the slice: x: 4, y: 8, z: 16, core: 2. Of those that a mesh axis runs over, the one named last changes fastest.
Arguments:
- tokens: bfloat16 [256, 4, 1792], P('group', None, 'expert'), may hold values from -6 to 6
- out_grad: bfloat16 [256, 4, 1792], P('group', None, 'expert'), may hold values from -6 to 6
- route_weights: bfloat16 [256, 8], P('group'), may hold values from 0.049804688 to 0.5
- expert_ids: int32 [256, 8], P('group'), may hold values from 0 to 15, all different within a row; in each aligned block of 4 rows (0 to 3, 4 to 7, ...) at most 4 rows name the same one
- w_gate: bfloat16 [64, 1792, 2048], P('group', None, 'expert'), may hold values from -0.0625 to 0.0625
- w_up: bfloat16 [64, 1792, 2048], P('group', None, 'expert'), may hold values from -0.0625 to 0.0625
- w_down: bfloat16 [64, 2048, 1792], P('group', 'expert'), may hold values from -0.125 to 0.125
Outputs:
- token_grad: bfloat16 [256, 4, 1792], P('group', None, 'expert')
- down_grad: bfloat16 [64, 2048, 1792], P('group', 'expert')
- route_grad: float32 [256, 8], P('group')
Inputs may be any that keep to these rules, and one draw needn't show every extreme that they name: `expert_ids`: each row names 8 different experts; among the 4 rows of one index of group, no expert is named more than 4 times, a bound that some block reaches.
All inputs are finite; a program needn't handle non-finite values.
Results may differ from a plain program's by a relative error of at most 0.029.
Values may be sent and summed in bfloat16 or wider, within the bound.
No kernel may reach another device: no remote copies, remote signals or barrier semaphores. Data moves between devices by JAX's collectives and lax.ppermute only.
A program may use at most 32 MiB of HBM per device.

v0:
```python
import jax
import jax.numpy as jnp
from jax import lax
from jax.sharding import PartitionSpec as P

OWNERS = 4


def partner(block, axis, bit):
    count = lax.axis_size(axis)
    route = []
    for low in range(count):
        high = low | 1 << bit
        if high != low and high < count:
            route += [(low, high), (high, low)]
    return lax.ppermute(block, axis, route)


def placing_tensor(expert_ids, experts_win, capacity):
    onehot = (
        expert_ids.reshape(-1)[:, None] == jnp.arange(experts_win, dtype=jnp.int32)[None, :]
    ).astype(jnp.int32)
    slot_pos = jnp.sum((jnp.cumsum(onehot, axis=0) - 1) * onehot, axis=1)
    slot_hot = (slot_pos[:, None] == jnp.arange(capacity, dtype=jnp.int32)[None, :]).astype(
        jnp.int32
    )
    return (onehot[:, :, None] * slot_hot[:, None, :]).astype(jnp.bfloat16)


def finish_rows(stacked, weight_col):
    gate_pre = stacked[0]
    up_pre = stacked[1]
    hidden_grad = stacked[2]
    sigmoid_gate = jax.nn.sigmoid(gate_pre)
    hidden = (gate_pre * sigmoid_gate * up_pre).astype(jnp.bfloat16)
    route_part = jnp.sum(hidden.astype(jnp.float32) * hidden_grad, axis=1)
    scaled = weight_col * hidden_grad
    gate_grad = (scaled * up_pre * sigmoid_gate * (1.0 + gate_pre * (1.0 - sigmoid_gate))).astype(
        jnp.bfloat16
    )
    up_grad = (scaled * gate_pre * sigmoid_gate).astype(jnp.bfloat16)
    return (hidden, gate_grad, up_grad, route_part)


def body(tokens, out_grad, route_weights, expert_ids, w_gate, w_up, w_down):
    groups = lax.axis_size("group")
    experts_win = groups // OWNERS
    levels = OWNERS.bit_length() - 1
    tok_rows, top_count = expert_ids.shape
    capacity = min(tok_rows, 2 * tok_rows * top_count // experts_win)
    slot_rows = groups * capacity
    sub_width = tokens.shape[2]
    placing = placing_tensor(expert_ids, experts_win, capacity)
    weight_one = jnp.einsum(
        "pec,p->ec", placing, route_weights.reshape(-1), preferred_element_type=jnp.float32
    ).astype(jnp.bfloat16)
    weight_buf = jnp.broadcast_to(weight_one[:, None, :], (experts_win, OWNERS, capacity)).reshape(
        groups, capacity
    )
    in_buf = (
        jnp.einsum(
            "pec,pqw->eqcw",
            placing,
            jnp.repeat(tokens, top_count, axis=0),
            preferred_element_type=jnp.float32,
        )
        .astype(jnp.bfloat16)
        .reshape(groups, capacity, sub_width)
    )
    grad_buf = (
        jnp.einsum(
            "pec,pqw->eqcw",
            placing,
            jnp.repeat(out_grad, top_count, axis=0),
            preferred_element_type=jnp.float32,
        )
        .astype(jnp.bfloat16)
        .reshape(groups, capacity, sub_width)
    )
    recv_in, recv_grad, recv_weight = (
        lax.all_to_all(in_buf, "group", split_axis=0, concat_axis=0, tiled=True),
        lax.all_to_all(grad_buf, "group", split_axis=0, concat_axis=0, tiled=True),
        lax.all_to_all(weight_buf, "group", split_axis=0, concat_axis=0, tiled=True),
    )
    full_in, full_grad = (
        lax.all_gather(recv_in, "expert", axis=2, tiled=True),
        lax.all_gather(recv_grad, "expert", axis=2, tiled=True),
    )
    width = full_in.shape[2]
    slot_in = full_in.reshape(slot_rows, width)
    slot_grad = full_grad.reshape(slot_rows, width)
    weight_col = recv_weight.reshape(slot_rows, 1).astype(jnp.float32)
    gate_mat = w_gate[0]
    up_mat = w_up[0]
    down_mat = w_down[0]
    gate_part = jnp.dot(slot_in, gate_mat, preferred_element_type=jnp.float32)
    up_part = jnp.dot(slot_in, up_mat, preferred_element_type=jnp.float32)
    grad_part = lax.dot_general(
        slot_grad, down_mat, (((1,), (1,)), ((), ())), preferred_element_type=jnp.float32
    )
    stacked = jnp.stack([gate_part, up_part, grad_part])
    sums = stacked
    for bit_num in range(levels):
        sums = sums + partner(sums.astype(jnp.bfloat16), "group", bit_num).astype(sums.dtype)
    hidden, gate_grad, up_grad, route_part = finish_rows(sums, weight_col)
    weighted_hidden = (weight_col * hidden.astype(jnp.float32)).astype(jnp.bfloat16)
    down_grad = lax.dot_general(
        weighted_hidden, slot_grad, (((0,), (0,)), ((), ())), preferred_element_type=jnp.float32
    ).astype(jnp.bfloat16)
    input_part = lax.dot_general(
        gate_grad, gate_mat, (((1,), (1,)), ((), ())), preferred_element_type=jnp.float32
    )
    input_part = (
        input_part
        + lax.dot_general(
            up_grad, up_mat, (((1,), (1,)), ((), ())), preferred_element_type=jnp.float32
        )
    ).astype(jnp.bfloat16)
    input_sums = lax.psum_scatter(input_part, "expert", scatter_dimension=1, tiled=True).astype(
        jnp.float32
    )
    route_sums = lax.psum(route_part, "expert")
    back_input, back_route = (
        lax.all_to_all(
            input_sums.reshape(groups, capacity, sub_width).astype(jnp.bfloat16),
            "group",
            split_axis=0,
            concat_axis=0,
            tiled=True,
        ).astype(jnp.float32),
        lax.all_to_all(
            route_sums.reshape(groups, capacity).astype(jnp.bfloat16),
            "group",
            split_axis=0,
            concat_axis=0,
            tiled=True,
        ).astype(jnp.float32),
    )
    placing_f = placing.astype(jnp.float32)
    per_route = jnp.einsum(
        "pec,eqcw->pqw",
        placing_f,
        back_input.reshape(experts_win, OWNERS, capacity, sub_width),
        precision=lax.Precision.HIGHEST,
    )
    token_grad = jnp.sum(per_route.reshape(tok_rows, top_count, OWNERS, sub_width), axis=1).astype(
        jnp.bfloat16
    )
    route_rows = back_route.reshape(experts_win, OWNERS, capacity)[:, 0, :]
    route_grad = jnp.einsum(
        "pec,ec->p", placing_f, route_rows, precision=lax.Precision.HIGHEST
    ).reshape(tok_rows, top_count)
    return (token_grad, down_grad[None], route_grad)


def solution(mesh):
    return jax.shard_map(
        body,
        mesh=mesh,
        in_specs=(
            P("group", None, "expert"),
            P("group", None, "expert"),
            P("group", None),
            P("group", None),
            P("group", None, "expert"),
            P("group", None, "expert"),
            P("group", "expert", None),
        ),
        out_specs=(P("group", None, "expert"), P("group", "expert", None), P("group", None)),
        check_vma=False,
    )
```

profile of v0, /device:TPU:1, one launch (start us, length us, event | category | flops | bytes accessed | tf_op | source)
XLA Modules:
  0.0 258.4 jit_solution(14785301119792414005)
XLA Ops:
  7.2 0.8 eq.55
  8.2 0.2 select_reduce_fusion
  8.4 0.7 copy.51
  9.1 0.1 fusion.2
  9.3 0.7 copy.53
  9.9 18.2 %all-to-all-start.1 = ((bf16[64,4,112]{2,1,0:T(4,128)(2,1)}), bf16[64,4,112]{2,1,0:T(4,128)(2,1)S(1)}, u32[]{:S(2)}, u32[]{:S(2)}) async-start(bf16[64,4,112]{2,1,0:T(4,128)(2,1)} %copy.53), calls=%async_computation.1 | async-start | bytes 131072 | tf_op jit(solution)/shard_map/all_to_all | solution.py:81
  28.1 0.7 copy.56
  28.8 0.1 fusion.3
  29.0 0.7 copy.58
  29.7 8.6 %all-to-all-done.1 = bf16[64,4,112]{2,1,0:T(4,128)(2,1)S(1)} async-done(((bf16[64,4,112]{2,1,0:T(4,128)(2,1)}), bf16[64,4,112]{2,1,0:T(4,128)(2,1)S(1)}, u32[]{:S(2)}, u32[]{:S(2)}) %all-to-all-start.1) | async-done | bytes 57376 | tf_op jit(solution)/shard_map/all_to_all | solution.py:81
  38.3 4.4 %all-to-all-start.2 = ((bf16[64,4,112]{2,1,0:T(4,128)(2,1)}), bf16[64,4,112]{2,1,0:T(4,128)(2,1)S(1)}, u32[]{:S(2)}, u32[]{:S(2)}) async-start(bf16[64,4,112]{2,1,0:T(4,128)(2,1)} %copy.58), calls=%async_computation.2 | async-start | bytes 131072 | tf_op jit(solution)/shard_map/all_to_all | solution.py:82
  42.8 0.1 copy.54
  42.9 41.0 %all_gather.6 = bf16[64,4,1792]{0,1,2:T(4,128)(2,1)S(1)} all-gather(bf16[64,4,112]{0,1,2:T(4,128)(2,1)S(1)} %copy.54), channel_id=1, replica_groups=mesh['group'=64,'expert'=16] {'expert'}, dimensions={2}, use_global_device_ids=true | all-gather | bytes 974848 | tf_op jit(solution)/shard_map/all_gather | solution.py:86
  83.9 2.3 copy.55
  86.3 0.2 reshape.153
  86.5 0.8 copy-done.1
  87.3 0.5 convolution_bitcast_fusion.1
  87.7 0.5 convolution_bitcast_fusion.2
  88.2 0.1 copy.59
  88.4 33.1 %all_gather.7 = bf16[64,4,1792]{0,1,2:T(4,128)(2,1)S(1)} all-gather(bf16[64,4,112]{0,1,2:T(4,128)(2,1)S(1)} %copy.59), channel_id=1, replica_groups=mesh['group'=64,'expert'=16] {'expert'}, dimensions={2}, use_global_device_ids=true | all-gather | bytes 974848 | tf_op jit(solution)/shard_map/all_gather | solution.py:87
  121.4 2.3 copy.60
  123.8 0.2 reshape.156
  124.0 1.5 convolution_bitcast_fusion
  125.5 14.0 %collective-permute-start = (bf16[3,256,128]{1,2,0:T(8,128)(2,1)S(1)}, bf16[3,256,128]{1,2,0:T(8,128)(2,1)S(1)}, u32[]{:S(2)}, u32[]{:S(2)}) collective-permute-start(bf16[3,256,128]{1,2,0:T(8,128)(2,1)S(1)} %fusion.11), channel_id=1, source_target_pairs={{0,16},{16,0},{32,48},{48,32},{64,80},{80,64},{96,112},{112,96},{1... | collective-permute-start | bytes 589832 | tf_op jit(solution)/shard_map/ppermute | solution.py:16
  139.6 1.0 collective-permute-done
  140.6 4.7 %collective-permute-start.1 = (bf16[3,256,128]{1,2,0:T(8,128)(2,1)S(1)}, bf16[3,256,128]{1,2,0:T(8,128)(2,1)S(1)}, u32[]{:S(2)}, u32[]{:S(2)}) collective-permute-start(bf16[3,256,128]{1,2,0:T(8,128)(2,1)S(1)} %fusion.12), channel_id=1, source_target_pairs={{0,32},{32,0},{16,48},{48,16},{64,96},{96,64},{80,112},{112,80},{1... | collective-permute-start | bytes 589832 | tf_op jit(solution)/shard_map/ppermute | solution.py:16
  145.3 0.1 fusion.37
  145.5 0.1 all_to_all.19
  145.6 0.1 copy.50
  145.7 18.4 %all_to_all.30 = bf16[64,1,4]{2,1,0:T(2,128)(2,1)S(1)} all-to-all(bf16[64,1,4]{2,1,0:T(2,128)(2,1)S(1)} %copy.50), channel_id=1, replica_groups=mesh['group'=64,'expert'=16] {'group'}, dimensions={0} | all-to-all | bytes 1024 | tf_op jit(solution)/shard_map/all_to_all | solution.py:83
  164.2 0.1 convert_reduce_fusion
  164.3 0.1 reshape.159
  164.5 0.4 fusion.8
  164.9 0.4 copy-done.2
  165.3 1.3 fusion
  166.9 23.1 %psum.7 = bf16[256]{0:T(256)(128)(2,1)S(1)} all-reduce(f32[256]{0:T(256)S(1)} %fusion.13), channel_id=1, replica_groups=mesh['group'=64,'expert'=16] {'expert'}, use_global_device_ids=true, to_apply=%region_5.6 | all-reduce | flops 256 | bytes 1536 | tf_op jit(solution)/shard_map/psum | solution.py:122
  190.0 0.7 convert_element_type.160
  190.8 11.1 %all-to-all-start.4 = ((bf16[64,1,4]{2,1,0:T(2,128)(2,1)}), bf16[64,1,4]{2,1,0:T(2,128)(2,1)S(1)}, u32[]{:S(2)}, u32[]{:S(2)}) async-start(bf16[64,1,4]{2,1,0:T(2,128)(2,1)} %convert_element_type.160), calls=%async_computation.5 | async-start | bytes 65536 | tf_op jit(solution)/shard_map/all_to_all | solution.py:131
  201.9 1.1 fusion.1
  203.0 8.4 %all-to-all-done.4 = bf16[64,1,4]{2,1,0:T(2,128)(2,1)S(1)} async-done(((bf16[64,1,4]{2,1,0:T(2,128)(2,1)}), bf16[64,1,4]{2,1,0:T(2,128)(2,1)S(1)}, u32[]{:S(2)}, u32[]{:S(2)}) %all-to-all-start.4) | async-done | bytes 544 | tf_op jit(solution)/shard_map/all_to_all | solution.py:131
  211.4 0.1 copy.65
  211.5 0.1 reshape.158
  211.7 6.8 %reduce-scatter.2.cloned.1.call-done = bf16[256,112]{0,1:T(8,128)(2,1)} async-done(((bf16[256,1792]{0,1:T(8,128)(2,1)}), bf16[256,112]{0,1:T(8,128)(2,1)}) %reduce-scatter.2.cloned.1.call-update) | async-done | bytes 57360 | tf_op jit(solution)/shard_map/reduce_scatter | solution.py:119
  218.5 1.5 copy.61
  220.1 20.5 %all-to-all-start.3 = ((bf16[64,4,112]{2,1,0:T(4,128)(2,1)}), bf16[64,4,112]{2,1,0:T(4,128)(2,1)S(1)}, u32[]{:S(2)}, u32[]{:S(2)}) async-start(bf16[64,4,112]{2,1,0:T(4,128)(2,1)} %bitcast.22), calls=%async_computation.4 | async-start | bytes 131072 | tf_op jit(solution)/shard_map/all_to_all | solution.py:124
  240.6 0.8 fusion.27
  241.4 9.3 %all-to-all-done.3 = bf16[64,4,112]{2,1,0:T(4,128)(2,1)S(1)} async-done(((bf16[64,4,112]{2,1,0:T(4,128)(2,1)}), bf16[64,4,112]{2,1,0:T(4,128)(2,1)S(1)}, u32[]{:S(2)}, u32[]{:S(2)}) %all-to-all-start.3) | async-done | bytes 57376 | tf_op jit(solution)/shard_map/all_to_all | solution.py:124
  250.7 0.9 fusion.4
  (30 shorter events, 1.0 us)
Async XLA Ops:
  7.2 80.6 %copy-start = (bf16[1,1792,128]{2,1,0:T(8,128)(2,1)S(1)}, bf16[1,1792,128]{2,1,0:T(8,128)(2,1)}, u32[]{:S(2)}) copy-start(bf16[1,1792,128]{2,1,0:T(8,128)(2,1)} %param.11) | copy-start | bytes 1376260
  9.9 28.3 %all-to-all-start.1 = ((bf16[64,4,112]{2,1,0:T(4,128)(2,1)}), bf16[64,4,112]{2,1,0:T(4,128)(2,1)S(1)}, u32[]{:S(2)}, u32[]{:S(2)}) async-start(bf16[64,4,112]{2,1,0:T(4,128)(2,1)} %copy.53), calls=%async_computation.1 | async-start | bytes 131072 | tf_op jit(solution)/shard_map/all_to_all | solution.py:81
  38.3 49.9 %all-to-all-start.2 = ((bf16[64,4,112]{2,1,0:T(4,128)(2,1)}), bf16[64,4,112]{2,1,0:T(4,128)(2,1)S(1)}, u32[]{:S(2)}, u32[]{:S(2)}) async-start(bf16[64,4,112]{2,1,0:T(4,128)(2,1)} %copy.58), calls=%async_computation.2 | async-start | bytes 131072 | tf_op jit(solution)/shard_map/all_to_all | solution.py:82
  42.7 175.8 %reduce-scatter.2.cloned.1.call-start = ((), (), s32[]{:S(2)}) async-start(), calls=%async_computation.6 | async-start | bytes 974848 | tf_op jit(solution)/shard_map/reduce_scatter | solution.py:119
  86.3 1.0 copy-start.1
  123.8 15.7 %copy-start.4 = (bf16[4,8]{1,0:T(4,128)(2,1)S(1)}, bf16[4,8]{1,0:T(4,128)(2,1)}, u32[]{:S(2)}) copy-start(bf16[4,8]{1,0:T(4,128)(2,1)} %param.9) | copy-start | bytes 196
  125.5 15.0 %collective-permute-start = (bf16[3,256,128]{1,2,0:T(8,128)(2,1)S(1)}, bf16[3,256,128]{1,2,0:T(8,128)(2,1)S(1)}, u32[]{:S(2)}, u32[]{:S(2)}) collective-permute-start(bf16[3,256,128]{1,2,0:T(8,128)(2,1)S(1)} %fusion.11), channel_id=1, source_target_pairs={{0,16},{16,0},{32,48},{48,32},{64,80},{80,64},{96,112},{112,96},{1... | collective-permute-start | bytes 589832 | tf_op jit(solution)/shard_map/ppermute | solution.py:16
  140.6 23.8 %collective-permute-start.1 = (bf16[3,256,128]{1,2,0:T(8,128)(2,1)S(1)}, bf16[3,256,128]{1,2,0:T(8,128)(2,1)S(1)}, u32[]{:S(2)}, u32[]{:S(2)}) collective-permute-start(bf16[3,256,128]{1,2,0:T(8,128)(2,1)S(1)} %fusion.12), channel_id=1, source_target_pairs={{0,32},{32,0},{16,48},{48,16},{64,96},{96,64},{80,112},{112,80},{1... | collective-permute-start | bytes 589832 | tf_op jit(solution)/shard_map/ppermute | solution.py:16
  164.3 1.0 copy-start.2
  165.3 1.5 copy-start.3
  190.8 20.6 %all-to-all-start.4 = ((bf16[64,1,4]{2,1,0:T(2,128)(2,1)}), bf16[64,1,4]{2,1,0:T(2,128)(2,1)S(1)}, u32[]{:S(2)}, u32[]{:S(2)}) async-start(bf16[64,1,4]{2,1,0:T(2,128)(2,1)} %convert_element_type.160), calls=%async_computation.5 | async-start | bytes 65536 | tf_op jit(solution)/shard_map/all_to_all | solution.py:131
  220.1 30.6 %all-to-all-start.3 = ((bf16[64,4,112]{2,1,0:T(4,128)(2,1)}), bf16[64,4,112]{2,1,0:T(4,128)(2,1)S(1)}, u32[]{:S(2)}, u32[]{:S(2)}) async-start(bf16[64,4,112]{2,1,0:T(4,128)(2,1)} %bitcast.22), calls=%async_computation.4 | async-start | bytes 131072 | tf_op jit(solution)/shard_map/all_to_all | solution.py:124
Sparse Core Ops, SparseCore 0:
  166.8 51.6 reduce-scatter.1
where the time goes:
time: 259 us; the launch traced here: 258 us
  blocking collectives  116 us (45%)
  starting transfers between devices  73 us (28%)
  waiting for transfers between devices  34.1 us (13%)
  between operations  14.3 us (6%)
  local copies, waits for them, and re-layouts  13.4 us (5%)
  matrix products  7.38 us (3%)
    all_gather x1, blocking collectives, body(): lax.all_gather(recv_in, 'expert', axis=2, tiled=True)  41 us
    all_gather x1, blocking collectives, body(): lax.all_gather(recv_grad, 'expert', axis=2, tiled=True)  33.1 us
    psum x1, blocking collectives, body(): route_sums = lax.psum(route_part, 'expert')  23.1 us
    all_to_all x1, starting transfers between devices, body(): lax.all_to_all(input_sums.reshape(groups, capacity, sub_width).astype(jnp...  20.5 us
    ppermute x2, starting transfers between devices, partner(): return lax.ppermute(block, axis, route)  18.6 us
    all_to_all x1, blocking collectives, body(): lax.all_to_all(weight_buf, 'group', split_axis=0, concat_axis=0, tiled=True)  18.4 us
    all_to_all x1, starting transfers between devices, body(): lax.all_to_all(in_buf, 'group', split_axis=0, concat_axis=0, tiled=True)  18.2 us
    all_to_all x1, starting transfers between devices, body(): lax.all_to_all(route_sums.reshape(groups, capacity).astype(jnp.bfloat16),...  11.1 us
  transfers between devices with their start and end apart: 7, of which 5 were waited for; matrix products, arithmetic and copies ran while one was open for 3% of the time, Pallas kernels for 0%

commit v1 on v0

v1 whole, which is shorter than its diff:
```python
import jax
import jax.numpy as jnp
from jax import lax
from jax.sharding import Mesh, PartitionSpec as P

OWNERS = 4
LANES = 128


def split_hi_lo(v):
    hi = v.astype(jnp.bfloat16)
    lo = (v - hi.astype(jnp.float32)).astype(jnp.bfloat16)
    return hi, lo


def weight_table(expert_ids, route_weights, experts):
    onehot = expert_ids[:, :, None] == jnp.arange(experts, dtype=jnp.int32)[None, None, :]
    weights = jnp.where(onehot, route_weights.astype(jnp.float32)[:, :, None], 0.0)
    return jnp.sum(weights, axis=1).astype(jnp.bfloat16), onehot


def y_ring(block):
    count = lax.axis_size("y")
    up = [(i, (i + 1) % count) for i in range(count)]
    down = [((i + 1) % count, i) for i in range(count)]
    blocks = [None] * count
    blocks[0] = block
    fwd = bwd = block
    for step in range(1, count // 2 + 1):
        fwd = lax.ppermute(fwd, "y", up)
        blocks[(-step) % count] = fwd
        if step < count // 2:
            bwd = lax.ppermute(bwd, "y", down)
            blocks[step] = bwd
    return blocks


def body(tokens, out_grad, route_weights, expert_ids, w_gate, w_up, w_down):
    f32, bf16 = jnp.float32, jnp.bfloat16
    ny, nxh, nz = lax.axis_size("y"), lax.axis_size("xh"), lax.axis_size("z")
    experts = ny * nxh
    toks, _, sub = tokens.shape
    per_y = nxh * OWNERS
    groups = ny * per_y
    my_y = lax.axis_index("y")
    expert = my_y * nxh + lax.axis_index("xh")

    table, onehot = weight_table(expert_ids, route_weights, experts)
    x_rows = jnp.concatenate(
        [tokens.transpose(1, 0, 2), jnp.broadcast_to(table[None], (OWNERS, toks, experts))], axis=2
    )
    g_rows = jnp.pad(out_grad.transpose(1, 0, 2), ((0, 0), (0, 0), (0, LANES - sub)))
    send = jnp.concatenate([x_rows, g_rows], axis=1)
    send = jnp.broadcast_to(
        send[None, :, None], (nxh, OWNERS, nz, 2 * toks, LANES)
    ).reshape(nxh * OWNERS * nz, 2 * toks, LANES)
    got = lax.all_to_all(send, ("xh", "xl", "c", "z"), 0, 0, tiled=True)

    blocks = y_ring(got)

    gate_p = jnp.pad(w_gate[0].reshape(nz, sub, LANES), ((0, 0), (0, LANES - sub), (0, 0)))
    up_p = jnp.pad(w_up[0].reshape(nz, sub, LANES), ((0, 0), (0, LANES - sub), (0, 0)))
    gate_up = jnp.concatenate([gate_p, up_p], axis=2).reshape(nz * LANES, 2 * LANES)
    down_p = jnp.pad(w_down[0].reshape(LANES, nz, sub), ((0, 0), (0, 0), (0, LANES - sub)))
    down_p = down_p.reshape(LANES, nz * LANES)

    mats, parts = [], []
    for block in blocks:
        mat = (
            block.reshape(per_y, nz, 2 * toks, LANES)
            .transpose(0, 2, 1, 3)
            .reshape(per_y * 2 * toks, nz * LANES)
        )
        first = jnp.dot(mat, gate_up, preferred_element_type=f32)
        second = lax.dot_general(mat, down_p, (((1,), (1,)), ((), ())), preferred_element_type=f32)
        first = first.reshape(per_y, 2 * toks, 2 * LANES)[:, :toks]
        second = second.reshape(per_y, 2 * toks, LANES)[:, toks:]
        part = jnp.concatenate([first, second], axis=2).astype(bf16)
        mats.append(mat)
        parts.append(part.reshape(per_y * toks, 3 * LANES))
    rows = jnp.concatenate(mats, axis=0)
    part = jnp.concatenate(parts, axis=0)

    quad = lax.all_gather(part, ("xl", "c"), axis=0, tiled=False)
    sums = jnp.sum(quad.astype(f32), axis=0)
    gate_pre = sums[:, :LANES]
    up_pre = sums[:, LANES : 2 * LANES]
    hidden_grad = sums[:, 2 * LANES :]

    w_rows = rows[:, sub:LANES].reshape(ny * per_y, 2 * toks, experts)[:, :toks]
    mine = jnp.arange(experts, dtype=jnp.int32) == expert
    weight = jnp.sum(jnp.where(mine, w_rows.astype(f32), 0.0), axis=2).reshape(-1, 1)

    sig = jax.nn.sigmoid(gate_pre)
    hidden = (gate_pre * sig * up_pre).astype(bf16)
    route = jnp.sum(hidden.astype(f32) * hidden_grad, axis=1)
    scaled = weight * hidden_grad
    gate_grad = (scaled * up_pre * sig * (1.0 + gate_pre * (1.0 - sig))).astype(bf16)
    up_grad = (scaled * gate_pre * sig).astype(bf16)
    weighted = (weight * hidden.astype(f32)).astype(bf16)

    route_hi, route_lo = split_hi_lo(route)
    extra = jnp.stack([route_hi, route_lo], axis=1)
    small = jnp.concatenate([gate_grad, up_grad, jnp.pad(extra, ((0, 0), (0, LANES - 2)))], axis=1)
    small = small.reshape(ny, per_y * toks, 3 * LANES)
    small = lax.dynamic_slice_in_dim(
        jnp.concatenate([small, small], axis=0), lax.rem(ny - my_y, ny), ny, axis=0
    )
    small = small.reshape(groups, 1, toks, 3 * LANES)
    grads = small[..., : 2 * LANES]
    half = jnp.arange(2)
    lhs = jnp.where(
        (half[:, None] == half[None, :])[None, :, None, :, None],
        grads[:, :, :, None, :],
        jnp.zeros((), bf16),
    )
    lhs = jnp.broadcast_to(lhs, (groups, 2, toks, 2, 2 * LANES)).reshape(
        groups * 2 * toks, 4 * LANES
    )
    halves = gate_up.reshape(2, nz * LANES // 2, 2 * LANES).transpose(0, 2, 1)
    halves = halves.reshape(4 * LANES, nz * LANES // 2)
    back = jnp.dot(lhs, halves, preferred_element_type=f32)
    lane = jnp.arange(nz * LANES // 2, dtype=jnp.int32)
    hi_col = jnp.broadcast_to(
        small[..., 2 * LANES : 2 * LANES + 1], (groups, 2, toks, 1)
    ).reshape(-1, 1)
    lo_col = jnp.broadcast_to(
        small[..., 2 * LANES + 1 : 2 * LANES + 2], (groups, 2, toks, 1)
    ).reshape(-1, 1)
    back = jnp.where(
        lane == sub, hi_col.astype(f32), jnp.where(lane == sub + 1, lo_col.astype(f32), back)
    )
    back = back.astype(bf16).reshape(groups, 2 * toks, nz * LANES // 2)
    landed = lax.all_to_all(back, ("y", "xh", "xl", "c"), 0, 0, tiled=True)

    wide = jnp.pad(
        weighted.reshape(groups, toks, LANES), ((0, 0), (0, toks), (0, 0)), constant_values=0
    )
    g_only = jnp.concatenate([wide[:, toks:], wide[:, :toks]], axis=1).reshape(-1, LANES)
    down_grad = lax.dot_general(
        g_only, rows, (((0,), (0,)), ((), ())), preferred_element_type=f32
    ).astype(bf16)
    down_grad = down_grad.reshape(LANES, nz, LANES)[:, :, :sub].reshape(1, LANES, nz * sub)

    landed = landed.reshape(experts, OWNERS, 2 * toks, nz * LANES // 2).astype(f32)
    summed = jnp.sum(landed, axis=0)
    route_part = landed[:, 0, :toks, sub] + landed[:, 0, :toks, sub + 1]
    part_hi, part_lo = split_hi_lo(route_part.T)
    zero = jnp.zeros_like(part_hi)
    pad_rows = jnp.concatenate([part_hi, part_lo, zero, zero], axis=0)
    pieces = (
        summed.astype(bf16)
        .reshape(OWNERS, 2, toks, nz // 2, LANES)
        .transpose(1, 3, 0, 2, 4)
        .reshape(nz, OWNERS * toks, LANES)
    )
    pieces = jnp.concatenate(
        [pieces[..., :sub], jnp.broadcast_to(pad_rows[None], (nz, OWNERS * toks, experts))], axis=2
    )
    final = lax.all_to_all(pieces, "z", 0, 0, tiled=True)
    final = jnp.sum(final.astype(f32), axis=0)
    token_grad = final[:, :sub].reshape(OWNERS, toks, sub).transpose(1, 0, 2).astype(bf16)
    routes = final[:toks, sub:] + final[toks : 2 * toks, sub:]
    route_grad = jnp.sum(jnp.where(onehot, routes[:, None, :], 0.0), axis=2)
    return token_grad, down_grad, route_grad


def solution(mesh):
    fine = Mesh(
        mesh.devices.reshape(-1, 2, 2, 2, mesh.devices.shape[1]), ("y", "xh", "xl", "c", "z")
    )
    group = ("y", "xh", "xl", "c")
    return jax.shard_map(
        body,
        mesh=fine,
        in_specs=(
            P(group, None, "z"),
            P(group, None, "z"),
            P(group, None),
            P(group, None),
            P(group, None, "z"),
            P(group, None, "z"),
            P(group, "z", None),
        ),
        out_specs=(P(group, None, "z"), P(group, "z", None), P(group, None)),
        check_vma=False,
    )
```

time: 259 us -> 176 us (0.68)
  blocking collectives: 116 us -> 11 us
  waiting for transfers between devices: 34.1 us -> 81.2 us
  starting transfers between devices: 73 us -> 54.2 us
  between operations: 14.3 us -> 1.33 us
  other arithmetic: 0.69 us -> 5.08 us
    all_gather x2 -> x1, blocking collectives: 74 us -> 11 us  [body(): quad = lax.all_gather(part, ('xl', 'c'), axis=0, tiled=False)]
    all_to_all x4 -> x3, waiting for transfers between devices: 26.2 us -> 57.7 us  [the longest x1 27.9 us: body(): landed = lax.all_to_all(back, ('y', 'xh', 'xl', 'c'), 0, 0, tiled=True)]
    psum x1 -> x0, blocking collectives: 23.1 us -> none  [body(): route_sums = lax.psum(route_part, 'expert')]
    ppermute x2 -> x7, waiting for transfers between devices: 0.96 us -> 23.5 us  [the longest x4 15.1 us: y_ring(): fwd = lax.ppermute(fwd, 'y', up)]
    all_to_all x4 -> x3, starting transfers between devices: 54.3 us -> 34.7 us  [the longest x1 24.1 us: body(): got = lax.all_to_all(send, ('xh', 'xl', 'c', 'z'), 0, 0, tiled=True)]
    all_to_all x1 -> x0, blocking collectives: 18.4 us -> none  [body(): lax.all_to_all(weight_buf, 'group', split_axis=0, concat_axis=0, tiled=True)]
    reduce_scatter x1 -> x0, waiting for transfers between devices: 6.84 us -> none  [body(): lax.psum_scatter(input_part, 'expert', scatter_dimension=1, tiled=True)]
    unnamed x12 -> x25, local copies, waits for them, and re-layouts: 2.6 us -> 8.34 us
  transfers between devices with their start and end apart: 7 -> 10, of which waited for: 5 -> 10; matrix products, arithmetic and copies ran while one was open for 3% -> 5% of each run, Pallas kernels for 0% -> 0%
where the time goes in v1:
time: 176 us; the launch traced here: 175 us
  waiting for transfers between devices  81.2 us (46%)
  starting transfers between devices  54.2 us (31%)
  local copies, waits for them, and re-layouts  15 us (9%)
  blocking collectives  11 us (6%)
  matrix products  6.87 us (4%)
  other arithmetic  5.08 us (3%)
    all_to_all x1, waiting for transfers between devices, body(): landed = lax.all_to_all(back, ('y', 'xh', 'xl', 'c'), 0, 0, tiled=True)  27.9 us
    all_to_all x1, starting transfers between devices, body(): got = lax.all_to_all(send, ('xh', 'xl', 'c', 'z'), 0, 0, tiled=True)  24.1 us
    all_to_all x1, waiting for transfers between devices, body(): got = lax.all_to_all(send, ('xh', 'xl', 'c', 'z'), 0, 0, tiled=True)  20 us
    ppermute x4, waiting for transfers between devices, y_ring(): fwd = lax.ppermute(fwd, 'y', up)  15.1 us
    all_gather x1, blocking collectives, body(): quad = lax.all_gather(part, ('xl', 'c'), axis=0, tiled=False)  11 us
    ppermute x4, starting transfers between devices, y_ring(): fwd = lax.ppermute(fwd, 'y', up)  10.6 us
    all_to_all x1, waiting for transfers between devices, body(): final = lax.all_to_all(pieces, 'z', 0, 0, tiled=True)  9.79 us
    ppermute x3, starting transfers between devices, y_ring(): bwd = lax.ppermute(bwd, 'y', down)  8.93 us
  transfers between devices with their start and end apart: 10, of which 10 were waited for; matrix products, arithmetic and copies ran while one was open for 5% of the time, Pallas kernels for 0%

profile of v1, /device:TPU:1, one launch (start us, length us, event | category | flops | bytes accessed | tf_op | source)
XLA Modules:
  0.0 174.6 jit_solution(14808549566238984185)
XLA Ops:
  0.7 0.8 convert_element_type.152
  1.4 0.8 select_reduce_fusion.2
  2.3 0.7 fusion.36
  3.0 0.7 broadcast_in_dim.113
  3.7 24.1 %all-to-all-start = ((bf16[128,8,128]{2,1,0:T(8,128)(2,1)}), bf16[128,8,128]{2,1,0:T(8,128)(2,1)S(1)}, u32[]{:S(2)}, u32[]{:S(2)}) async-start(bf16[128,8,128]{2,1,0:T(8,128)(2,1)} %bitcast.2), calls=%async_computation | async-start | bytes 524288 | tf_op jit(solution)/shard_map/all_to_all | solution.py:57
  27.8 1.3 copy.106
  29.5 1.3 copy.113
  30.9 20.0 %all-to-all-done = bf16[128,8,128]{2,1,0:T(8,128)(2,1)S(1)} async-done(((bf16[128,8,128]{2,1,0:T(8,128)(2,1)}), bf16[128,8,128]{2,1,0:T(8,128)(2,1)S(1)}, u32[]{:S(2)}, u32[]{:S(2)}) %all-to-all-start) | async-done | bytes 262176 | tf_op jit(solution)/shard_map/all_to_all | solution.py:57
  51.6 5.1 %collective-permute-start = (bf16[128,8,128]{2,1,0:T(8,128)(2,1)S(1)}, bf16[128,8,128]{2,1,0:T(8,128)(2,1)S(1)}, u32[]{:S(2)}, u32[]{:S(2)}) collective-permute-start(bf16[128,8,128]{2,1,0:T(8,128)(2,1)S(1)} %all-to-all-done), channel_id=1, source_target_pairs={{128,0},{256,128},{384,256},{512,384},{640,512},{768,640},{896,768... | collective-permute-start | bytes 786440 | tf_op jit(solution)/shard_map/ppermute | solution.py:33
  56.7 1.9 %collective-permute-start.3 = (bf16[128,8,128]{2,1,0:T(8,128)(2,1)S(1)}, bf16[128,8,128]{2,1,0:T(8,128)(2,1)S(1)}, u32[]{:S(2)}, u32[]{:S(2)}) collective-permute-start(bf16[128,8,128]{2,1,0:T(8,128)(2,1)S(1)} %all-to-all-done), channel_id=1, source_target_pairs={{0,128},{128,256},{256,384},{384,512},{512,640},{640,768},{768,896... | collective-permute-start | bytes 786440 | tf_op jit(solution)/shard_map/ppermute | solution.py:30
  58.6 0.7 constant_dynamic-update-slice_fusion.7
  59.3 3.4 %collective-permute-done = bf16[128,8,128]{2,1,0:T(8,128)(2,1)S(1)} collective-permute-done((bf16[128,8,128]{2,1,0:T(8,128)(2,1)S(1)}, bf16[128,8,128]{2,1,0:T(8,128)(2,1)S(1)}, u32[]{:S(2)}, u32[]{:S(2)}) %collective-permute-start) | collective-permute-done | bytes 262176 | tf_op jit(solution)/shard_map/ppermute | solution.py:33
  63.1 0.3 convolution_bitcast_fusion.6
  63.4 4.5 %collective-permute-done.3 = bf16[128,8,128]{2,1,0:T(8,128)(2,1)S(1)} collective-permute-done((bf16[128,8,128]{2,1,0:T(8,128)(2,1)S(1)}, bf16[128,8,128]{2,1,0:T(8,128)(2,1)S(1)}, u32[]{:S(2)}, u32[]{:S(2)}) %collective-permute-start.3) | collective-permute-done | bytes 262176 | tf_op jit(solution)/shard_map/ppermute | solution.py:30
  67.8 0.3 convolution_bitcast_fusion.8
  68.1 0.3 convolution_bitcast_fusion
  68.5 1.9 %collective-permute-start.1 = (bf16[128,8,128]{2,1,0:T(8,128)(2,1)S(1)}, bf16[128,8,128]{2,1,0:T(8,128)(2,1)S(1)}, u32[]{:S(2)}, u32[]{:S(2)}) collective-permute-start(bf16[128,8,128]{2,1,0:T(8,128)(2,1)S(1)} %collective-permute-done), channel_id=1, source_target_pairs={{128,0},{256,128},{384,256},{512,384},{640,512},{768,640},{896,768... | collective-permute-start | bytes 786440 | tf_op jit(solution)/shard_map/ppermute | solution.py:33
  70.5 3.4 %collective-permute-start.4 = (bf16[128,8,128]{2,1,0:T(8,128)(2,1)S(1)}, bf16[128,8,128]{2,1,0:T(8,128)(2,1)S(1)}, u32[]{:S(2)}, u32[]{:S(2)}) collective-permute-start(bf16[128,8,128]{2,1,0:T(8,128)(2,1)S(1)} %collective-permute-done.3), channel_id=1, source_target_pairs={{0,128},{128,256},{256,384},{384,512},{512,640},{640,768},{768,896... | collective-permute-start | bytes 786440 | tf_op jit(solution)/shard_map/ppermute | solution.py:30
  73.8 0.7 constant_dynamic-update-slice_fusion.6
  74.5 3.0 %collective-permute-done.1 = bf16[128,8,128]{2,1,0:T(8,128)(2,1)S(1)} collective-permute-done((bf16[128,8,128]{2,1,0:T(8,128)(2,1)S(1)}, bf16[128,8,128]{2,1,0:T(8,128)(2,1)S(1)}, u32[]{:S(2)}, u32[]{:S(2)}) %collective-permute-start.1) | collective-permute-done | bytes 262176 | tf_op jit(solution)/shard_map/ppermute | solution.py:33
  78.1 2.5 %collective-permute-done.4 = bf16[128,8,128]{2,1,0:T(8,128)(2,1)S(1)} collective-permute-done((bf16[128,8,128]{2,1,0:T(8,128)(2,1)S(1)}, bf16[128,8,128]{2,1,0:T(8,128)(2,1)S(1)}, u32[]{:S(2)}, u32[]{:S(2)}) %collective-permute-start.4) | collective-permute-done | bytes 262176 | tf_op jit(solution)/shard_map/ppermute | solution.py:30
  80.6 0.3 convolution_bitcast_fusion.9
  80.9 0.3 convolution_bitcast_fusion.1
  81.2 1.9 %collective-permute-start.2 = (bf16[128,8,128]{2,1,0:T(8,128)(2,1)S(1)}, bf16[128,8,128]{2,1,0:T(8,128)(2,1)S(1)}, u32[]{:S(2)}, u32[]{:S(2)}) collective-permute-start(bf16[128,8,128]{2,1,0:T(8,128)(2,1)S(1)} %collective-permute-done.1), channel_id=1, source_target_pairs={{128,0},{256,128},{384,256},{512,384},{640,512},{768,640},{896,768... | collective-permute-start | bytes 786440 | tf_op jit(solution)/shard_map/ppermute | solution.py:33
  83.2 3.4 %collective-permute-start.5 = (bf16[128,8,128]{2,1,0:T(8,128)(2,1)S(1)}, bf16[128,8,128]{2,1,0:T(8,128)(2,1)S(1)}, u32[]{:S(2)}, u32[]{:S(2)}) collective-permute-start(bf16[128,8,128]{2,1,0:T(8,128)(2,1)S(1)} %collective-permute-done.4), channel_id=1, source_target_pairs={{0,128},{128,256},{256,384},{384,512},{512,640},{640,768},{768,896... | collective-permute-start | bytes 786440 | tf_op jit(solution)/shard_map/ppermute | solution.py:30
  86.6 0.7 constant_dynamic-update-slice_fusion.5
  87.3 1.9 %collective-permute-done.2 = bf16[128,8,128]{2,1,0:T(8,128)(2,1)S(1)} collective-permute-done((bf16[128,8,128]{2,1,0:T(8,128)(2,1)S(1)}, bf16[128,8,128]{2,1,0:T(8,128)(2,1)S(1)}, u32[]{:S(2)}, u32[]{:S(2)}) %collective-permute-start.2) | collective-permute-done | bytes 262176 | tf_op jit(solution)/shard_map/ppermute | solution.py:33
  89.8 2.6 %collective-permute-done.5 = bf16[128,8,128]{2,1,0:T(8,128)(2,1)S(1)} collective-permute-done((bf16[128,8,128]{2,1,0:T(8,128)(2,1)S(1)}, bf16[128,8,128]{2,1,0:T(8,128)(2,1)S(1)}, u32[]{:S(2)}, u32[]{:S(2)}) %collective-permute-start.5) | collective-permute-done | bytes 262176 | tf_op jit(solution)/shard_map/ppermute | solution.py:30
  93.1 1.9 %collective-permute-start.6 = (bf16[128,8,128]{2,1,0:T(8,128)(2,1)S(1)}, bf16[128,8,128]{2,1,0:T(8,128)(2,1)S(1)}, u32[]{:S(2)}, u32[]{:S(2)}) collective-permute-start(bf16[128,8,128]{2,1,0:T(8,128)(2,1)S(1)} %collective-permute-done.5), channel_id=1, source_target_pairs={{0,128},{128,256},{256,384},{384,512},{512,640},{640,768},{768,896... | collective-permute-start | bytes 786440 | tf_op jit(solution)/shard_map/ppermute | solution.py:30
  95.0 0.7 constant_dynamic-update-slice_fusion.4
  95.8 5.6 %collective-permute-done.6 = bf16[128,8,128]{2,1,0:T(8,128)(2,1)S(1)} collective-permute-done((bf16[128,8,128]{2,1,0:T(8,128)(2,1)S(1)}, bf16[128,8,128]{2,1,0:T(8,128)(2,1)S(1)}, u32[]{:S(2)}, u32[]{:S(2)}) %collective-permute-start.6) | collective-permute-done | bytes 262176 | tf_op jit(solution)/shard_map/ppermute | solution.py:30
  102.0 0.7 constant_dynamic-update-slice_fusion.3
  102.7 0.7 constant_dynamic-update-slice_fusion.2
  103.5 0.7 constant_dynamic-update-slice_fusion.1
  104.2 0.7 constant_dynamic-update-slice_fusion
  104.9 1.0 slice_bitcast_fusion.1
  106.4 11.0 %all-gather = bf16[1024,384]{1,0:T(8,128)(2,1)S(1)} all-gather(bf16[256,384]{1,0:T(8,128)(2,1)S(1)} %constant_dynamic-update-slice_fusion.8), channel_id=2, replica_groups=mesh['y'=8,'xh'=2,'xl'=2,'c'=2,'z'=16] {'xl','c'}, dimensions={0}, use_global_device_ids=true | all-gather | bytes 983040 | tf_op jit(solution)/shard_map/all_gather | solution.py:84
  118.3 0.5 broadcast_select_fusion
  119.7 1.7 fusion.2
  121.4 7.1 %all-to-all-start.1 = ((bf16[64,8,1024]{2,1,0:T(8,128)(2,1)}), bf16[64,8,1024]{2,1,0:T(8,128)(2,1)S(1)}, u32[]{:S(2)}, u32[]{:S(2)}) async-start(bf16[64,8,1024]{2,1,0:T(8,128)(2,1)} %fusion.2), calls=%async_computation.1 | async-start | bytes 2097152 | tf_op jit(solution)/shard_map/all_to_all | solution.py:134
  128.6 27.9 %all-to-all-done.1 = bf16[64,8,1024]{2,1,0:T(8,128)(2,1)S(1)} async-done(((bf16[64,8,1024]{2,1,0:T(8,128)(2,1)}), bf16[64,8,1024]{2,1,0:T(8,128)(2,1)S(1)}, u32[]{:S(2)}, u32[]{:S(2)}) %all-to-all-start.1) | async-done | bytes 1048608 | tf_op jit(solution)/shard_map/all_to_all | solution.py:134
  157.4 0.6 copy.116
  158.1 3.5 %all-to-all-start.2 = ((bf16[16,16,128]{2,1,0:T(8,128)(2,1)}), bf16[16,16,128]{2,1,0:T(8,128)(2,1)S(1)}, u32[]{:S(2)}, u32[]{:S(2)}) async-start(bf16[16,16,128]{2,1,0:T(8,128)(2,1)} %copy.116), calls=%async_computation.2 | async-start | bytes 131072 | tf_op jit(solution)/shard_map/all_to_all | solution.py:160
  161.6 0.5 convolution_convert_fusion
  162.4 1.0 copy.119
  163.4 9.8 %all-to-all-done.2 = bf16[16,16,128]{2,1,0:T(8,128)(2,1)S(1)} async-done(((bf16[16,16,128]{2,1,0:T(8,128)(2,1)}), bf16[16,16,128]{2,1,0:T(8,128)(2,1)S(1)}, u32[]{:S(2)}, u32[]{:S(2)}) %all-to-all-start.2) | async-done | bytes 65568 | tf_op jit(solution)/shard_map/all_to_all | solution.py:160
  173.3 0.6 copy.118
  173.9 0.7 select_reduce_fusion.1
  (103 shorter events, 7.5 us)
Async XLA Ops:
  0.6 28.8 %copy-start.2 = (bf16[1,1792,128]{2,1,0:T(8,128)(2,1)S(1)}, bf16[1,1792,128]{2,1,0:T(8,128)(2,1)}, u32[]{:S(2)}) copy-start(bf16[1,1792,128]{2,1,0:T(8,128)(2,1)} %param.12) | copy-start | bytes 1376260
  0.6 28.8 %copy-start.3 = (bf16[1,1792,128]{2,1,0:T(8,128)(2,1)S(1)}, bf16[1,1792,128]{2,1,0:T(8,128)(2,1)}, u32[]{:S(2)}) copy-start(bf16[1,1792,128]{2,1,0:T(8,128)(2,1)} %param.11) | copy-start | bytes 1376260
  3.7 47.2 %all-to-all-start = ((bf16[128,8,128]{2,1,0:T(8,128)(2,1)}), bf16[128,8,128]{2,1,0:T(8,128)(2,1)S(1)}, u32[]{:S(2)}, u32[]{:S(2)}) async-start(bf16[128,8,128]{2,1,0:T(8,128)(2,1)} %bitcast.2), calls=%async_computation | async-start | bytes 524288 | tf_op jit(solution)/shard_map/all_to_all | solution.py:57
  51.6 11.2 %collective-permute-start = (bf16[128,8,128]{2,1,0:T(8,128)(2,1)S(1)}, bf16[128,8,128]{2,1,0:T(8,128)(2,1)S(1)}, u32[]{:S(2)}, u32[]{:S(2)}) collective-permute-start(bf16[128,8,128]{2,1,0:T(8,128)(2,1)S(1)} %all-to-all-done), channel_id=1, source_target_pairs={{128,0},{256,128},{384,256},{512,384},{640,512},{768,640},{896,768... | collective-permute-start | bytes 786440 | tf_op jit(solution)/shard_map/ppermute | solution.py:33
  56.7 11.1 %collective-permute-start.3 = (bf16[128,8,128]{2,1,0:T(8,128)(2,1)S(1)}, bf16[128,8,128]{2,1,0:T(8,128)(2,1)S(1)}, u32[]{:S(2)}, u32[]{:S(2)}) collective-permute-start(bf16[128,8,128]{2,1,0:T(8,128)(2,1)S(1)} %all-to-all-done), channel_id=1, source_target_pairs={{0,128},{128,256},{256,384},{384,512},{512,640},{640,768},{768,896... | collective-permute-start | bytes 786440 | tf_op jit(solution)/shard_map/ppermute | solution.py:30
  68.5 9.1 %collective-permute-start.1 = (bf16[128,8,128]{2,1,0:T(8,128)(2,1)S(1)}, bf16[128,8,128]{2,1,0:T(8,128)(2,1)S(1)}, u32[]{:S(2)}, u32[]{:S(2)}) collective-permute-start(bf16[128,8,128]{2,1,0:T(8,128)(2,1)S(1)} %collective-permute-done), channel_id=1, source_target_pairs={{128,0},{256,128},{384,256},{512,384},{640,512},{768,640},{896,768... | collective-permute-start | bytes 786440 | tf_op jit(solution)/shard_map/ppermute | solution.py:33
  70.5 10.1 %collective-permute-start.4 = (bf16[128,8,128]{2,1,0:T(8,128)(2,1)S(1)}, bf16[128,8,128]{2,1,0:T(8,128)(2,1)S(1)}, u32[]{:S(2)}, u32[]{:S(2)}) collective-permute-start(bf16[128,8,128]{2,1,0:T(8,128)(2,1)S(1)} %collective-permute-done.3), channel_id=1, source_target_pairs={{0,128},{128,256},{256,384},{384,512},{512,640},{640,768},{768,896... | collective-permute-start | bytes 786440 | tf_op jit(solution)/shard_map/ppermute | solution.py:30
  81.2 8.0 %collective-permute-start.2 = (bf16[128,8,128]{2,1,0:T(8,128)(2,1)S(1)}, bf16[128,8,128]{2,1,0:T(8,128)(2,1)S(1)}, u32[]{:S(2)}, u32[]{:S(2)}) collective-permute-start(bf16[128,8,128]{2,1,0:T(8,128)(2,1)S(1)} %collective-permute-done.1), channel_id=1, source_target_pairs={{128,0},{256,128},{384,256},{512,384},{640,512},{768,640},{896,768... | collective-permute-start | bytes 786440 | tf_op jit(solution)/shard_map/ppermute | solution.py:33
  83.2 9.2 %collective-permute-start.5 = (bf16[128,8,128]{2,1,0:T(8,128)(2,1)S(1)}, bf16[128,8,128]{2,1,0:T(8,128)(2,1)S(1)}, u32[]{:S(2)}, u32[]{:S(2)}) collective-permute-start(bf16[128,8,128]{2,1,0:T(8,128)(2,1)S(1)} %collective-permute-done.4), channel_id=1, source_target_pairs={{0,128},{128,256},{256,384},{384,512},{512,640},{640,768},{768,896... | collective-permute-start | bytes 786440 | tf_op jit(solution)/shard_map/ppermute | solution.py:30
  93.1 8.3 %collective-permute-start.6 = (bf16[128,8,128]{2,1,0:T(8,128)(2,1)S(1)}, bf16[128,8,128]{2,1,0:T(8,128)(2,1)S(1)}, u32[]{:S(2)}, u32[]{:S(2)}) collective-permute-start(bf16[128,8,128]{2,1,0:T(8,128)(2,1)S(1)} %collective-permute-done.5), channel_id=1, source_target_pairs={{0,128},{128,256},{256,384},{384,512},{512,640},{640,768},{768,896... | collective-permute-start | bytes 786440 | tf_op jit(solution)/shard_map/ppermute | solution.py:30
  117.7 2.0 %copy-start.1 = (bf16[2,1024,256]{1,2,0:T(8,128)(2,1)S(1)}, bf16[2,1024,256]{1,2,0:T(8,128)(2,1)}, u32[]{:S(2)}) copy-start(bf16[2,1024,256]{1,2,0:T(8,128)(2,1)} %copy.113) | copy-start | bytes 3145732
  121.4 35.1 %all-to-all-start.1 = ((bf16[64,8,1024]{2,1,0:T(8,128)(2,1)}), bf16[64,8,1024]{2,1,0:T(8,128)(2,1)S(1)}, u32[]{:S(2)}, u32[]{:S(2)}) async-start(bf16[64,8,1024]{2,1,0:T(8,128)(2,1)} %fusion.2), calls=%async_computation.1 | async-start | bytes 2097152 | tf_op jit(solution)/shard_map/all_to_all | solution.py:134
  128.6 32.9 %copy-start = (bf16[512,2048]{1,0:T(8,128)(2,1)S(1)}, bf16[512,2048]{1,0:T(8,128)(2,1)}, u32[]{:S(2)}) copy-start(bf16[512,2048]{1,0:T(8,128)(2,1)} %constant_dynamic-update-slice_fusion) | copy-start | bytes 6291460
  158.1 15.1 %all-to-all-start.2 = ((bf16[16,16,128]{2,1,0:T(8,128)(2,1)}), bf16[16,16,128]{2,1,0:T(8,128)(2,1)S(1)}, u32[]{:S(2)}, u32[]{:S(2)}) async-start(bf16[16,16,128]{2,1,0:T(8,128)(2,1)} %copy.116), calls=%async_computation.2 | async-start | bytes 131072 | tf_op jit(solution)/shard_map/all_to_all | solution.py:160
  162.1 11.8 %copy-start.4 = (s32[4,8]{1,0:T(4,128)S(1)}, s32[4,8]{1,0:T(4,128)}, u32[]{:S(2)}) copy-start(s32[4,8]{1,0:T(4,128)} %param.10) | copy-start | bytes 388

commit v2 on v1

v2 whole, which is shorter than its diff:
```python
import functools

import jax
import jax.numpy as jnp
from jax import lax
from jax.experimental import pallas as pl
from jax.experimental.pallas import tpu as pltpu
from jax.sharding import Mesh, PartitionSpec as P

OWNERS = 4
LANES = 128


VMEM_LIMIT = 40 * 1024 * 1024


def hi_lo(v):
    hi = v.astype(jnp.bfloat16).astype(jnp.float32)
    return hi, v - hi


def call(kernel, out_shape, in_specs, scratch, flops, moved):
    return pl.pallas_call(
        kernel,
        out_shape=out_shape,
        in_specs=in_specs,
        out_specs=jax.tree.map(lambda _: pl.BlockSpec(memory_space=pltpu.VMEM), out_shape),
        scratch_shapes=scratch,
        compiler_params=pltpu.CompilerParams(vmem_limit_bytes=VMEM_LIMIT),
        cost_estimate=pl.CostEstimate(flops=flops, bytes_accessed=moved, transcendentals=0),
    )


def whole(count):
    return [pl.BlockSpec(memory_space=pltpu.VMEM)] * count


def upper(shape):
    return lax.broadcasted_iota(jnp.int32, shape, len(shape) - 2) >= 4


def swap(v):
    return pltpu.roll(v, 4, axis=v.ndim - 2)


def first_fours(v):
    pairs = v.reshape(v.shape[0] // 16, 2, 8, v.shape[1])
    even, odd = pairs[:, 0], pairs[:, 1]
    return jnp.where(upper(even.shape), swap(odd), even).reshape(-1, v.shape[1])


def last_fours(v):
    pairs = v.reshape(v.shape[0] // 16, 2, 8, v.shape[1])
    even, odd = pairs[:, 0], pairs[:, 1]
    return jnp.where(upper(even.shape), odd, swap(even)).reshape(-1, v.shape[1])


def lay_rows(my_y, blocks, rows):
    count = len(blocks)
    for index, block in enumerate(blocks):
        per_y, nz, tall, _ = block.shape
        size = per_y * tall
        base = pl.multiple_of(lax.rem(my_y + index, count) * size, size)
        for z in range(nz):
            tile = block[:, z].astype(jnp.float32).reshape(size, LANES).astype(jnp.bfloat16)
            rows[pl.ds(base, size), z * LANES : (z + 1) * LANES] = tile


def part_kernel(place, *refs):
    *blocks, gate_up, down, part, weight, rows = refs
    f32 = jnp.float32
    lay_rows(place[0], blocks, rows)
    mat = rows[...]
    first = jnp.dot(mat, gate_up[...], preferred_element_type=f32)
    second = lax.dot_general(mat, down[...], (((1,), (1,)), ((), ())), preferred_element_type=f32)
    part[:, : 2 * LANES] = first_fours(first).astype(part.dtype)
    part[:, 2 * LANES :] = last_fours(second).astype(part.dtype)
    tags = rows[:, :LANES].astype(f32)
    lane = lax.broadcasted_iota(jnp.int32, tags.shape, 1)
    tags = jnp.sum(jnp.where(lane == place[1], tags, 0.0), axis=1, keepdims=True)
    weight[...] = first_fours(jnp.broadcast_to(tags, mat[:, :LANES].shape))


def grad_kernel(sub, quad, weight, halves, back, wide):
    f32, bf16 = jnp.float32, jnp.bfloat16
    sums = quad[0].astype(f32)
    for index in range(1, OWNERS):
        sums = sums + quad[index].astype(f32)
    gate_pre = sums[:, :LANES]
    up_pre = sums[:, LANES : 2 * LANES]
    hidden_grad = sums[:, 2 * LANES :]
    sig = jax.nn.sigmoid(gate_pre)
    hidden = (gate_pre * sig * up_pre).astype(bf16).astype(f32)
    route = jnp.sum(hidden * hidden_grad, axis=1, keepdims=True)
    scaled = weight[...] * hidden_grad
    gate_grad = (scaled * up_pre * sig * (1.0 + gate_pre * (1.0 - sig))).astype(bf16)
    up_grad = (scaled * gate_pre * sig).astype(bf16)
    both = jnp.concatenate([gate_grad, up_grad], axis=1)
    route_hi, route_lo = hi_lo(route)
    pairs = both.shape[0] // 8
    width = halves.shape[2]
    step = 2 * LANES
    for start in range(0, width, step):
        outs = []
        for half in range(2):
            out = jnp.dot(
                both, halves[half, :, start : start + step], preferred_element_type=f32
            )
            if start == 0:
                lane = lax.broadcasted_iota(jnp.int32, out.shape, 1)
                out = jnp.where(lane == sub, route_hi, jnp.where(lane == sub + 1, route_lo, out))
            outs.append(out.reshape(pairs, 8, step))
        top, low = outs
        mask = upper(top.shape)
        even = jnp.where(mask, swap(low), top)
        odd = jnp.where(mask, low, swap(top))
        both_rows = jnp.stack([even, odd], axis=1).reshape(2 * pairs, 8, step)
        back[:, :, start : start + step] = both_rows.astype(bf16)
    weighted = (weight[...] * hidden).reshape(pairs, 8, LANES)
    mask = upper(weighted.shape)
    even = jnp.where(mask, swap(weighted), 0.0)
    odd = jnp.where(mask, weighted, 0.0)
    wide[...] = jnp.stack([even, odd], axis=1).reshape(pairs * 16, LANES).astype(bf16)


def down_kernel(place, *refs):
    *blocks, wide, out, rows = refs
    lay_rows(place[0], blocks, rows)
    out[...] = lax.dot_general(
        wide[...], rows[...], (((0,), (0,)), ((), ())), preferred_element_type=jnp.float32
    ).astype(out.dtype)


def sum_kernel(sub, landed, pieces):
    f32 = jnp.float32
    experts = landed.shape[0]
    width = landed.shape[3]
    tags = jnp.zeros((8, LANES), f32)
    lane = lax.broadcasted_iota(jnp.int32, (8, LANES), 1)
    for e in range(experts):
        pair = landed[e, 0, :, :LANES].astype(f32)
        both = jnp.sum(
            jnp.where((lane == sub) | (lane == sub + 1), pair, 0.0), axis=1, keepdims=True
        )
        tags = jnp.where(lane == sub + e, both, tags)
    tag_hi, tag_lo = hi_lo(tags)
    mask = upper((8, LANES))
    tags = jnp.where(mask, swap(tag_lo), tag_hi)
    for mm in range(width // LANES):
        cols = slice(mm * LANES, (mm + 1) * LANES)
        acc = landed[0, :, :, cols].astype(f32)
        for e in range(1, experts):
            acc = acc + landed[e, :, :, cols].astype(f32)
        for half in range(2):
            tiles = []
            for pair in range(2):
                one, two = acc[2 * pair], acc[2 * pair + 1]
                tile = jnp.where(mask, swap(two), one) if half == 0 else jnp.where(mask, two, swap(one))
                tiles.append(jnp.where(lane < sub, tile, tags if pair == 0 else 0.0))
            full = jnp.concatenate(tiles, axis=0).astype(pieces.dtype)
            pieces[half * (width // LANES) + mm] = full


def weight_table(expert_ids, route_weights, experts):
    onehot = expert_ids[:, :, None] == jnp.arange(experts, dtype=jnp.int32)[None, None, :]
    weights = jnp.where(onehot, route_weights.astype(jnp.float32)[:, :, None], 0.0)
    return jnp.sum(weights, axis=1).astype(jnp.bfloat16), onehot


def y_ring(block):
    count = lax.axis_size("y")
    up = [(i, (i + 1) % count) for i in range(count)]
    down = [((i + 1) % count, i) for i in range(count)]
    blocks = [None] * count
    blocks[0] = block
    fwd = bwd = block
    for step in range(1, count // 2 + 1):
        fwd = lax.ppermute(fwd, "y", up)
        blocks[(-step) % count] = fwd
        if step < count // 2:
            bwd = lax.ppermute(bwd, "y", down)
            blocks[step] = bwd
    return blocks


def body(tokens, out_grad, route_weights, expert_ids, w_gate, w_up, w_down):
    f32, bf16 = jnp.float32, jnp.bfloat16
    ny, nxh, nz = lax.axis_size("y"), lax.axis_size("xh"), lax.axis_size("z")
    experts = ny * nxh
    toks, _, sub = tokens.shape
    per_y = nxh * OWNERS
    groups = ny * per_y
    tall = 2 * toks
    my_y = lax.axis_index("y")
    expert = my_y * nxh + lax.axis_index("xh")
    place = jnp.stack([my_y, sub + expert]).astype(jnp.int32)

    table, onehot = weight_table(expert_ids, route_weights, experts)
    x_rows = jnp.concatenate(
        [tokens.transpose(1, 0, 2), jnp.broadcast_to(table[None], (OWNERS, toks, experts))], axis=2
    )
    g_rows = jnp.pad(out_grad.transpose(1, 0, 2), ((0, 0), (0, 0), (0, LANES - sub)))
    send = jnp.concatenate([x_rows, g_rows], axis=1)
    send = jnp.broadcast_to(send[None, :, None], (nxh, OWNERS, nz, tall, LANES))
    send = send.reshape(nxh * OWNERS * nz, tall, LANES)
    got = lax.all_to_all(send, ("xh", "xl", "c", "z"), 0, 0, tiled=True)
    blocks = [b.reshape(per_y, nz, tall, LANES) for b in y_ring(got)]

    gate_p = jnp.pad(w_gate[0].reshape(nz, sub, LANES), ((0, 0), (0, LANES - sub), (0, 0)))
    up_p = jnp.pad(w_up[0].reshape(nz, sub, LANES), ((0, 0), (0, LANES - sub), (0, 0)))
    gate_up = jnp.concatenate([gate_p, up_p], axis=2).reshape(nz * LANES, 2 * LANES)
    halves = gate_up.reshape(2, nz * LANES // 2, 2 * LANES).transpose(0, 2, 1)
    down_p = jnp.pad(w_down[0].reshape(LANES, nz, sub), ((0, 0), (0, 0), (0, LANES - sub)))
    down_p = down_p.reshape(LANES, nz * LANES)

    smem = pl.BlockSpec(memory_space=pltpu.SMEM)
    slots = groups * toks
    scratch = [pltpu.VMEM((groups * tall, nz * LANES), bf16)]
    part, weight = call(
        part_kernel,
        (
            jax.ShapeDtypeStruct((slots, 3 * LANES), bf16),
            jax.ShapeDtypeStruct((slots, LANES), f32),
        ),
        [smem] + whole(ny + 2),
        scratch,
        2 * groups * tall * nz * LANES * 3 * LANES,
        4 << 20,
    )(place, *blocks, gate_up, down_p)

    quad = lax.all_gather(part, ("xl", "c"), axis=0, tiled=False)

    back, wide = call(
        functools.partial(grad_kernel, sub),
        (
            jax.ShapeDtypeStruct((groups, tall, nz * LANES // 2), bf16),
            jax.ShapeDtypeStruct((groups * tall, LANES), bf16),
        ),
        whole(3),
        [],
        2 * slots * 2 * LANES * nz * LANES,
        3 << 20,
    )(quad, weight, halves)
    landed = lax.all_to_all(back, ("y", "xh", "xl", "c"), 0, 0, tiled=True)

    down_grad = call(
        down_kernel,
        jax.ShapeDtypeStruct((LANES, nz * LANES), bf16),
        [smem] + whole(ny + 1),
        scratch,
        2 * groups * tall * nz * LANES * LANES,
        4 << 20,
    )(place, *blocks, wide)
    down_grad = down_grad.reshape(LANES, nz, LANES)[:, :, :sub].reshape(1, LANES, nz * sub)

    pieces = call(
        functools.partial(sum_kernel, sub),
        jax.ShapeDtypeStruct((nz, OWNERS * toks, LANES), bf16),
        whole(1),
        [],
        groups * tall * nz * LANES // 2,
        1 << 20,
    )(landed.reshape(experts, OWNERS, tall, nz * LANES // 2))
    final = lax.all_to_all(pieces, "z", 0, 0, tiled=True)
    final = jnp.sum(final.astype(f32), axis=0)
    token_grad = final[:, :sub].reshape(OWNERS, toks, sub).transpose(1, 0, 2).astype(bf16)
    routes = final[:toks, sub:] + final[toks : 2 * toks, sub:]
    route_grad = jnp.sum(jnp.where(onehot, routes[:, None, :], 0.0), axis=2)
    return token_grad, down_grad, route_grad


def solution(mesh):
    fine = Mesh(
        mesh.devices.reshape(-1, 2, 2, 2, mesh.devices.shape[1]), ("y", "xh", "xl", "c", "z")
    )
    group = ("y", "xh", "xl", "c")
    return jax.shard_map(
        body,
        mesh=fine,
        in_specs=(
            P(group, None, "z"),
            P(group, None, "z"),
            P(group, None),
            P(group, None),
            P(group, None, "z"),
            P(group, None, "z"),
            P(group, "z", None),
        ),
        out_specs=(P(group, None, "z"), P(group, "z", None), P(group, None)),
        check_vma=False,
    )
```

time: 176 us -> 162 us (0.920)
  blocking collectives: 11 us -> 94.6 us
  waiting for transfers between devices: 81.2 us -> 23.8 us
  starting transfers between devices: 54.2 us -> 26.5 us
  local copies, waits for them, and re-layouts: 15 us -> 4.9 us
  matrix products: 6.87 us -> 0 us
  Pallas kernels: 0 us -> 6.21 us
  other arithmetic: 5.08 us -> 3.25 us
    all_to_all x0 -> x2, blocking collectives: none -> 83.5 us  [the longest x1 47 us: body(): got = lax.all_to_all(send, ('xh', 'xl', 'c', 'z'), 0, 0, tiled=True)]
    all_to_all x2 -> x0, waiting for transfers between devices: 47.9 us -> none  [the longest x1 27.9 us: body(): landed = lax.all_to_all(back, ('y', 'xh', 'xl', 'c'), 0, 0, tiled=True)]
    all_to_all x2 -> x0, starting transfers between devices: 31.2 us -> none  [the longest x1 24.1 us: body(): got = lax.all_to_all(send, ('xh', 'xl', 'c', 'z'), 0, 0, tiled=True)]
    ppermute x3, waiting for transfers between devices: 8.33 us -> 0.01 us  [y_ring(): bwd = lax.ppermute(bwd, 'y', down)]
    dot_general x18 -> x0, matrix products: 6.87 us -> none  [the longest x8 2.35 us: body(): first = jnp.dot(mat, gate_up, preferred_element_type=f32)]
    pallas_call x0 -> x4, Pallas kernels: none -> 6.21 us  [the longest x1 2.8 us: body(): call(part_kernel, (jax.ShapeDtypeStruct((slots, 3 * LANES), bf16), jax.Sh...]
    ppermute x3, starting transfers between devices: 8.93 us -> 14 us  [y_ring(): bwd = lax.ppermute(bwd, 'y', down)]
    unnamed x25 -> x17, local copies, waits for them, and re-layouts: 8.34 us -> 3.67 us
  transfers between devices with their start and end apart: 10 -> 8, of which waited for: 10 -> 5; matrix products, arithmetic and copies ran while one was open for 5% -> 2% of each run, Pallas kernels for 0% -> 1%
where the time goes in v2:
time: 162 us; the launch traced here: 160 us
  blocking collectives  94.6 us (58%)
  starting transfers between devices  26.5 us (16%)
  waiting for transfers between devices  23.8 us (15%)
  Pallas kernels  6.21 us (4%)
  local copies, waits for them, and re-layouts  4.9 us (3%)
  other arithmetic  3.25 us (2%)
    all_to_all x1, blocking collectives, body(): got = lax.all_to_all(send, ('xh', 'xl', 'c', 'z'), 0, 0, tiled=True)  47 us
    all_to_all x1, blocking collectives, body(): landed = lax.all_to_all(back, ('y', 'xh', 'xl', 'c'), 0, 0, tiled=True)  36.6 us
    ppermute x4, waiting for transfers between devices, y_ring(): fwd = lax.ppermute(fwd, 'y', up)  15.5 us
    ppermute x3, starting transfers between devices, y_ring(): bwd = lax.ppermute(bwd, 'y', down)  14 us
    all_gather x1, blocking collectives, body(): quad = lax.all_gather(part, ('xl', 'c'), axis=0, tiled=False)  11 us
    ppermute x4, starting transfers between devices, y_ring(): fwd = lax.ppermute(fwd, 'y', up)  8.99 us
    all_to_all x1, waiting for transfers between devices, body(): final = lax.all_to_all(pieces, 'z', 0, 0, tiled=True)  8.23 us
    unnamed x17, local copies, waits for them, and re-layouts  3.67 us
  transfers between devices with their start and end apart: 8, of which 5 were waited for; matrix products, arithmetic and copies ran while one was open for 2% of the time, Pallas kernels for 1%

profile of v2, /device:TPU:1, one launch (start us, length us, event | category | flops | bytes accessed | tf_op | source)
XLA Modules:
  0.0 160.1 jit_solution(7223154671365406060)
XLA Ops:
  0.6 0.0 copy-start.3
  0.6 0.7 convert_element_type.27
  1.4 0.8 select_reduce_fusion.1
  2.1 0.1 pad.22.clone
  2.2 0.7 fusion.4
  3.0 47.0 %all_to_all.15 = bf16[128,8,128]{2,1,0:T(8,128)(2,1)S(1)} all-to-all(bf16[128,8,128]{2,1,0:T(8,128)(2,1)S(1)} %bitcast.44), channel_id=1, replica_groups=mesh['y'=8,'xh'=2,'xl'=2,'c'=2,'z'=16] {'xh','xl','c','z'}, dimensions={0} | all-to-all | bytes 524288 | tf_op jit(solution)/shard_map/all_to_all | solution.py:206
  50.0 3.2 %collective-permute-start.3 = (bf16[128,8,128]{2,1,0:T(8,128)(2,1)S(1)}, bf16[128,8,128]{2,1,0:T(8,128)(2,1)S(1)}, u32[]{:S(2)}, u32[]{:S(2)}) collective-permute-start(bf16[128,8,128]{2,1,0:T(8,128)(2,1)S(1)} %all_to_all.15), channel_id=1, source_target_pairs={{0,128},{128,256},{256,384},{384,512},{512,640},{640,768},{768,896... | collective-permute-start | bytes 786440 | tf_op jit(solution)/shard_map/ppermute | solution.py:178
  53.2 3.8 %collective-permute-start = (bf16[128,8,128]{2,1,0:T(8,128)(2,1)S(1)}, bf16[128,8,128]{2,1,0:T(8,128)(2,1)S(1)}, u32[]{:S(2)}, u32[]{:S(2)}) collective-permute-start(bf16[128,8,128]{2,1,0:T(8,128)(2,1)S(1)} %all_to_all.15), channel_id=1, source_target_pairs={{128,0},{256,128},{384,256},{512,384},{640,512},{768,640},{896,768... | collective-permute-start | bytes 786440 | tf_op jit(solution)/shard_map/ppermute | solution.py:181
  57.0 4.4 %collective-permute-done.3 = bf16[128,8,128]{2,1,0:T(8,128)(2,1)S(1)} collective-permute-done((bf16[128,8,128]{2,1,0:T(8,128)(2,1)S(1)}, bf16[128,8,128]{2,1,0:T(8,128)(2,1)S(1)}, u32[]{:S(2)}, u32[]{:S(2)}) %collective-permute-start.3) | collective-permute-done | bytes 262176 | tf_op jit(solution)/shard_map/ppermute | solution.py:178
  61.4 2.0 %collective-permute-start.4 = (bf16[128,8,128]{2,1,0:T(8,128)(2,1)S(1)}, bf16[128,8,128]{2,1,0:T(8,128)(2,1)S(1)}, u32[]{:S(2)}, u32[]{:S(2)}) collective-permute-start(bf16[128,8,128]{2,1,0:T(8,128)(2,1)S(1)} %collective-permute-done.3), channel_id=1, source_target_pairs={{0,128},{128,256},{256,384},{384,512},{512,640},{640,768},{768,896... | collective-permute-start | bytes 786440 | tf_op jit(solution)/shard_map/ppermute | solution.py:178
  63.4 0.0 collective-permute-done
  63.4 5.0 %collective-permute-start.1 = (bf16[128,8,128]{2,1,0:T(8,128)(2,1)S(1)}, bf16[128,8,128]{2,1,0:T(8,128)(2,1)}, u32[]{:S(2)}, u32[]{:S(2)}) collective-permute-start(bf16[128,8,128]{2,1,0:T(8,128)(2,1)S(1)} %collective-permute-done), channel_id=1, source_target_pairs={{128,0},{256,128},{384,256},{512,384},{640,512},{768,640},{896,768... | collective-permute-start | bytes 786440 | tf_op jit(solution)/shard_map/ppermute | solution.py:181
  68.4 3.6 %collective-permute-done.4 = bf16[128,8,128]{2,1,0:T(8,128)(2,1)S(1)} collective-permute-done((bf16[128,8,128]{2,1,0:T(8,128)(2,1)S(1)}, bf16[128,8,128]{2,1,0:T(8,128)(2,1)S(1)}, u32[]{:S(2)}, u32[]{:S(2)}) %collective-permute-start.4) | collective-permute-done | bytes 262176 | tf_op jit(solution)/shard_map/ppermute | solution.py:178
  72.0 1.9 %collective-permute-start.5 = (bf16[128,8,128]{2,1,0:T(8,128)(2,1)S(1)}, bf16[128,8,128]{2,1,0:T(8,128)(2,1)}, u32[]{:S(2)}, u32[]{:S(2)}) collective-permute-start(bf16[128,8,128]{2,1,0:T(8,128)(2,1)S(1)} %collective-permute-done.4), channel_id=1, source_target_pairs={{0,128},{128,256},{256,384},{384,512},{512,640},{640,768},{768,896... | collective-permute-start | bytes 786440 | tf_op jit(solution)/shard_map/ppermute | solution.py:178
  73.9 0.0 collective-permute-done.1
  73.9 5.2 %collective-permute-start.2 = (bf16[128,8,128]{2,1,0:T(8,128)(2,1)}, bf16[128,8,128]{2,1,0:T(8,128)(2,1)}, u32[]{:S(2)}, u32[]{:S(2)}) collective-permute-start(bf16[128,8,128]{2,1,0:T(8,128)(2,1)} %collective-permute-done.1), channel_id=1, source_target_pairs={{128,0},{256,128},{384,256},{512,384},{640,512},{768,640},{896,768... | collective-permute-start | bytes 786440 | tf_op jit(solution)/shard_map/ppermute | solution.py:181
  79.1 2.7 %collective-permute-done.5 = bf16[128,8,128]{2,1,0:T(8,128)(2,1)} collective-permute-done((bf16[128,8,128]{2,1,0:T(8,128)(2,1)S(1)}, bf16[128,8,128]{2,1,0:T(8,128)(2,1)}, u32[]{:S(2)}, u32[]{:S(2)}) %collective-permute-start.5) | collective-permute-done | bytes 262176 | tf_op jit(solution)/shard_map/ppermute | solution.py:178
  81.7 1.9 %collective-permute-start.6 = (bf16[128,8,128]{2,1,0:T(8,128)(2,1)}, bf16[128,8,128]{2,1,0:T(8,128)(2,1)}, u32[]{:S(2)}, u32[]{:S(2)}) collective-permute-start(bf16[128,8,128]{2,1,0:T(8,128)(2,1)} %collective-permute-done.5), channel_id=1, source_target_pairs={{0,128},{128,256},{256,384},{384,512},{512,640},{640,768},{768,896... | collective-permute-start | bytes 786440 | tf_op jit(solution)/shard_map/ppermute | solution.py:178
  83.7 0.0 copy-done.3
  83.7 0.3 copy.19
  83.9 0.0 copy-start.4
  84.0 0.0 copy-start.5
  84.0 0.1 pad.18
  84.0 0.0 copy-done
  84.0 0.2 copy.25.refs_9_
  84.2 0.7 copy-done.4
  85.0 0.1 copy-done.5
  85.1 0.1 fusion.2
  85.2 0.5 copy.21
  85.8 0.1 pad_add_fusion.place
  85.9 0.0 collective-permute-done.2
  85.9 4.9 %collective-permute-done.6 = bf16[128,8,128]{2,1,0:T(8,128)(2,1)} collective-permute-done((bf16[128,8,128]{2,1,0:T(8,128)(2,1)}, bf16[128,8,128]{2,1,0:T(8,128)(2,1)}, u32[]{:S(2)}, u32[]{:S(2)}) %collective-permute-start.6) | collective-permute-done | bytes 262176 | tf_op jit(solution)/shard_map/ppermute | solution.py:178
  90.8 0.9 copy-done.1
  91.8 2.8 %shard_map.94 = (bf16[256,384]{1,0:T(8,128)(2,1)S(1)}, f32[256,128]{1,0:T(8,128)S(1)}) custom-call(s32[2]{0:T(128)S(1)} %pad_add_fusion.place, bf16[8,16,8,128]{3,2,1,0:T(8,128)(2,1)S(1)} %bitcast.32, bf16[8,16,8,128]{3,2,1,0:T(8,128)(2,1)S(1)} %bitcast.36, bf16[8,16,8,128]{3,2,1,0:T(8,128)(2,1)} %bitcast.7.refs_2_, bf16[8,16,8,128]{3,2,1,0:T(8,128)(2,1)} %bitcast.8.refs_3_, ...), custom_call_target="tpu_custom_call" | custom-call | flops 805306368 | bytes 4194304 | tf_op jit(solution)/shard_map/pallas_call | solution.py:219
  94.6 11.0 %all-gather = bf16[1024,384]{1,0:T(8,128)(2,1)S(1)} all-gather(bf16[256,384]{1,0:T(8,128)(2,1)S(1)} %get-tuple-element.7), channel_id=2, replica_groups=mesh['y'=8,'xh'=2,'xl'=2,'c'=2,'z'=16] {'xl','c'}, dimensions={0}, use_global_device_ids=true | all-gather | bytes 983040 | tf_op jit(solution)/shard_map/all_gather | solution.py:231
  105.6 0.6 shard_map.95
  106.2 36.6 %all_to_all.16 = bf16[64,8,1024]{2,1,0:T(8,128)(2,1)S(1)} all-to-all(bf16[64,8,1024]{2,1,0:T(8,128)(2,1)S(1)} %get-tuple-element.9), channel_id=1, replica_groups=mesh['y'=8,'xh'=2,'xl'=2,'c'=2,'z'=16] {'y','xh','xl','c'}, dimensions={0} | all-to-all | bytes 2097152 | tf_op jit(solution)/shard_map/all_to_all | solution.py:244
  142.7 0.8 shard_map.96
  143.5 3.5 %all-to-all-start.2 = ((bf16[16,16,128]{2,1,0:T(8,128)(2,1)}), bf16[16,16,128]{2,1,0:T(8,128)(2,1)S(1)}, u32[]{:S(2)}, u32[]{:S(2)}) async-start(bf16[16,16,128]{2,1,0:T(8,128)(2,1)} %shard_map.96), calls=%async_computation.2 | async-start | bytes 131072 | tf_op jit(solution)/shard_map/all_to_all | solution.py:264
  147.0 2.0 %shard_map.97 = bf16[128,2048]{1,0:T(8,128)(2,1)S(1)} custom-call(s32[2]{0:T(128)S(1)} %pad_add_fusion.place, bf16[8,16,8,128]{3,2,1,0:T(8,128)(2,1)S(1)} %bitcast.33, bf16[8,16,8,128]{3,2,1,0:T(8,128)(2,1)S(1)} %bitcast.37, bf16[8,16,8,128]{3,2,1,0:T(8,128)(2,1)} %bitcast.7.refs_2_, bf16[8,16,8,128]{3,2,1,0:T(8,128)(2,1)} %bitcast.8.refs_3_, ...), custom_call_target="tpu_custom_call" | custom-call | flops 268435456 | bytes 4194304 | tf_op jit(solution)/shard_map/pallas_call | solution.py:246
  149.1 0.3 copy.26
  149.3 0.0 copy-start.6
  149.4 1.0 copy.24
  150.4 8.2 %all-to-all-done.2 = bf16[16,16,128]{2,1,0:T(8,128)(2,1)S(1)} async-done(((bf16[16,16,128]{2,1,0:T(8,128)(2,1)}), bf16[16,16,128]{2,1,0:T(8,128)(2,1)S(1)}, u32[]{:S(2)}, u32[]{:S(2)}) %all-to-all-start.2) | async-done | bytes 65568 | tf_op jit(solution)/shard_map/all_to_all | solution.py:264
  158.6 0.1 slice_add_fusion
  158.7 0.6 copy.23
  159.3 0.0 copy-done.6
  159.3 0.7 select_reduce_fusion
  (9 shorter events, 0.1 us)
Async XLA Ops:
  0.6 83.0 %copy-start.3 = (bf16[1,128,1792]{2,1,0:T(8,128)(2,1)S(1)}, bf16[1,128,1792]{2,1,0:T(8,128)(2,1)}, u32[]{:S(2)}) copy-start(bf16[1,128,1792]{2,1,0:T(8,128)(2,1)} %param.13) | copy-start | bytes 1376260
  50.0 11.4 %collective-permute-start.3 = (bf16[128,8,128]{2,1,0:T(8,128)(2,1)S(1)}, bf16[128,8,128]{2,1,0:T(8,128)(2,1)S(1)}, u32[]{:S(2)}, u32[]{:S(2)}) collective-permute-start(bf16[128,8,128]{2,1,0:T(8,128)(2,1)S(1)} %all_to_all.15), channel_id=1, source_target_pairs={{0,128},{128,256},{256,384},{384,512},{512,640},{640,768},{768,896... | collective-permute-start | bytes 786440 | tf_op jit(solution)/shard_map/ppermute | solution.py:178
  53.2 10.2 %collective-permute-start = (bf16[128,8,128]{2,1,0:T(8,128)(2,1)S(1)}, bf16[128,8,128]{2,1,0:T(8,128)(2,1)S(1)}, u32[]{:S(2)}, u32[]{:S(2)}) collective-permute-start(bf16[128,8,128]{2,1,0:T(8,128)(2,1)S(1)} %all_to_all.15), channel_id=1, source_target_pairs={{128,0},{256,128},{384,256},{512,384},{640,512},{768,640},{896,768... | collective-permute-start | bytes 786440 | tf_op jit(solution)/shard_map/ppermute | solution.py:181
  61.4 10.6 %collective-permute-start.4 = (bf16[128,8,128]{2,1,0:T(8,128)(2,1)S(1)}, bf16[128,8,128]{2,1,0:T(8,128)(2,1)S(1)}, u32[]{:S(2)}, u32[]{:S(2)}) collective-permute-start(bf16[128,8,128]{2,1,0:T(8,128)(2,1)S(1)} %collective-permute-done.3), channel_id=1, source_target_pairs={{0,128},{128,256},{256,384},{384,512},{512,640},{640,768},{768,896... | collective-permute-start | bytes 786440 | tf_op jit(solution)/shard_map/ppermute | solution.py:178
  63.4 10.5 %collective-permute-start.1 = (bf16[128,8,128]{2,1,0:T(8,128)(2,1)S(1)}, bf16[128,8,128]{2,1,0:T(8,128)(2,1)}, u32[]{:S(2)}, u32[]{:S(2)}) collective-permute-start(bf16[128,8,128]{2,1,0:T(8,128)(2,1)S(1)} %collective-permute-done), channel_id=1, source_target_pairs={{128,0},{256,128},{384,256},{512,384},{640,512},{768,640},{896,768... | collective-permute-start | bytes 786440 | tf_op jit(solution)/shard_map/ppermute | solution.py:181
  72.0 12.0 %copy-start = (bf16[128,8,128]{2,1,0:T(8,128)(2,1)}, bf16[128,8,128]{2,1,0:T(8,128)(2,1)S(1)}, u32[]{:S(2)}) copy-start(bf16[128,8,128]{2,1,0:T(8,128)(2,1)S(1)} %collective-permute-done.4) | copy-start | bytes 786436
  72.0 9.8 %collective-permute-start.5 = (bf16[128,8,128]{2,1,0:T(8,128)(2,1)S(1)}, bf16[128,8,128]{2,1,0:T(8,128)(2,1)}, u32[]{:S(2)}, u32[]{:S(2)}) collective-permute-start(bf16[128,8,128]{2,1,0:T(8,128)(2,1)S(1)} %collective-permute-done.4), channel_id=1, source_target_pairs={{0,128},{128,256},{256,384},{384,512},{512,640},{640,768},{768,896... | collective-permute-start | bytes 786440 | tf_op jit(solution)/shard_map/ppermute | solution.py:178
  73.9 12.0 %collective-permute-start.2 = (bf16[128,8,128]{2,1,0:T(8,128)(2,1)}, bf16[128,8,128]{2,1,0:T(8,128)(2,1)}, u32[]{:S(2)}, u32[]{:S(2)}) collective-permute-start(bf16[128,8,128]{2,1,0:T(8,128)(2,1)} %collective-permute-done.1), channel_id=1, source_target_pairs={{128,0},{256,128},{384,256},{512,384},{640,512},{768,640},{896,768... | collective-permute-start | bytes 786440 | tf_op jit(solution)/shard_map/ppermute | solution.py:181
  81.7 9.1 %collective-permute-start.6 = (bf16[128,8,128]{2,1,0:T(8,128)(2,1)}, bf16[128,8,128]{2,1,0:T(8,128)(2,1)}, u32[]{:S(2)}, u32[]{:S(2)}) collective-permute-start(bf16[128,8,128]{2,1,0:T(8,128)(2,1)} %collective-permute-done.5), channel_id=1, source_target_pairs={{0,128},{128,256},{256,384},{384,512},{512,640},{640,768},{768,896... | collective-permute-start | bytes 786440 | tf_op jit(solution)/shard_map/ppermute | solution.py:178
  83.9 1.0 copy-start.4
  84.0 1.2 copy-start.5
  90.8 1.0 copy-start.1
  142.7 4.3 %copy-start.2 = (bf16[128,8,128]{2,1,0:T(8,128)(2,1)S(1)}, bf16[128,8,128]{2,1,0:T(8,128)(2,1)}, u32[]{:S(2)}) copy-start(bf16[128,8,128]{2,1,0:T(8,128)(2,1)} %copy-done) | copy-start | bytes 786436
  143.5 15.1 %all-to-all-start.2 = ((bf16[16,16,128]{2,1,0:T(8,128)(2,1)}), bf16[16,16,128]{2,1,0:T(8,128)(2,1)S(1)}, u32[]{:S(2)}, u32[]{:S(2)}) async-start(bf16[16,16,128]{2,1,0:T(8,128)(2,1)} %shard_map.96), calls=%async_computation.2 | async-start | bytes 131072 | tf_op jit(solution)/shard_map/all_to_all | solution.py:264
  149.3 10.0 %copy-start.6 = (s32[4,8]{1,0:T(4,128)S(1)}, s32[4,8]{1,0:T(4,128)}, u32[]{:S(2)}) copy-start(s32[4,8]{1,0:T(4,128)} %param.10) | copy-start | bytes 388

commit v3 on v2

v3 whole, which is shorter than its diff:
```python
import functools

import jax
import jax.numpy as jnp
from jax import lax
from jax.experimental import pallas as pl
from jax.experimental.pallas import tpu as pltpu
from jax.sharding import Mesh, PartitionSpec as P

OWNERS = 4
LANES = 128


VMEM_LIMIT = 40 * 1024 * 1024


def hi_lo(v):
    hi = v.astype(jnp.bfloat16).astype(jnp.float32)
    return hi, v - hi


def call(kernel, out_shape, in_specs, scratch, flops, moved):
    return pl.pallas_call(
        kernel,
        out_shape=out_shape,
        in_specs=in_specs,
        out_specs=jax.tree.map(lambda _: pl.BlockSpec(memory_space=pltpu.VMEM), out_shape),
        scratch_shapes=scratch,
        compiler_params=pltpu.CompilerParams(vmem_limit_bytes=VMEM_LIMIT),
        cost_estimate=pl.CostEstimate(flops=flops, bytes_accessed=moved, transcendentals=0),
    )


def whole(count):
    return [pl.BlockSpec(memory_space=pltpu.VMEM)] * count


def upper(shape):
    return lax.broadcasted_iota(jnp.int32, shape, len(shape) - 2) >= 4


def swap(v):
    return pltpu.roll(v, 4, axis=v.ndim - 2)


def first_fours(v):
    pairs = v.reshape(v.shape[0] // 16, 2, 8, v.shape[1])
    even, odd = pairs[:, 0], pairs[:, 1]
    return jnp.where(upper(even.shape), swap(odd), even).reshape(-1, v.shape[1])


def last_fours(v):
    pairs = v.reshape(v.shape[0] // 16, 2, 8, v.shape[1])
    even, odd = pairs[:, 0], pairs[:, 1]
    return jnp.where(upper(even.shape), odd, swap(even)).reshape(-1, v.shape[1])


def lay_rows(my_y, blocks, rows):
    count = len(blocks)
    tiles = rows.shape[1] // LANES
    for index, block in enumerate(blocks):
        per_y = block.shape[0] // tiles
        size = per_y * 8
        base = pl.multiple_of(lax.rem(my_y + index, count) * size, size)
        for k in range(tiles):
            tile = block[k * per_y : (k + 1) * per_y].astype(jnp.float32)
            rows[pl.ds(base, size), k * LANES : (k + 1) * LANES] = tile.reshape(
                size, LANES
            ).astype(jnp.bfloat16)


def pack_kernel(sub, got, block):
    f32 = jnp.float32
    per_y, nz, _, _ = got.shape
    size = per_y * 8
    tiles = nz * sub // LANES
    lane = lax.broadcasted_iota(jnp.int32, (size, LANES), 1)
    for k in range(tiles):
        first, skip = divmod(k * LANES, sub)
        tile = got[:, first].astype(f32).reshape(size, LANES)
        if skip:
            tile = pltpu.roll(tile, LANES - skip, axis=1)
        after = got[:, first + 1].astype(f32).reshape(size, LANES)
        after = pltpu.roll(after, sub - skip, axis=1)
        tile = jnp.where(lane < sub - skip, tile, after)
        block[k * per_y : (k + 1) * per_y] = tile.reshape(per_y, 8, LANES).astype(block.dtype)
    width = LANES - sub
    lane = lax.broadcasted_iota(jnp.int32, (8, LANES), 1)
    tags = jnp.zeros((8, LANES), f32)
    for s in range(per_y):
        moved = pltpu.roll(got[s, 0].astype(f32), (width * s - sub) % LANES, axis=1)
        tags = jnp.where((lane >= width * s) & (lane < width * (s + 1)), moved, tags)
    block[tiles * per_y] = tags.astype(block.dtype)


def part_kernel(place, *refs):
    *blocks, gate, up, down, part, weight, rows, spread = refs
    f32 = jnp.float32
    lay_rows(place[0], blocks, rows)
    mat = rows[...]
    count = len(blocks)
    size = rows.shape[0] // count
    per_y = size // 8
    shape = (per_y, 8, LANES)
    lane = lax.broadcasted_iota(jnp.int32, shape, 2)
    want = place[1] + lax.broadcasted_iota(jnp.int32, shape, 0) * (LANES // per_y)
    for index, block in enumerate(blocks):
        tags = jnp.broadcast_to(block[block.shape[0] - 1].astype(f32)[None], shape)
        tags = jnp.sum(jnp.where(lane == want, tags, 0.0), axis=2, keepdims=True)
        base = pl.multiple_of(lax.rem(place[0] + index, count) * size, size)
        spread[pl.ds(base, size), :] = jnp.broadcast_to(tags, shape).reshape(size, LANES)
    weight[...] = first_fours(spread[...])
    for index, mats in enumerate((gate, up)):
        out = jnp.dot(mat, mats[...], preferred_element_type=f32)
        part[:, index * LANES : (index + 1) * LANES] = first_fours(out).astype(part.dtype)
    out = lax.dot_general(mat, down[...], (((1,), (1,)), ((), ())), preferred_element_type=f32)
    part[:, 2 * LANES :] = last_fours(out).astype(part.dtype)


def grad_kernel(quad, weight, gate, up, back, wide):
    f32, bf16 = jnp.float32, jnp.bfloat16
    sums = quad[0].astype(f32)
    for index in range(1, OWNERS):
        sums = sums + quad[index].astype(f32)
    gate_pre = sums[:, :LANES]
    up_pre = sums[:, LANES : 2 * LANES]
    hidden_grad = sums[:, 2 * LANES :]
    sig = jax.nn.sigmoid(gate_pre)
    hidden = (gate_pre * sig * up_pre).astype(bf16).astype(f32)
    route = jnp.sum(hidden * hidden_grad, axis=1, keepdims=True)
    scaled = weight[...] * hidden_grad
    gate_grad = (scaled * up_pre * sig * (1.0 + gate_pre * (1.0 - sig))).astype(bf16)
    up_grad = (scaled * gate_pre * sig).astype(bf16)
    route_hi, route_lo = hi_lo(route)
    slots = route.shape[0]
    groups, tiles, toks, _ = back.shape
    lane = lax.broadcasted_iota(jnp.int32, (slots, LANES), 1)
    tags = jnp.where(lane == 0, route_hi, jnp.where(lane == 1, route_lo, 0.0))
    back[:, tiles - 1] = tags.reshape(groups, toks, LANES).astype(bf16)
    across = (((1,), (1,)), ((), ()))
    for k in range(0, tiles - 1, 2):
        cols = slice(k * LANES, (k + 2) * LANES)
        out = lax.dot_general(gate_grad, gate[cols], across, preferred_element_type=f32)
        out = out + lax.dot_general(up_grad, up[cols], across, preferred_element_type=f32)
        for j in range(2):
            tile = out[:, j * LANES : (j + 1) * LANES]
            back[:, k + j] = tile.reshape(groups, toks, LANES).astype(bf16)
    pairs = slots // 8
    weighted = (weight[...] * hidden).reshape(pairs, 8, LANES)
    mask = upper(weighted.shape)
    even = jnp.where(mask, swap(weighted), 0.0)
    odd = jnp.where(mask, weighted, 0.0)
    wide[...] = jnp.stack([even, odd], axis=1).reshape(pairs * 16, LANES).astype(bf16)


def down_kernel(place, *refs):
    *blocks, wide, out, rows = refs
    lay_rows(place[0], blocks, rows)
    out[...] = lax.dot_general(
        wide[...], rows[...], (((0,), (0,)), ((), ())), preferred_element_type=jnp.float32
    ).astype(out.dtype)


def sum_kernel(sub, landed, pieces, acc):
    f32 = jnp.float32
    experts, owners, tiles, toks, _ = landed.shape
    tags = jnp.zeros((2 * toks, LANES), f32)
    lane = lax.broadcasted_iota(jnp.int32, (toks, LANES), 1)
    tag_hi = jnp.zeros((toks, LANES), f32)
    for e in range(experts):
        pair = landed[e, 0, tiles - 1].astype(f32)
        both = jnp.sum(jnp.where(lane < 2, pair, 0.0), axis=1, keepdims=True)
        tag_hi = jnp.where(lane == sub + e, both, tag_hi)
    tag_hi, tag_lo = hi_lo(tag_hi)
    acc[tiles - 1] = jnp.zeros_like(acc[tiles - 1])
    acc[tiles - 1, :toks] = tag_hi
    acc[tiles - 1, toks : 2 * toks] = tag_lo
    for k in range(tiles - 1):
        for q in range(owners):
            acc[k, q * toks : (q + 1) * toks] = jnp.sum(landed[:, q, k].astype(f32), axis=0)
    tags = acc[tiles - 1]
    lane = lax.broadcasted_iota(jnp.int32, tags.shape, 1)
    for m in range(pieces.shape[0]):
        first, skip = divmod(m * sub, LANES)
        tile = acc[first]
        if skip:
            tile = pltpu.roll(tile, LANES - skip, axis=1)
        if skip + sub > LANES:
            after = pltpu.roll(acc[first + 1], LANES - skip, axis=1)
            tile = jnp.where(lane < LANES - skip, tile, after)
        pieces[m] = jnp.where(lane < sub, tile, tags).astype(pieces.dtype)


def weight_table(expert_ids, route_weights, experts):
    onehot = expert_ids[:, :, None] == jnp.arange(experts, dtype=jnp.int32)[None, None, :]
    weights = jnp.where(onehot, route_weights.astype(jnp.float32)[:, :, None], 0.0)
    return jnp.sum(weights, axis=1).astype(jnp.bfloat16), onehot


def y_ring(block):
    count = lax.axis_size("y")
    up = [(i, (i + 1) % count) for i in range(count)]
    down = [((i + 1) % count, i) for i in range(count)]
    blocks = [None] * count
    blocks[0] = block
    fwd = bwd = block
    for step in range(1, count // 2 + 1):
        fwd = lax.ppermute(fwd, "y", up)
        blocks[(-step) % count] = fwd
        if step < count // 2:
            bwd = lax.ppermute(bwd, "y", down)
            blocks[step] = bwd
    return blocks


def body(tokens, out_grad, route_weights, expert_ids, w_gate, w_up, w_down):
    f32, bf16 = jnp.float32, jnp.bfloat16
    ny, nxh, nz = lax.axis_size("y"), lax.axis_size("xh"), lax.axis_size("z")
    experts = ny * nxh
    toks, _, sub = tokens.shape
    per_y = nxh * OWNERS
    groups = ny * per_y
    tall = 2 * toks
    my_y = lax.axis_index("y")
    expert = my_y * nxh + lax.axis_index("xh")
    place = jnp.stack([my_y, expert]).astype(jnp.int32)

    table, onehot = weight_table(expert_ids, route_weights, experts)
    x_rows = jnp.concatenate(
        [tokens.transpose(1, 0, 2), jnp.broadcast_to(table[None], (OWNERS, toks, experts))], axis=2
    )
    g_rows = jnp.pad(out_grad.transpose(1, 0, 2), ((0, 0), (0, 0), (0, LANES - sub)))
    send = jnp.concatenate([x_rows, g_rows], axis=1)
    send = jnp.broadcast_to(send[None, :, None], (nxh, OWNERS, nz, tall, LANES))
    send = send.reshape(nxh * OWNERS * nz, tall, LANES)
    got = lax.all_to_all(send, ("xh", "xl", "c", "z"), 0, 0, tiled=True)
    tiles = nz * sub // LANES
    block = call(
        functools.partial(pack_kernel, sub),
        jax.ShapeDtypeStruct((tiles * per_y + 1, tall, LANES), bf16),
        whole(1),
        [],
        groups * tall * LANES,
        1 << 19,
    )(got.reshape(per_y, nz, tall, LANES))
    blocks = y_ring(block)

    smem = pl.BlockSpec(memory_space=pltpu.SMEM)
    slots = groups * toks
    rows = pltpu.VMEM((groups * tall, nz * sub), bf16)
    part, weight = call(
        part_kernel,
        (
            jax.ShapeDtypeStruct((slots, 3 * LANES), bf16),
            jax.ShapeDtypeStruct((slots, LANES), f32),
        ),
        [smem] + whole(ny + 3),
        [rows, pltpu.VMEM((groups * tall, LANES), f32)],
        2 * groups * tall * nz * LANES * 3 * LANES,
        4 << 20,
    )(place, *blocks, w_gate[0], w_up[0], w_down[0])

    quad = lax.all_gather(part, ("xl", "c"), axis=0, tiled=False)

    back, wide = call(
        grad_kernel,
        (
            jax.ShapeDtypeStruct((groups, tiles + 1, toks, LANES), bf16),
            jax.ShapeDtypeStruct((groups * tall, LANES), bf16),
        ),
        whole(4),
        [],
        2 * slots * 2 * LANES * nz * LANES,
        3 << 20,
    )(quad, weight, w_gate[0], w_up[0])
    landed = lax.all_to_all(back, ("y", "xh", "xl", "c"), 0, 0, tiled=True)

    down_grad = call(
        down_kernel,
        jax.ShapeDtypeStruct((LANES, nz * sub), bf16),
        [smem] + whole(ny + 1),
        [rows],
        2 * groups * tall * nz * LANES * LANES,
        4 << 20,
    )(place, *blocks, wide)
    pieces = call(
        functools.partial(sum_kernel, sub),
        jax.ShapeDtypeStruct((nz, OWNERS * toks, LANES), bf16),
        whole(1),
        [pltpu.VMEM((tiles + 1, OWNERS * toks, LANES), f32)],
        groups * toks * nz * LANES,
        1 << 20,
    )(landed.reshape(experts, OWNERS, tiles + 1, toks, LANES))
    final = lax.all_to_all(pieces, "z", 0, 0, tiled=True)
    final = jnp.sum(final.astype(f32), axis=0)
    token_grad = final[:, :sub].reshape(OWNERS, toks, sub).transpose(1, 0, 2).astype(bf16)
    routes = final[:toks, sub:] + final[toks : 2 * toks, sub:]
    route_grad = jnp.sum(jnp.where(onehot, routes[:, None, :], 0.0), axis=2)
    return token_grad, down_grad[None], route_grad


def solution(mesh):
    fine = Mesh(
        mesh.devices.reshape(-1, 2, 2, 2, mesh.devices.shape[1]), ("y", "xh", "xl", "c", "z")
    )
    group = ("y", "xh", "xl", "c")
    return jax.shard_map(
        body,
        mesh=fine,
        in_specs=(
            P(group, None, "z"),
            P(group, None, "z"),
            P(group, None),
            P(group, None),
            P(group, None, "z"),
            P(group, None, "z"),
            P(group, "z", None),
        ),
        out_specs=(P(group, None, "z"), P(group, "z", None), P(group, None)),
        check_vma=False,
    )
```

time: 162 us -> 157 us (0.969)
  local copies, waits for them, and re-layouts: 4.9 us -> 2.37 us
    unnamed x17 -> x13, local copies, waits for them, and re-layouts: 3.67 us -> 2.25 us
  transfers between devices with their start and end apart: 8 -> 8, of which waited for: 5 -> 5; matrix products, arithmetic and copies ran while one was open for 2% -> 0% of each run, Pallas kernels for 1% -> 1%
where the time goes in v3:
time: 157 us; the launch traced here: 155 us
  blocking collectives  93.4 us (59%)
  starting transfers between devices  26.4 us (17%)
  waiting for transfers between devices  24.2 us (15%)
  Pallas kernels  6.5 us (4%)
  local copies, waits for them, and re-layouts  2.37 us (2%)
  other arithmetic  1.69 us (1%)
    all_to_all x1, blocking collectives, body(): got = lax.all_to_all(send, ('xh', 'xl', 'c', 'z'), 0, 0, tiled=True)  47.1 us
    all_to_all x1, blocking collectives, body(): landed = lax.all_to_all(back, ('y', 'xh', 'xl', 'c'), 0, 0, tiled=True)  35.1 us
    ppermute x4, waiting for transfers between devices, y_ring(): fwd = lax.ppermute(fwd, 'y', up)  14.6 us
    ppermute x3, starting transfers between devices, y_ring(): bwd = lax.ppermute(bwd, 'y', down)  13.9 us
    all_gather x1, blocking collectives, body(): quad = lax.all_gather(part, ('xl', 'c'), axis=0, tiled=False)  11.2 us
    all_to_all x1, waiting for transfers between devices, body(): final = lax.all_to_all(pieces, 'z', 0, 0, tiled=True)  9.55 us
    ppermute x4, starting transfers between devices, y_ring(): fwd = lax.ppermute(fwd, 'y', up)  9 us
    all_to_all x1, starting transfers between devices, body(): final = lax.all_to_all(pieces, 'z', 0, 0, tiled=True)  3.5 us
  transfers between devices with their start and end apart: 8, of which 5 were waited for; matrix products, arithmetic and copies ran while one was open for 0% of the time, Pallas kernels for 1%

profile of v3, /device:TPU:1, one launch (start us, length us, event | category | flops | bytes accessed | tf_op | source)
XLA Modules:
  0.0 155.4 jit_solution(8804373426855801140)
XLA Ops:
  0.6 0.0 copy-start.3
  0.6 0.7 convert_element_type.22
  1.3 0.0 copy-done.3
  1.3 0.0 copy-start.5
  1.3 0.1 select_reduce_fusion.1
  1.4 0.0 copy-start.4
  1.4 0.1 pad.6.clone
  1.5 0.5 copy-done.5
  2.0 0.1 copy-done.4
  2.2 0.0 copy-start
  2.2 0.0 copy-start.1
  2.2 47.1 %all_to_all.15 = bf16[128,8,128]{2,1,0:T(8,128)(2,1)S(1)} all-to-all(bf16[128,8,128]{2,1,0:T(8,128)(2,1)S(1)} %bitcast.23), channel_id=1, replica_groups=mesh['y'=8,'xh'=2,'xl'=2,'c'=2,'z'=16] {'xh','xl','c','z'}, dimensions={0} | all-to-all | bytes 524288 | tf_op jit(solution)/shard_map/all_to_all | solution.py:236
  49.3 0.2 shard_map.94.refs_0_
  49.5 3.2 %collective-permute-start.3 = (bf16[113,8,128]{2,1,0:T(8,128)(2,1)S(1)}, bf16[113,8,128]{2,1,0:T(8,128)(2,1)S(1)}, u32[]{:S(2)}, u32[]{:S(2)}) collective-permute-start(bf16[113,8,128]{2,1,0:T(8,128)(2,1)S(1)} %shard_map.94.refs_0_), channel_id=1, source_target_pairs={{0,128},{128,256},{256,384},{384,512},{512,640},{640,768},{768,896... | collective-permute-start | bytes 694280 | tf_op jit(solution)/shard_map/ppermute | solution.py:208
  52.7 3.8 %collective-permute-start = (bf16[113,8,128]{2,1,0:T(8,128)(2,1)S(1)}, bf16[113,8,128]{2,1,0:T(8,128)(2,1)S(1)}, u32[]{:S(2)}, u32[]{:S(2)}) collective-permute-start(bf16[113,8,128]{2,1,0:T(8,128)(2,1)S(1)} %shard_map.94.refs_0_), channel_id=1, source_target_pairs={{128,0},{256,128},{384,256},{512,384},{640,512},{768,640},{896,768... | collective-permute-start | bytes 694280 | tf_op jit(solution)/shard_map/ppermute | solution.py:211
  56.5 3.7 %collective-permute-done.3.refs_7_ = bf16[113,8,128]{2,1,0:T(8,128)(2,1)S(1)} collective-permute-done((bf16[113,8,128]{2,1,0:T(8,128)(2,1)S(1)}, bf16[113,8,128]{2,1,0:T(8,128)(2,1)S(1)}, u32[]{:S(2)}, u32[]{:S(2)}) %collective-permute-start.3) | collective-permute-done | bytes 231456 | tf_op jit(solution)/shard_map/ppermute | solution.py:208
  60.3 2.0 %collective-permute-start.4 = (bf16[113,8,128]{2,1,0:T(8,128)(2,1)S(1)}, bf16[113,8,128]{2,1,0:T(8,128)(2,1)S(1)}, u32[]{:S(2)}, u32[]{:S(2)}) collective-permute-start(bf16[113,8,128]{2,1,0:T(8,128)(2,1)S(1)} %collective-permute-done.3.refs_7_), channel_id=1, source_target_pairs={{0,128},{128,256},{256,384},{384,512},{512,640},{640,768},{768,896... | collective-permute-start | bytes 694280 | tf_op jit(solution)/shard_map/ppermute | solution.py:208
  62.3 0.0 collective-permute-done.refs_1_
  62.3 5.0 %collective-permute-start.1 = (bf16[113,8,128]{2,1,0:T(8,128)(2,1)S(1)}, bf16[113,8,128]{2,1,0:T(8,128)(2,1)S(1)}, u32[]{:S(2)}, u32[]{:S(2)}) collective-permute-start(bf16[113,8,128]{2,1,0:T(8,128)(2,1)S(1)} %collective-permute-done.refs_1_), channel_id=1, source_target_pairs={{128,0},{256,128},{384,256},{512,384},{640,512},{768,640},{896,768... | collective-permute-start | bytes 694280 | tf_op jit(solution)/shard_map/ppermute | solution.py:211
  67.3 2.9 %collective-permute-done.4.refs_6_ = bf16[113,8,128]{2,1,0:T(8,128)(2,1)S(1)} collective-permute-done((bf16[113,8,128]{2,1,0:T(8,128)(2,1)S(1)}, bf16[113,8,128]{2,1,0:T(8,128)(2,1)S(1)}, u32[]{:S(2)}, u32[]{:S(2)}) %collective-permute-start.4) | collective-permute-done | bytes 231456 | tf_op jit(solution)/shard_map/ppermute | solution.py:208
  70.2 1.9 %collective-permute-start.5 = (bf16[113,8,128]{2,1,0:T(8,128)(2,1)S(1)}, bf16[113,8,128]{2,1,0:T(8,128)(2,1)S(1)}, u32[]{:S(2)}, u32[]{:S(2)}) collective-permute-start(bf16[113,8,128]{2,1,0:T(8,128)(2,1)S(1)} %collective-permute-done.4.refs_6_), channel_id=1, source_target_pairs={{0,128},{128,256},{256,384},{384,512},{512,640},{640,768},{768,896... | collective-permute-start | bytes 694280 | tf_op jit(solution)/shard_map/ppermute | solution.py:208
  72.1 0.0 collective-permute-done.1.refs_2_
  72.1 5.1 %collective-permute-start.2 = (bf16[113,8,128]{2,1,0:T(8,128)(2,1)S(1)}, bf16[113,8,128]{2,1,0:T(8,128)(2,1)S(1)}, u32[]{:S(2)}, u32[]{:S(2)}) collective-permute-start(bf16[113,8,128]{2,1,0:T(8,128)(2,1)S(1)} %collective-permute-done.1.refs_2_), channel_id=1, source_target_pairs={{128,0},{256,128},{384,256},{512,384},{640,512},{768,640},{896,768... | collective-permute-start | bytes 694280 | tf_op jit(solution)/shard_map/ppermute | solution.py:211
  77.2 2.0 %collective-permute-done.5.refs_5_ = bf16[113,8,128]{2,1,0:T(8,128)(2,1)S(1)} collective-permute-done((bf16[113,8,128]{2,1,0:T(8,128)(2,1)S(1)}, bf16[113,8,128]{2,1,0:T(8,128)(2,1)S(1)}, u32[]{:S(2)}, u32[]{:S(2)}) %collective-permute-start.5) | collective-permute-done | bytes 231456 | tf_op jit(solution)/shard_map/ppermute | solution.py:208
  79.2 1.9 %collective-permute-start.6 = (bf16[113,8,128]{2,1,0:T(8,128)(2,1)S(1)}, bf16[113,8,128]{2,1,0:T(8,128)(2,1)S(1)}, u32[]{:S(2)}, u32[]{:S(2)}) collective-permute-start(bf16[113,8,128]{2,1,0:T(8,128)(2,1)S(1)} %collective-permute-done.5.refs_5_), channel_id=1, source_target_pairs={{0,128},{128,256},{256,384},{384,512},{512,640},{640,768},{768,896... | collective-permute-start | bytes 694280 | tf_op jit(solution)/shard_map/ppermute | solution.py:208
  81.1 0.1 pad_add_fusion.place
  81.2 0.0 collective-permute-done.2.refs_3_
  81.2 6.0 %collective-permute-done.6.refs_4_ = bf16[113,8,128]{2,1,0:T(8,128)(2,1)S(1)} collective-permute-done((bf16[113,8,128]{2,1,0:T(8,128)(2,1)S(1)}, bf16[113,8,128]{2,1,0:T(8,128)(2,1)S(1)}, u32[]{:S(2)}, u32[]{:S(2)}) %collective-permute-start.6) | collective-permute-done | bytes 231456 | tf_op jit(solution)/shard_map/ppermute | solution.py:208
  87.2 0.0 copy-done
  87.2 0.0 copy-done.1
  87.2 0.0 copy-start.2
  87.2 1.0 copy-done.2
  88.2 2.4 %shard_map.95 = (bf16[256,384]{1,0:T(8,128)(2,1)S(1)}, f32[256,128]{1,0:T(8,128)S(1)}) custom-call(s32[2]{0:T(128)S(1)} %pad_add_fusion.place, bf16[113,8,128]{2,1,0:T(8,128)(2,1)S(1)} %shard_map.94.refs_0_, bf16[113,8,128]{2,1,0:T(8,128)(2,1)S(1)} %collective-permute-done.refs_1_, bf16[113,8,128]{2,1,0:T(8,128)(2,1)S(1)} %collective-permute-done.1.refs_2_, ...), custom_call_target="tpu_custom_call" | custom-call | flops 805306368 | bytes 4194304 | tf_op jit(solution)/shard_map/pallas_call | solution.py:251
  90.7 11.2 %all-gather = bf16[1024,384]{1,0:T(8,128)(2,1)S(1)} all-gather(bf16[256,384]{1,0:T(8,128)(2,1)S(1)} %get-tuple-element.7), channel_id=2, replica_groups=mesh['y'=8,'xh'=2,'xl'=2,'c'=2,'z'=16] {'xl','c'}, dimensions={0}, use_global_device_ids=true | all-gather | bytes 983040 | tf_op jit(solution)/shard_map/all_gather | solution.py:263
  101.9 0.7 shard_map.96
  102.6 35.1 %all_to_all.16 = bf16[64,15,4,128]{3,2,1,0:T(4,128)(2,1)S(1)} all-to-all(bf16[64,15,4,128]{3,2,1,0:T(4,128)(2,1)S(1)} %get-tuple-element.9), channel_id=1, replica_groups=mesh['y'=8,'xh'=2,'xl'=2,'c'=2,'z'=16] {'y','xh','xl','c'}, dimensions={0} | all-to-all | bytes 1966080 | tf_op jit(solution)/shard_map/all_to_all | solution.py:276
  137.7 1.1 shard_map.97
  138.8 3.5 %all-to-all-start.2 = ((bf16[16,16,128]{2,1,0:T(8,128)(2,1)}), bf16[16,16,128]{2,1,0:T(8,128)(2,1)S(1)}, u32[]{:S(2)}, u32[]{:S(2)}) async-start(bf16[16,16,128]{2,1,0:T(8,128)(2,1)} %shard_map.97), calls=%async_computation.2 | async-start | bytes 131072 | tf_op jit(solution)/shard_map/all_to_all | solution.py:294
  142.3 2.0 %shard_map.98 = bf16[128,1792]{1,0:T(8,128)(2,1)} custom-call(s32[2]{0:T(128)S(1)} %pad_add_fusion.place, bf16[113,8,128]{2,1,0:T(8,128)(2,1)S(1)} %shard_map.94.refs_0_, bf16[113,8,128]{2,1,0:T(8,128)(2,1)S(1)} %collective-permute-done.refs_1_, bf16[113,8,128]{2,1,0:T(8,128)(2,1)S(1)} %collective-permute-done.1.refs_2_, ...), custom_call_target="tpu_custom_call" | custom-call | flops 268435456 | bytes 4194304 | tf_op jit(solution)/shard_map/pallas_call | solution.py:278
  144.4 9.5 %all-to-all-done.2 = bf16[16,16,128]{2,1,0:T(8,128)(2,1)S(1)} async-done(((bf16[16,16,128]{2,1,0:T(8,128)(2,1)}), bf16[16,16,128]{2,1,0:T(8,128)(2,1)S(1)}, u32[]{:S(2)}, u32[]{:S(2)}) %all-to-all-start.2) | async-done | bytes 65568 | tf_op jit(solution)/shard_map/all_to_all | solution.py:294
  154.0 0.1 slice_add_fusion
  154.0 0.6 copy.14
  154.6 0.7 select_reduce_fusion
  (5 shorter events, 0.1 us)
Async XLA Ops:
  0.6 0.7 copy-start.3
  1.3 0.7 copy-start.5
  1.4 0.7 copy-start.4
  2.2 85.0 %copy-start = (bf16[1,1792,128]{2,1,0:T(8,128)(2,1)S(1)}, bf16[1,1792,128]{2,1,0:T(8,128)(2,1)}, u32[]{:S(2)}) copy-start(bf16[1,1792,128]{2,1,0:T(8,128)(2,1)} %param.11) | copy-start | bytes 1376260
  2.2 85.0 %copy-start.1 = (bf16[1,1792,128]{2,1,0:T(8,128)(2,1)S(1)}, bf16[1,1792,128]{2,1,0:T(8,128)(2,1)}, u32[]{:S(2)}) copy-start(bf16[1,1792,128]{2,1,0:T(8,128)(2,1)} %param.12) | copy-start | bytes 1376260
  49.5 10.8 %collective-permute-start.3 = (bf16[113,8,128]{2,1,0:T(8,128)(2,1)S(1)}, bf16[113,8,128]{2,1,0:T(8,128)(2,1)S(1)}, u32[]{:S(2)}, u32[]{:S(2)}) collective-permute-start(bf16[113,8,128]{2,1,0:T(8,128)(2,1)S(1)} %shard_map.94.refs_0_), channel_id=1, source_target_pairs={{0,128},{128,256},{256,384},{384,512},{512,640},{640,768},{768,896... | collective-permute-start | bytes 694280 | tf_op jit(solution)/shard_map/ppermute | solution.py:208
  52.7 9.5 %collective-permute-start = (bf16[113,8,128]{2,1,0:T(8,128)(2,1)S(1)}, bf16[113,8,128]{2,1,0:T(8,128)(2,1)S(1)}, u32[]{:S(2)}, u32[]{:S(2)}) collective-permute-start(bf16[113,8,128]{2,1,0:T(8,128)(2,1)S(1)} %shard_map.94.refs_0_), channel_id=1, source_target_pairs={{128,0},{256,128},{384,256},{512,384},{640,512},{768,640},{896,768... | collective-permute-start | bytes 694280 | tf_op jit(solution)/shard_map/ppermute | solution.py:211
  60.3 9.9 %collective-permute-start.4 = (bf16[113,8,128]{2,1,0:T(8,128)(2,1)S(1)}, bf16[113,8,128]{2,1,0:T(8,128)(2,1)S(1)}, u32[]{:S(2)}, u32[]{:S(2)}) collective-permute-start(bf16[113,8,128]{2,1,0:T(8,128)(2,1)S(1)} %collective-permute-done.3.refs_7_), channel_id=1, source_target_pairs={{0,128},{128,256},{256,384},{384,512},{512,640},{640,768},{768,896... | collective-permute-start | bytes 694280 | tf_op jit(solution)/shard_map/ppermute | solution.py:208
  62.3 9.9 %collective-permute-start.1 = (bf16[113,8,128]{2,1,0:T(8,128)(2,1)S(1)}, bf16[113,8,128]{2,1,0:T(8,128)(2,1)S(1)}, u32[]{:S(2)}, u32[]{:S(2)}) collective-permute-start(bf16[113,8,128]{2,1,0:T(8,128)(2,1)S(1)} %collective-permute-done.refs_1_), channel_id=1, source_target_pairs={{128,0},{256,128},{384,256},{512,384},{640,512},{768,640},{896,768... | collective-permute-start | bytes 694280 | tf_op jit(solution)/shard_map/ppermute | solution.py:211
  70.2 9.0 %collective-permute-start.5 = (bf16[113,8,128]{2,1,0:T(8,128)(2,1)S(1)}, bf16[113,8,128]{2,1,0:T(8,128)(2,1)S(1)}, u32[]{:S(2)}, u32[]{:S(2)}) collective-permute-start(bf16[113,8,128]{2,1,0:T(8,128)(2,1)S(1)} %collective-permute-done.4.refs_6_), channel_id=1, source_target_pairs={{0,128},{128,256},{256,384},{384,512},{512,640},{640,768},{768,896... | collective-permute-start | bytes 694280 | tf_op jit(solution)/shard_map/ppermute | solution.py:208
  72.1 9.1 %collective-permute-start.2 = (bf16[113,8,128]{2,1,0:T(8,128)(2,1)S(1)}, bf16[113,8,128]{2,1,0:T(8,128)(2,1)S(1)}, u32[]{:S(2)}, u32[]{:S(2)}) collective-permute-start(bf16[113,8,128]{2,1,0:T(8,128)(2,1)S(1)} %collective-permute-done.1.refs_2_), channel_id=1, source_target_pairs={{128,0},{256,128},{384,256},{512,384},{640,512},{768,640},{896,768... | collective-permute-start | bytes 694280 | tf_op jit(solution)/shard_map/ppermute | solution.py:211
  79.2 8.0 %collective-permute-start.6 = (bf16[113,8,128]{2,1,0:T(8,128)(2,1)S(1)}, bf16[113,8,128]{2,1,0:T(8,128)(2,1)S(1)}, u32[]{:S(2)}, u32[]{:S(2)}) collective-permute-start(bf16[113,8,128]{2,1,0:T(8,128)(2,1)S(1)} %collective-permute-done.5.refs_5_), channel_id=1, source_target_pairs={{0,128},{128,256},{256,384},{384,512},{512,640},{640,768},{768,896... | collective-permute-start | bytes 694280 | tf_op jit(solution)/shard_map/ppermute | solution.py:208
  87.2 1.0 copy-start.2
  138.8 15.1 %all-to-all-start.2 = ((bf16[16,16,128]{2,1,0:T(8,128)(2,1)}), bf16[16,16,128]{2,1,0:T(8,128)(2,1)S(1)}, u32[]{:S(2)}, u32[]{:S(2)}) async-start(bf16[16,16,128]{2,1,0:T(8,128)(2,1)} %shard_map.97), calls=%async_computation.2 | async-start | bytes 131072 | tf_op jit(solution)/shard_map/all_to_all | solution.py:294

commit v4 on v3

--- a/solution.py
+++ b/solution.py
@@ -55,13 +55,18 @@
     return jnp.where(upper(even.shape), odd, swap(even)).reshape(-1, v.shape[1])
 
 
-def lay_rows(my_y, blocks, rows):
+def block_home(place, index, count):
+    offset = jnp.where(place[2] == 0, index, count - index)
+    return lax.rem(place[0] + offset, count)
+
+
+def lay_rows(place, blocks, rows):
     count = len(blocks)
     tiles = rows.shape[1] // LANES
     for index, block in enumerate(blocks):
         per_y = block.shape[0] // tiles
         size = per_y * 8
-        base = pl.multiple_of(lax.rem(my_y + index, count) * size, size)
+        base = pl.multiple_of(block_home(place, index, count) * size, size)
         for k in range(tiles):
             tile = block[k * per_y : (k + 1) * per_y].astype(jnp.float32)
             rows[pl.ds(base, size), k * LANES : (k + 1) * LANES] = tile.reshape(
@@ -94,9 +99,11 @@
 
 
 def part_kernel(place, *refs):
-    *blocks, gate, up, down, part, weight, rows, spread = refs
+    *blocks, gate, up, down_far, part, weight, rows, spread, down, sem = refs
     f32 = jnp.float32
-    lay_rows(place[0], blocks, rows)
+    fetch = pltpu.make_async_copy(down_far, down, sem)
+    fetch.start()
+    lay_rows(place, blocks, rows)
     mat = rows[...]
     count = len(blocks)
     size = rows.shape[0] // count
@@ -107,12 +114,13 @@
     for index, block in enumerate(blocks):
         tags = jnp.broadcast_to(block[block.shape[0] - 1].astype(f32)[None], shape)
         tags = jnp.sum(jnp.where(lane == want, tags, 0.0), axis=2, keepdims=True)
-        base = pl.multiple_of(lax.rem(place[0] + index, count) * size, size)
+        base = pl.multiple_of(block_home(place, index, count) * size, size)
         spread[pl.ds(base, size), :] = jnp.broadcast_to(tags, shape).reshape(size, LANES)
     weight[...] = first_fours(spread[...])
     for index, mats in enumerate((gate, up)):
         out = jnp.dot(mat, mats[...], preferred_element_type=f32)
         part[:, index * LANES : (index + 1) * LANES] = first_fours(out).astype(part.dtype)
+    fetch.wait()
     out = lax.dot_general(mat, down[...], (((1,), (1,)), ((), ())), preferred_element_type=f32)
     part[:, 2 * LANES :] = last_fours(out).astype(part.dtype)
 
@@ -155,7 +163,7 @@
 
 def down_kernel(place, *refs):
     *blocks, wide, out, rows = refs
-    lay_rows(place[0], blocks, rows)
+    lay_rows(place, blocks, rows)
     out[...] = lax.dot_general(
         wide[...], rows[...], (((0,), (0,)), ((), ())), preferred_element_type=jnp.float32
     ).astype(out.dtype)
@@ -191,24 +199,48 @@
         pieces[m] = jnp.where(lane < sub, tile, tags).astype(pieces.dtype)
 
 
+def end_kernel(sub, final, ids, token_grad, route_grad, acc):
+    f32 = jnp.float32
+    toks, owners, _ = token_grad.shape
+    acc[...] = jnp.sum(final[...].astype(f32), axis=0)
+    for q in range(owners):
+        token_grad[:, q, :] = acc[q * toks : (q + 1) * toks, :sub].astype(token_grad.dtype)
+    routes = acc[:toks, :] + acc[toks : 2 * toks, :]
+    lane = lax.broadcasted_iota(jnp.int32, routes.shape, 1) - sub
+    cols = lax.broadcasted_iota(jnp.int32, ids.shape, 1)
+    out = jnp.zeros(ids.shape, f32)
+    for k in range(ids.shape[1]):
+        hit = jnp.sum(jnp.where(lane == ids[:, k : k + 1], routes, 0.0), axis=1, keepdims=True)
+        out = jnp.where(cols == k, hit, out)
+    route_grad[...] = out
+
+
 def weight_table(expert_ids, route_weights, experts):
     onehot = expert_ids[:, :, None] == jnp.arange(experts, dtype=jnp.int32)[None, None, :]
     weights = jnp.where(onehot, route_weights.astype(jnp.float32)[:, :, None], 0.0)
-    return jnp.sum(weights, axis=1).astype(jnp.bfloat16), onehot
+    return jnp.sum(weights, axis=1).astype(jnp.bfloat16)
 
 
 def y_ring(block):
     count = lax.axis_size("y")
-    up = [(i, (i + 1) % count) for i in range(count)]
-    down = [((i + 1) % count, i) for i in range(count)]
+    axes = ("y", "c")
+
+    def route(turn):
+        hops = []
+        for y in range(count):
+            for c in range(2):
+                step = turn if c == 0 else -turn
+                hops.append((2 * y + c, 2 * ((y + step) % count) + c))
+        return hops
+
     blocks = [None] * count
     blocks[0] = block
     fwd = bwd = block
     for step in range(1, count // 2 + 1):
-        fwd = lax.ppermute(fwd, "y", up)
+        fwd = lax.ppermute(fwd, axes, route(1))
         blocks[(-step) % count] = fwd
         if step < count // 2:
-            bwd = lax.ppermute(bwd, "y", down)
+            bwd = lax.ppermute(bwd, axes, route(-1))
             blocks[step] = bwd
     return blocks
 
@@ -223,9 +255,9 @@
     tall = 2 * toks
     my_y = lax.axis_index("y")
     expert = my_y * nxh + lax.axis_index("xh")
-    place = jnp.stack([my_y, expert]).astype(jnp.int32)
-
-    table, onehot = weight_table(expert_ids, route_weights, experts)
+    place = jnp.stack([my_y, expert, lax.axis_index("c")]).astype(jnp.int32)
+
+    table = weight_table(expert_ids, route_weights, experts)
     x_rows = jnp.concatenate(
         [tokens.transpose(1, 0, 2), jnp.broadcast_to(table[None], (OWNERS, toks, experts))], axis=2
     )
@@ -254,8 +286,13 @@
             jax.ShapeDtypeStruct((slots, 3 * LANES), bf16),
             jax.ShapeDtypeStruct((slots, LANES), f32),
         ),
-        [smem] + whole(ny + 3),
-        [rows, pltpu.VMEM((groups * tall, LANES), f32)],
+        [smem] + whole(ny + 2) + [pl.BlockSpec(memory_space=pl.ANY)],
+        [
+            rows,
+            pltpu.VMEM((groups * tall, LANES), f32),
+            pltpu.VMEM((LANES, nz * sub), bf16),
+            pltpu.SemaphoreType.DMA,
+        ],
         2 * groups * tall * nz * LANES * 3 * LANES,
         4 << 20,
     )(place, *blocks, w_gate[0], w_up[0], w_down[0])
@@ -292,10 +329,17 @@
         1 << 20,
     )(landed.reshape(experts, OWNERS, tiles + 1, toks, LANES))
     final = lax.all_to_all(pieces, "z", 0, 0, tiled=True)
-    final = jnp.sum(final.astype(f32), axis=0)
-    token_grad = final[:, :sub].reshape(OWNERS, toks, sub).transpose(1, 0, 2).astype(bf16)
-    routes = final[:toks, sub:] + final[toks : 2 * toks, sub:]
-    route_grad = jnp.sum(jnp.where(onehot, routes[:, None, :], 0.0), axis=2)
+    token_grad, route_grad = call(
+        functools.partial(end_kernel, sub),
+        (
+            jax.ShapeDtypeStruct((toks, OWNERS, sub), bf16),
+            jax.ShapeDtypeStruct(expert_ids.shape, f32),
+        ),
+        whole(2),
+        [pltpu.VMEM((OWNERS * toks, LANES), f32)],
+        nz * OWNERS * toks * LANES,
+        1 << 17,
+    )(final, expert_ids)
     return token_grad, down_grad[None], route_grad
 
 

time: 157 us -> 158 us (level)
  waiting for transfers between devices: 24.2 us -> 16 us
  blocking collectives: 93.4 us -> 98.1 us
  starting transfers between devices: 26.4 us -> 30.8 us
  local copies, waits for them, and re-layouts: 2.37 us -> 0.14 us
  Pallas kernels: 6.5 us -> 8.62 us
    ppermute x7, waiting for transfers between devices: 14.6 us -> 6.47 us  [the longest x4 6.44 us: y_ring(): fwd = lax.ppermute(fwd, axes, route(1))]
    all_to_all x1, blocking collectives: 35.1 us -> 39.7 us  [body(): landed = lax.all_to_all(back, ('y', 'xh', 'xl', 'c'), 0, 0, tiled=True)]
    ppermute x7, starting transfers between devices: 22.9 us -> 26.2 us  [the longest x4 20.4 us: y_ring(): fwd = lax.ppermute(fwd, axes, route(1))]
    unnamed x13 -> x8, local copies, waits for them, and re-layouts: 2.25 us -> 0.02 us
where the time goes in v4:
time: 158 us; the launch traced here: 156 us
  blocking collectives  98.1 us (62%)
  starting transfers between devices  30.8 us (19%)
  waiting for transfers between devices  16 us (10%)
  Pallas kernels  8.62 us (5%)
  other arithmetic  1.62 us (1%)
    all_to_all x1, blocking collectives, body(): got = lax.all_to_all(send, ('xh', 'xl', 'c', 'z'), 0, 0, tiled=True)  47.1 us
    all_to_all x1, blocking collectives, body(): landed = lax.all_to_all(back, ('y', 'xh', 'xl', 'c'), 0, 0, tiled=True)  39.7 us
    ppermute x4, starting transfers between devices, y_ring(): fwd = lax.ppermute(fwd, axes, route(1))  20.4 us
    all_gather x1, blocking collectives, body(): quad = lax.all_gather(part, ('xl', 'c'), axis=0, tiled=False)  11.3 us
    all_to_all x1, waiting for transfers between devices, body(): final = lax.all_to_all(pieces, 'z', 0, 0, tiled=True)  9.52 us
    ppermute x4, waiting for transfers between devices, y_ring(): fwd = lax.ppermute(fwd, axes, route(1))  6.44 us
    ppermute x3, starting transfers between devices, y_ring(): bwd = lax.ppermute(bwd, axes, route(-1))  5.75 us
    all_to_all x1, starting transfers between devices, body(): final = lax.all_to_all(pieces, 'z', 0, 0, tiled=True)  4.62 us
  transfers between devices with their start and end apart: 8, of which 5 were waited for; matrix products, arithmetic and copies ran while one was open for 0% of the time, Pallas kernels for 1%

profile of v4, /device:TPU:1, one launch (start us, length us, event | category | flops | bytes accessed | tf_op | source)
XLA Modules:
  0.0 156.1 jit_solution(3322638528770576408)
XLA Ops:
  0.6 0.0 copy-start.3
  0.6 0.0 copy-start.2
  0.7 0.7 convert_element_type.12
  1.4 0.0 copy-done.3
  1.4 0.1 select_reduce_fusion
  1.5 0.1 pad.6.clone
  1.6 0.7 fusion.1
  2.3 0.0 copy-start
  2.3 0.0 copy-start.1
  2.4 47.1 %all_to_all.15 = bf16[128,8,128]{2,1,0:T(8,128)(2,1)S(1)} all-to-all(bf16[128,8,128]{2,1,0:T(8,128)(2,1)S(1)} %bitcast.21), channel_id=1, replica_groups=mesh['y'=8,'xh'=2,'xl'=2,'c'=2,'z'=16] {'xh','xl','c','z'}, dimensions={0} | all-to-all | bytes 524288 | tf_op jit(solution)/shard_map/all_to_all | solution.py:268
  49.5 0.2 shard_map.94.refs_0_
  49.7 5.1 %collective-permute-start.3 = (bf16[113,8,128]{2,1,0:T(8,128)(2,1)S(1)}, bf16[113,8,128]{2,1,0:T(8,128)(2,1)S(1)}, u32[]{:S(2)}, u32[]{:S(2)}) collective-permute-start(bf16[113,8,128]{2,1,0:T(8,128)(2,1)S(1)} %shard_map.94.refs_0_), channel_id=1, source_target_pairs={{0,128},{16,912},{128,256},{144,16},{256,384},{272,144},{384,512},... | collective-permute-start | bytes 694280 | tf_op jit(solution)/shard_map/ppermute | solution.py:240
  54.8 1.9 %collective-permute-start = (bf16[113,8,128]{2,1,0:T(8,128)(2,1)S(1)}, bf16[113,8,128]{2,1,0:T(8,128)(2,1)S(1)}, u32[]{:S(2)}, u32[]{:S(2)}) collective-permute-start(bf16[113,8,128]{2,1,0:T(8,128)(2,1)S(1)} %shard_map.94.refs_0_), channel_id=1, source_target_pairs={{0,896},{16,144},{128,0},{144,272},{256,128},{272,400},{384,256},{... | collective-permute-start | bytes 694280 | tf_op jit(solution)/shard_map/ppermute | solution.py:243
  56.7 1.5 collective-permute-done.3.refs_7_
  58.2 5.3 %collective-permute-start.4 = (bf16[113,8,128]{2,1,0:T(8,128)(2,1)S(1)}, bf16[113,8,128]{2,1,0:T(8,128)(2,1)S(1)}, u32[]{:S(2)}, u32[]{:S(2)}) collective-permute-start(bf16[113,8,128]{2,1,0:T(8,128)(2,1)S(1)} %collective-permute-done.3.refs_7_), channel_id=1, source_target_pairs={{0,128},{16,912},{128,256},{144,16},{256,384},{272,144},{384,512},... | collective-permute-start | bytes 694280 | tf_op jit(solution)/shard_map/ppermute | solution.py:240
  63.5 0.0 collective-permute-done.refs_1_
  63.5 1.9 %collective-permute-start.1 = (bf16[113,8,128]{2,1,0:T(8,128)(2,1)S(1)}, bf16[113,8,128]{2,1,0:T(8,128)(2,1)S(1)}, u32[]{:S(2)}, u32[]{:S(2)}) collective-permute-start(bf16[113,8,128]{2,1,0:T(8,128)(2,1)S(1)} %collective-permute-done.refs_1_), channel_id=1, source_target_pairs={{0,896},{16,144},{128,0},{144,272},{256,128},{272,400},{384,256},{... | collective-permute-start | bytes 694280 | tf_op jit(solution)/shard_map/ppermute | solution.py:243
  65.5 1.0 collective-permute-done.4.refs_6_
  66.5 5.0 %collective-permute-start.5 = (bf16[113,8,128]{2,1,0:T(8,128)(2,1)S(1)}, bf16[113,8,128]{2,1,0:T(8,128)(2,1)S(1)}, u32[]{:S(2)}, u32[]{:S(2)}) collective-permute-start(bf16[113,8,128]{2,1,0:T(8,128)(2,1)S(1)} %collective-permute-done.4.refs_6_), channel_id=1, source_target_pairs={{0,128},{16,912},{128,256},{144,16},{256,384},{272,144},{384,512},... | collective-permute-start | bytes 694280 | tf_op jit(solution)/shard_map/ppermute | solution.py:240
  71.5 0.0 collective-permute-done.1.refs_2_
  71.5 1.9 %collective-permute-start.2 = (bf16[113,8,128]{2,1,0:T(8,128)(2,1)S(1)}, bf16[113,8,128]{2,1,0:T(8,128)(2,1)S(1)}, u32[]{:S(2)}, u32[]{:S(2)}) collective-permute-start(bf16[113,8,128]{2,1,0:T(8,128)(2,1)S(1)} %collective-permute-done.1.refs_2_), channel_id=1, source_target_pairs={{0,896},{16,144},{128,0},{144,272},{256,128},{272,400},{384,256},{... | collective-permute-start | bytes 694280 | tf_op jit(solution)/shard_map/ppermute | solution.py:243
  73.5 1.0 collective-permute-done.5.refs_5_
  74.5 5.0 %collective-permute-start.6 = (bf16[113,8,128]{2,1,0:T(8,128)(2,1)S(1)}, bf16[113,8,128]{2,1,0:T(8,128)(2,1)S(1)}, u32[]{:S(2)}, u32[]{:S(2)}) collective-permute-start(bf16[113,8,128]{2,1,0:T(8,128)(2,1)S(1)} %collective-permute-done.5.refs_5_), channel_id=1, source_target_pairs={{0,128},{16,912},{128,256},{144,16},{256,384},{272,144},{384,512},... | collective-permute-start | bytes 694280 | tf_op jit(solution)/shard_map/ppermute | solution.py:240
  79.5 0.1 pad_add_fusion.place
  79.6 0.0 collective-permute-done.2.refs_3_
  79.6 2.9 %collective-permute-done.6.refs_4_ = bf16[113,8,128]{2,1,0:T(8,128)(2,1)S(1)} collective-permute-done((bf16[113,8,128]{2,1,0:T(8,128)(2,1)S(1)}, bf16[113,8,128]{2,1,0:T(8,128)(2,1)S(1)}, u32[]{:S(2)}, u32[]{:S(2)}) %collective-permute-start.6) | collective-permute-done | bytes 231456 | tf_op jit(solution)/shard_map/ppermute | solution.py:240
  82.5 0.0 copy-done.2
  82.5 0.0 copy-done
  82.5 0.0 copy-done.1
  82.5 3.8 %shard_map.95 = (bf16[256,384]{1,0:T(8,128)(2,1)S(1)}, f32[256,128]{1,0:T(8,128)S(1)}) custom-call(s32[3]{0:T(128)S(1)} %pad_add_fusion.place, bf16[113,8,128]{2,1,0:T(8,128)(2,1)S(1)} %shard_map.94.refs_0_, bf16[113,8,128]{2,1,0:T(8,128)(2,1)S(1)} %collective-permute-done.refs_1_, bf16[113,8,128]{2,1,0:T(8,128)(2,1)S(1)} %collective-permute-done.1.refs_2_, ...), custom_call_target="tpu_custom_call" | custom-call | flops 805306368 | bytes 4194304 | tf_op jit(solution)/shard_map/pallas_call | solution.py:283
  86.3 11.3 %all-gather = bf16[1024,384]{1,0:T(8,128)(2,1)S(1)} all-gather(bf16[256,384]{1,0:T(8,128)(2,1)S(1)} %get-tuple-element.9), channel_id=2, replica_groups=mesh['y'=8,'xh'=2,'xl'=2,'c'=2,'z'=16] {'xl','c'}, dimensions={0}, use_global_device_ids=true | all-gather | bytes 983040 | tf_op jit(solution)/shard_map/all_gather | solution.py:300
  97.6 0.7 shard_map.96
  98.3 39.7 %all_to_all.16 = bf16[64,15,4,128]{3,2,1,0:T(4,128)(2,1)S(1)} all-to-all(bf16[64,15,4,128]{3,2,1,0:T(4,128)(2,1)S(1)} %get-tuple-element.11), channel_id=1, replica_groups=mesh['y'=8,'xh'=2,'xl'=2,'c'=2,'z'=16] {'y','xh','xl','c'}, dimensions={0} | all-to-all | bytes 1966080 | tf_op jit(solution)/shard_map/all_to_all | solution.py:313
  138.1 1.1 shard_map.97
  139.1 4.6 %all-to-all-start.2 = ((bf16[16,16,128]{2,1,0:T(8,128)(2,1)}), bf16[16,16,128]{2,1,0:T(8,128)(2,1)S(1)}, u32[]{:S(2)}, u32[]{:S(2)}) async-start(bf16[16,16,128]{2,1,0:T(8,128)(2,1)} %shard_map.97), calls=%async_computation.2 | async-start | bytes 131072 | tf_op jit(solution)/shard_map/all_to_all | solution.py:331
  143.8 2.1 %shard_map.99 = bf16[128,1792]{1,0:T(8,128)(2,1)} custom-call(s32[3]{0:T(128)S(1)} %pad_add_fusion.place, bf16[113,8,128]{2,1,0:T(8,128)(2,1)S(1)} %shard_map.94.refs_0_, bf16[113,8,128]{2,1,0:T(8,128)(2,1)S(1)} %collective-permute-done.refs_1_, bf16[113,8,128]{2,1,0:T(8,128)(2,1)S(1)} %collective-permute-done.1.refs_2_, ...), custom_call_target="tpu_custom_call" | custom-call | flops 268435456 | bytes 4194304 | tf_op jit(solution)/shard_map/pallas_call | solution.py:315
  145.8 9.5 %all-to-all-done.2.final = bf16[16,16,128]{2,1,0:T(8,128)(2,1)S(1)} async-done(((bf16[16,16,128]{2,1,0:T(8,128)(2,1)}), bf16[16,16,128]{2,1,0:T(8,128)(2,1)S(1)}, u32[]{:S(2)}, u32[]{:S(2)}) %all-to-all-start.2) | async-done | bytes 65568 | tf_op jit(solution)/shard_map/all_to_all | solution.py:331
  155.4 0.7 shard_map.98
  (2 shorter events, 0.0 us)
Async XLA Ops:
  0.6 0.8 copy-start.3
  0.6 81.8 %copy-start.2 = (bf16[1,128,1792]{2,1,0:T(8,128)(2,1)S(1)}, bf16[1,128,1792]{2,1,0:T(8,128)(2,1)}, u32[]{:S(2)}) copy-start(bf16[1,128,1792]{2,1,0:T(8,128)(2,1)} %param.13) | copy-start | bytes 1376260
  2.3 80.1 %copy-start = (bf16[1,1792,128]{2,1,0:T(8,128)(2,1)S(1)}, bf16[1,1792,128]{2,1,0:T(8,128)(2,1)}, u32[]{:S(2)}) copy-start(bf16[1,1792,128]{2,1,0:T(8,128)(2,1)} %param.11) | copy-start | bytes 1376260
  2.3 80.1 %copy-start.1 = (bf16[1,1792,128]{2,1,0:T(8,128)(2,1)S(1)}, bf16[1,1792,128]{2,1,0:T(8,128)(2,1)}, u32[]{:S(2)}) copy-start(bf16[1,1792,128]{2,1,0:T(8,128)(2,1)} %param.12) | copy-start | bytes 1376260
  49.7 8.5 %collective-permute-start.3 = (bf16[113,8,128]{2,1,0:T(8,128)(2,1)S(1)}, bf16[113,8,128]{2,1,0:T(8,128)(2,1)S(1)}, u32[]{:S(2)}, u32[]{:S(2)}) collective-permute-start(bf16[113,8,128]{2,1,0:T(8,128)(2,1)S(1)} %shard_map.94.refs_0_), channel_id=1, source_target_pairs={{0,128},{16,912},{128,256},{144,16},{256,384},{272,144},{384,512},... | collective-permute-start | bytes 694280 | tf_op jit(solution)/shard_map/ppermute | solution.py:240
  54.8 8.8 %collective-permute-start = (bf16[113,8,128]{2,1,0:T(8,128)(2,1)S(1)}, bf16[113,8,128]{2,1,0:T(8,128)(2,1)S(1)}, u32[]{:S(2)}, u32[]{:S(2)}) collective-permute-start(bf16[113,8,128]{2,1,0:T(8,128)(2,1)S(1)} %shard_map.94.refs_0_), channel_id=1, source_target_pairs={{0,896},{16,144},{128,0},{144,272},{256,128},{272,400},{384,256},{... | collective-permute-start | bytes 694280 | tf_op jit(solution)/shard_map/ppermute | solution.py:243
  58.2 8.3 %collective-permute-start.4 = (bf16[113,8,128]{2,1,0:T(8,128)(2,1)S(1)}, bf16[113,8,128]{2,1,0:T(8,128)(2,1)S(1)}, u32[]{:S(2)}, u32[]{:S(2)}) collective-permute-start(bf16[113,8,128]{2,1,0:T(8,128)(2,1)S(1)} %collective-permute-done.3.refs_7_), channel_id=1, source_target_pairs={{0,128},{16,912},{128,256},{144,16},{256,384},{272,144},{384,512},... | collective-permute-start | bytes 694280 | tf_op jit(solution)/shard_map/ppermute | solution.py:240
  63.5 8.0 %collective-permute-start.1 = (bf16[113,8,128]{2,1,0:T(8,128)(2,1)S(1)}, bf16[113,8,128]{2,1,0:T(8,128)(2,1)S(1)}, u32[]{:S(2)}, u32[]{:S(2)}) collective-permute-start(bf16[113,8,128]{2,1,0:T(8,128)(2,1)S(1)} %collective-permute-done.refs_1_), channel_id=1, source_target_pairs={{0,896},{16,144},{128,0},{144,272},{256,128},{272,400},{384,256},{... | collective-permute-start | bytes 694280 | tf_op jit(solution)/shard_map/ppermute | solution.py:243
  66.5 8.0 %collective-permute-start.5 = (bf16[113,8,128]{2,1,0:T(8,128)(2,1)S(1)}, bf16[113,8,128]{2,1,0:T(8,128)(2,1)S(1)}, u32[]{:S(2)}, u32[]{:S(2)}) collective-permute-start(bf16[113,8,128]{2,1,0:T(8,128)(2,1)S(1)} %collective-permute-done.4.refs_6_), channel_id=1, source_target_pairs={{0,128},{16,912},{128,256},{144,16},{256,384},{272,144},{384,512},... | collective-permute-start | bytes 694280 | tf_op jit(solution)/shard_map/ppermute | solution.py:240
  71.5 8.1 %collective-permute-start.2 = (bf16[113,8,128]{2,1,0:T(8,128)(2,1)S(1)}, bf16[113,8,128]{2,1,0:T(8,128)(2,1)S(1)}, u32[]{:S(2)}, u32[]{:S(2)}) collective-permute-start(bf16[113,8,128]{2,1,0:T(8,128)(2,1)S(1)} %collective-permute-done.1.refs_2_), channel_id=1, source_target_pairs={{0,896},{16,144},{128,0},{144,272},{256,128},{272,400},{384,256},{... | collective-permute-start | bytes 694280 | tf_op jit(solution)/shard_map/ppermute | solution.py:243
  74.5 8.0 %collective-permute-start.6 = (bf16[113,8,128]{2,1,0:T(8,128)(2,1)S(1)}, bf16[113,8,128]{2,1,0:T(8,128)(2,1)S(1)}, u32[]{:S(2)}, u32[]{:S(2)}) collective-permute-start(bf16[113,8,128]{2,1,0:T(8,128)(2,1)S(1)} %collective-permute-done.5.refs_5_), channel_id=1, source_target_pairs={{0,128},{16,912},{128,256},{144,16},{256,384},{272,144},{384,512},... | collective-permute-start | bytes 694280 | tf_op jit(solution)/shard_map/ppermute | solution.py:240
  139.1 16.2 %all-to-all-start.2 = ((bf16[16,16,128]{2,1,0:T(8,128)(2,1)}), bf16[16,16,128]{2,1,0:T(8,128)(2,1)S(1)}, u32[]{:S(2)}, u32[]{:S(2)}) async-start(bf16[16,16,128]{2,1,0:T(8,128)(2,1)} %shard_map.97), calls=%async_computation.2 | async-start | bytes 131072 | tf_op jit(solution)/shard_map/all_to_all | solution.py:331

commit v5 on v4

--- a/solution.py
+++ b/solution.py
@@ -55,9 +55,26 @@
     return jnp.where(upper(even.shape), odd, swap(even)).reshape(-1, v.shape[1])
 
 
+def block_offsets(count):
+    offsets = [0, 1]
+    for step in range(1, count // 2):
+        if step % 2:
+            offsets += [-step, -step - 1]
+        else:
+            offsets += [step, step + 1]
+    return offsets
+
+
 def block_home(place, index, count):
-    offset = jnp.where(place[2] == 0, index, count - index)
-    return lax.rem(place[0] + offset, count)
+    offset = block_offsets(count)[index]
+    return lax.rem(place[0] + place[2] * offset + count, count)
+
+
+def split_blocks(refs):
+    blocks = list(refs[:2])
+    for ref in refs[2:]:
+        blocks += [ref.at[0], ref.at[1]]
+    return blocks
 
 
 def lay_rows(place, blocks, rows):
@@ -99,10 +116,9 @@
 
 
 def part_kernel(place, *refs):
-    *blocks, gate, up, down_far, part, weight, rows, spread, down, sem = refs
+    *blocks, gate, up, down, part, weight, rows, spread = refs
+    blocks = split_blocks(blocks)
     f32 = jnp.float32
-    fetch = pltpu.make_async_copy(down_far, down, sem)
-    fetch.start()
     lay_rows(place, blocks, rows)
     mat = rows[...]
     count = len(blocks)
@@ -120,7 +136,6 @@
     for index, mats in enumerate((gate, up)):
         out = jnp.dot(mat, mats[...], preferred_element_type=f32)
         part[:, index * LANES : (index + 1) * LANES] = first_fours(out).astype(part.dtype)
-    fetch.wait()
     out = lax.dot_general(mat, down[...], (((1,), (1,)), ((), ())), preferred_element_type=f32)
     part[:, 2 * LANES :] = last_fours(out).astype(part.dtype)
 
@@ -163,6 +178,7 @@
 
 def down_kernel(place, *refs):
     *blocks, wide, out, rows = refs
+    blocks = split_blocks(blocks)
     lay_rows(place, blocks, rows)
     out[...] = lax.dot_general(
         wide[...], rows[...], (((0,), (0,)), ((), ())), preferred_element_type=jnp.float32
@@ -221,28 +237,25 @@
     return jnp.sum(weights, axis=1).astype(jnp.bfloat16)
 
 
-def y_ring(block):
+def swap_with(block, toward):
     count = lax.axis_size("y")
-    axes = ("y", "c")
-
-    def route(turn):
-        hops = []
-        for y in range(count):
-            for c in range(2):
-                step = turn if c == 0 else -turn
-                hops.append((2 * y + c, 2 * ((y + step) % count) + c))
-        return hops
-
-    blocks = [None] * count
-    blocks[0] = block
-    fwd = bwd = block
-    for step in range(1, count // 2 + 1):
-        fwd = lax.ppermute(fwd, axes, route(1))
-        blocks[(-step) % count] = fwd
-        if step < count // 2:
-            bwd = lax.ppermute(bwd, axes, route(-1))
-            blocks[step] = bwd
-    return blocks
+    hops = []
+    for y in range(count):
+        for c in range(2):
+            step = 1 if (y + c) % 2 == 0 else -1
+            step = step if toward else -step
+            hops.append((2 * y + c, 2 * ((y + step) % count) + c))
+    return lax.ppermute(block, ("y", "c"), hops)
+
+
+def y_gather(block):
+    first = swap_with(block, True)
+    pair = swap_with(jnp.stack([block, first]), False)
+    found = [block, first, pair]
+    for step in range(2, lax.axis_size("y") // 2):
+        pair = swap_with(pair, step % 2 == 0)
+        found.append(pair)
+    return found
 
 
 def body(tokens, out_grad, route_weights, expert_ids, w_gate, w_up, w_down):
@@ -255,7 +268,8 @@
     tall = 2 * toks
     my_y = lax.axis_index("y")
     expert = my_y * nxh + lax.axis_index("xh")
-    place = jnp.stack([my_y, expert, lax.axis_index("c")]).astype(jnp.int32)
+    turn = 1 - 2 * lax.rem(my_y + lax.axis_index("c"), 2)
+    place = jnp.stack([my_y, expert, turn]).astype(jnp.int32)
 
     table = weight_table(expert_ids, route_weights, experts)
     x_rows = jnp.concatenate(
@@ -275,7 +289,7 @@
         groups * tall * LANES,
         1 << 19,
     )(got.reshape(per_y, nz, tall, LANES))
-    blocks = y_ring(block)
+    blocks = y_gather(block)
 
     smem = pl.BlockSpec(memory_space=pltpu.SMEM)
     slots = groups * toks
@@ -286,13 +300,8 @@
             jax.ShapeDtypeStruct((slots, 3 * LANES), bf16),
             jax.ShapeDtypeStruct((slots, LANES), f32),
         ),
-        [smem] + whole(ny + 2) + [pl.BlockSpec(memory_space=pl.ANY)],
-        [
-            rows,
-            pltpu.VMEM((groups * tall, LANES), f32),
-            pltpu.VMEM((LANES, nz * sub), bf16),
-            pltpu.SemaphoreType.DMA,
-        ],
+        [smem] + whole(len(blocks) + 3),
+        [rows, pltpu.VMEM((groups * tall, LANES), f32)],
         2 * groups * tall * nz * LANES * 3 * LANES,
         4 << 20,
     )(place, *blocks, w_gate[0], w_up[0], w_down[0])
@@ -315,7 +324,7 @@
     down_grad = call(
         down_kernel,
         jax.ShapeDtypeStruct((LANES, nz * sub), bf16),
-        [smem] + whole(ny + 1),
+        [smem] + whole(len(blocks) + 1),
         [rows],
         2 * groups * tall * nz * LANES * LANES,
         4 << 20,

time: 158 us -> 156 us (0.987)
  waiting for transfers between devices: 16 us -> 34 us
  starting transfers between devices: 30.8 us -> 17.6 us
  blocking collectives: 98.1 us -> 93.2 us
    ppermute x7 -> x4, waiting for transfers between devices: 6.47 us -> 24.5 us  [swap_with(): return lax.ppermute(block, ('y', 'c'), hops)]
    ppermute x7 -> x4, starting transfers between devices: 26.2 us -> 13.6 us  [swap_with(): return lax.ppermute(block, ('y', 'c'), hops)]
    all_to_all x1, blocking collectives: 39.7 us -> 35.2 us  [body(): landed = lax.all_to_all(back, ('y', 'xh', 'xl', 'c'), 0, 0, tiled=True)]
  transfers between devices with their start and end apart: 8 -> 5, of which waited for: 5 -> 5; matrix products, arithmetic and copies ran while one was open for 0% -> 0% of each run, Pallas kernels for 1% -> 1%
where the time goes in v5:
time: 156 us; the launch traced here: 154 us
  blocking collectives  93.2 us (60%)
  waiting for transfers between devices  34 us (22%)
  starting transfers between devices  17.6 us (11%)
  Pallas kernels  7.24 us (5%)
    all_to_all x1, blocking collectives, body(): got = lax.all_to_all(send, ('xh', 'xl', 'c', 'z'), 0, 0, tiled=True)  47 us
    all_to_all x1, blocking collectives, body(): landed = lax.all_to_all(back, ('y', 'xh', 'xl', 'c'), 0, 0, tiled=True)  35.2 us
    ppermute x4, waiting for transfers between devices, swap_with(): return lax.ppermute(block, ('y', 'c'), hops)  24.5 us
    ppermute x4, starting transfers between devices, swap_with(): return lax.ppermute(block, ('y', 'c'), hops)  13.6 us
    all_gather x1, blocking collectives, body(): quad = lax.all_gather(part, ('xl', 'c'), axis=0, tiled=False)  11 us
    all_to_all x1, waiting for transfers between devices, body(): final = lax.all_to_all(pieces, 'z', 0, 0, tiled=True)  9.53 us
    all_to_all x1, starting transfers between devices, body(): final = lax.all_to_all(pieces, 'z', 0, 0, tiled=True)  3.95 us
  transfers between devices with their start and end apart: 5, of which 5 were waited for; matrix products, arithmetic and copies ran while one was open for 0% of the time, Pallas kernels for 1%

profile of v5, /device:TPU:1, one launch (start us, length us, event | category | flops | bytes accessed | tf_op | source)
XLA Modules:
  0.0 154.4 jit_solution(9856616604281686260)
XLA Ops:
  0.6 0.0 copy-start.3
  0.6 0.7 convert_element_type.12
  1.3 0.0 copy-done.3
  1.3 0.0 copy-start.5
  1.3 0.1 select_reduce_fusion
  1.4 0.0 copy-start.4
  1.4 0.1 pad.8.clone
  1.5 0.5 copy-done.5
  2.0 0.1 copy-done.4
  2.2 47.0 %all_to_all.15 = bf16[128,8,128]{2,1,0:T(8,128)(2,1)S(1)} all-to-all(bf16[128,8,128]{2,1,0:T(8,128)(2,1)S(1)} %bitcast.25), channel_id=1, replica_groups=mesh['y'=8,'xh'=2,'xl'=2,'c'=2,'z'=16] {'xh','xl','c','z'}, dimensions={0} | all-to-all | bytes 524288 | tf_op jit(solution)/shard_map/all_to_all | solution.py:282
  49.2 0.0 copy-start.2
  49.2 0.2 shard_map.94.refs_0_
  49.4 5.1 %collective-permute-start = (bf16[113,8,128]{2,1,0:T(8,128)(2,1)S(1)}, bf16[113,8,128]{2,1,0:T(8,128)(2,1)S(1)}, u32[]{:S(2)}, u32[]{:S(2)}) collective-permute-start(bf16[113,8,128]{2,1,0:T(8,128)(2,1)S(1)} %shard_map.94.refs_0_), channel_id=1, source_target_pairs={{0,128},{16,912},{128,0},{144,272},{256,384},{272,144},{384,256},{... | collective-permute-start | bytes 694280 | tf_op jit(solution)/shard_map/ppermute | solution.py:248
  54.5 3.4 %collective-permute-done.refs_1_ = bf16[113,8,128]{2,1,0:T(8,128)(2,1)S(1)} collective-permute-done((bf16[113,8,128]{2,1,0:T(8,128)(2,1)S(1)}, bf16[113,8,128]{2,1,0:T(8,128)(2,1)S(1)}, u32[]{:S(2)}, u32[]{:S(2)}) %collective-permute-start) | collective-permute-done | bytes 231456 | tf_op jit(solution)/shard_map/ppermute | solution.py:248
  57.9 0.0 copy-start
  57.9 0.0 copy-start.1
  57.9 2.1 %collective-permute-start.1 = (bf16[2,113,8,128]{3,2,1,0:T(8,128)(2,1)S(1)}, bf16[2,113,8,128]{3,2,1,0:T(8,128)(2,1)S(1)}, u32[]{:S(2)}, u32[]{:S(2)}) collective-permute-start(bf16[2,113,8,128]{3,2,1,0:T(8,128)(2,1)S(1)} %pad_maximum_fusion), channel_id=1, source_target_pairs={{0,896},{16,144},{128,256},{144,16},{256,128},{272,400},{384,512},... | collective-permute-start | bytes 1388552 | tf_op jit(solution)/shard_map/ppermute | solution.py:248
  60.0 7.6 %collective-permute-done.1.refs_2_ = bf16[2,113,8,128]{3,2,1,0:T(8,128)(2,1)S(1)} collective-permute-done((bf16[2,113,8,128]{3,2,1,0:T(8,128)(2,1)S(1)}, bf16[2,113,8,128]{3,2,1,0:T(8,128)(2,1)S(1)}, u32[]{:S(2)}, u32[]{:S(2)}) %collective-permute-start.1) | collective-permute-done | bytes 462880 | tf_op jit(solution)/shard_map/ppermute | solution.py:248
  67.6 4.6 %collective-permute-start.2 = (bf16[2,113,8,128]{3,2,1,0:T(8,128)(2,1)S(1)}, bf16[2,113,8,128]{3,2,1,0:T(8,128)(2,1)S(1)}, u32[]{:S(2)}, u32[]{:S(2)}) collective-permute-start(bf16[2,113,8,128]{3,2,1,0:T(8,128)(2,1)S(1)} %collective-permute-done.1.refs_2_), channel_id=1, source_target_pairs={{0,128},{16,912},{128,0},{144,272},{256,384},{272,144},{384,256},{... | collective-permute-start | bytes 1388552 | tf_op jit(solution)/shard_map/ppermute | solution.py:248
  72.2 5.9 %collective-permute-done.2.refs_3_ = bf16[2,113,8,128]{3,2,1,0:T(8,128)(2,1)S(1)} collective-permute-done((bf16[2,113,8,128]{3,2,1,0:T(8,128)(2,1)S(1)}, bf16[2,113,8,128]{3,2,1,0:T(8,128)(2,1)S(1)}, u32[]{:S(2)}, u32[]{:S(2)}) %collective-permute-start.2) | collective-permute-done | bytes 462880 | tf_op jit(solution)/shard_map/ppermute | solution.py:248
  78.1 1.9 %collective-permute-start.3 = (bf16[2,113,8,128]{3,2,1,0:T(8,128)(2,1)S(1)}, bf16[2,113,8,128]{3,2,1,0:T(8,128)(2,1)S(1)}, u32[]{:S(2)}, u32[]{:S(2)}) collective-permute-start(bf16[2,113,8,128]{3,2,1,0:T(8,128)(2,1)S(1)} %collective-permute-done.2.refs_3_), channel_id=1, source_target_pairs={{0,896},{16,144},{128,256},{144,16},{256,128},{272,400},{384,512},... | collective-permute-start | bytes 1388552 | tf_op jit(solution)/shard_map/ppermute | solution.py:248
  80.0 0.1 pad_add_fusion.place
  80.1 7.5 %collective-permute-done.3.refs_4_ = bf16[2,113,8,128]{3,2,1,0:T(8,128)(2,1)S(1)} collective-permute-done((bf16[2,113,8,128]{3,2,1,0:T(8,128)(2,1)S(1)}, bf16[2,113,8,128]{3,2,1,0:T(8,128)(2,1)S(1)}, u32[]{:S(2)}, u32[]{:S(2)}) %collective-permute-start.3) | collective-permute-done | bytes 462880 | tf_op jit(solution)/shard_map/ppermute | solution.py:248
  87.6 0.0 copy-done.2
  87.7 0.0 copy-done
  87.7 0.0 copy-done.1
  87.7 2.4 %shard_map.95 = (bf16[256,384]{1,0:T(8,128)(2,1)S(1)}, f32[256,128]{1,0:T(8,128)S(1)}) custom-call(s32[3]{0:T(128)S(1)} %pad_add_fusion.place, bf16[113,8,128]{2,1,0:T(8,128)(2,1)S(1)} %shard_map.94.refs_0_, bf16[113,8,128]{2,1,0:T(8,128)(2,1)S(1)} %collective-permute-done.refs_1_, bf16[2,113,8,128]{3,2,1,0:T(8,128)(2,1)S(1)} %collective-permute-done.1.refs_2_, ...), custom_call_target="tpu_custom_call" | custom-call | flops 805306368 | bytes 4194304 | tf_op jit(solution)/shard_map/pallas_call | solution.py:297
  90.1 11.0 %all-gather = bf16[1024,384]{1,0:T(8,128)(2,1)S(1)} all-gather(bf16[256,384]{1,0:T(8,128)(2,1)S(1)} %get-tuple-element.9), channel_id=2, replica_groups=mesh['y'=8,'xh'=2,'xl'=2,'c'=2,'z'=16] {'xl','c'}, dimensions={0}, use_global_device_ids=true | all-gather | bytes 983040 | tf_op jit(solution)/shard_map/all_gather | solution.py:309
  101.1 0.7 shard_map.96
  101.9 35.2 %all_to_all.16 = bf16[64,15,4,128]{3,2,1,0:T(4,128)(2,1)S(1)} all-to-all(bf16[64,15,4,128]{3,2,1,0:T(4,128)(2,1)S(1)} %get-tuple-element.11), channel_id=1, replica_groups=mesh['y'=8,'xh'=2,'xl'=2,'c'=2,'z'=16] {'y','xh','xl','c'}, dimensions={0} | all-to-all | bytes 1966080 | tf_op jit(solution)/shard_map/all_to_all | solution.py:322
  137.0 1.1 shard_map.97
  138.1 4.0 %all-to-all-start.2 = ((bf16[16,16,128]{2,1,0:T(8,128)(2,1)}), bf16[16,16,128]{2,1,0:T(8,128)(2,1)S(1)}, u32[]{:S(2)}, u32[]{:S(2)}) async-start(bf16[16,16,128]{2,1,0:T(8,128)(2,1)} %shard_map.97), calls=%async_computation.2 | async-start | bytes 131072 | tf_op jit(solution)/shard_map/all_to_all | solution.py:340
  142.1 2.1 %shard_map.99 = bf16[128,1792]{1,0:T(8,128)(2,1)} custom-call(s32[3]{0:T(128)S(1)} %pad_add_fusion.place, bf16[113,8,128]{2,1,0:T(8,128)(2,1)S(1)} %shard_map.94.refs_0_, bf16[113,8,128]{2,1,0:T(8,128)(2,1)S(1)} %collective-permute-done.refs_1_, bf16[2,113,8,128]{3,2,1,0:T(8,128)(2,1)S(1)} %collective-permute-done.1.refs_2_, ...), custom_call_target="tpu_custom_call" | custom-call | flops 268435456 | bytes 4194304 | tf_op jit(solution)/shard_map/pallas_call | solution.py:324
  144.1 9.5 %all-to-all-done.2.final = bf16[16,16,128]{2,1,0:T(8,128)(2,1)S(1)} async-done(((bf16[16,16,128]{2,1,0:T(8,128)(2,1)}), bf16[16,16,128]{2,1,0:T(8,128)(2,1)S(1)}, u32[]{:S(2)}, u32[]{:S(2)}) %all-to-all-start.2) | async-done | bytes 65568 | tf_op jit(solution)/shard_map/all_to_all | solution.py:340
  153.7 0.7 shard_map.98
  (4 shorter events, 0.1 us)
Async XLA Ops:
  0.6 0.7 copy-start.3
  1.3 0.7 copy-start.5
  1.4 0.7 copy-start.4
  49.2 38.5 %copy-start.2 = (bf16[1,128,1792]{2,1,0:T(8,128)(2,1)S(1)}, bf16[1,128,1792]{2,1,0:T(8,128)(2,1)}, u32[]{:S(2)}) copy-start(bf16[1,128,1792]{2,1,0:T(8,128)(2,1)} %param.13) | copy-start | bytes 1376260
  49.4 8.5 %collective-permute-start = (bf16[113,8,128]{2,1,0:T(8,128)(2,1)S(1)}, bf16[113,8,128]{2,1,0:T(8,128)(2,1)S(1)}, u32[]{:S(2)}, u32[]{:S(2)}) collective-permute-start(bf16[113,8,128]{2,1,0:T(8,128)(2,1)S(1)} %shard_map.94.refs_0_), channel_id=1, source_target_pairs={{0,128},{16,912},{128,0},{144,272},{256,384},{272,144},{384,256},{... | collective-permute-start | bytes 694280 | tf_op jit(solution)/shard_map/ppermute | solution.py:248
  57.9 29.8 %copy-start = (bf16[1,1792,128]{2,1,0:T(8,128)(2,1)S(1)}, bf16[1,1792,128]{2,1,0:T(8,128)(2,1)}, u32[]{:S(2)}) copy-start(bf16[1,1792,128]{2,1,0:T(8,128)(2,1)} %param.11) | copy-start | bytes 1376260
  57.9 29.8 %copy-start.1 = (bf16[1,1792,128]{2,1,0:T(8,128)(2,1)S(1)}, bf16[1,1792,128]{2,1,0:T(8,128)(2,1)}, u32[]{:S(2)}) copy-start(bf16[1,1792,128]{2,1,0:T(8,128)(2,1)} %param.12) | copy-start | bytes 1376260
  57.9 9.7 %collective-permute-start.1 = (bf16[2,113,8,128]{3,2,1,0:T(8,128)(2,1)S(1)}, bf16[2,113,8,128]{3,2,1,0:T(8,128)(2,1)S(1)}, u32[]{:S(2)}, u32[]{:S(2)}) collective-permute-start(bf16[2,113,8,128]{3,2,1,0:T(8,128)(2,1)S(1)} %pad_maximum_fusion), channel_id=1, source_target_pairs={{0,896},{16,144},{128,256},{144,16},{256,128},{272,400},{384,512},... | collective-permute-start | bytes 1388552 | tf_op jit(solution)/shard_map/ppermute | solution.py:248
  67.6 10.5 %collective-permute-start.2 = (bf16[2,113,8,128]{3,2,1,0:T(8,128)(2,1)S(1)}, bf16[2,113,8,128]{3,2,1,0:T(8,128)(2,1)S(1)}, u32[]{:S(2)}, u32[]{:S(2)}) collective-permute-start(bf16[2,113,8,128]{3,2,1,0:T(8,128)(2,1)S(1)} %collective-permute-done.1.refs_2_), channel_id=1, source_target_pairs={{0,128},{16,912},{128,0},{144,272},{256,384},{272,144},{384,256},{... | collective-permute-start | bytes 1388552 | tf_op jit(solution)/shard_map/ppermute | solution.py:248
  78.1 9.6 %collective-permute-start.3 = (bf16[2,113,8,128]{3,2,1,0:T(8,128)(2,1)S(1)}, bf16[2,113,8,128]{3,2,1,0:T(8,128)(2,1)S(1)}, u32[]{:S(2)}, u32[]{:S(2)}) collective-permute-start(bf16[2,113,8,128]{3,2,1,0:T(8,128)(2,1)S(1)} %collective-permute-done.2.refs_3_), channel_id=1, source_target_pairs={{0,896},{16,144},{128,256},{144,16},{256,128},{272,400},{384,512},... | collective-permute-start | bytes 1388552 | tf_op jit(solution)/shard_map/ppermute | solution.py:248
  138.1 15.5 %all-to-all-start.2 = ((bf16[16,16,128]{2,1,0:T(8,128)(2,1)}), bf16[16,16,128]{2,1,0:T(8,128)(2,1)S(1)}, u32[]{:S(2)}, u32[]{:S(2)}) async-start(bf16[16,16,128]{2,1,0:T(8,128)(2,1)} %shard_map.97), calls=%async_computation.2 | async-start | bytes 131072 | tf_op jit(solution)/shard_map/all_to_all | solution.py:340

commit v6 on v5

--- a/solution.py
+++ b/solution.py
@@ -12,6 +12,10 @@
 
 
 VMEM_LIMIT = 40 * 1024 * 1024
+BLOCK_PICKS = ((0, None), (1, None), (2, 0), (2, 1), (3, 0), (3, 1), (4, 0), (4, 1))
+BLOCK_OFFSETS = (0, 1, -1, -2, 2, 3, -3, -4)
+BLOCK_ORDER = (0, 1, -1, 2, -2, 3, -3, 4)
+PART_FLOPS = 4 * 10**9
 
 
 def hi_lo(v):
@@ -65,30 +69,26 @@
     return offsets
 
 
-def block_home(place, index, count):
-    offset = block_offsets(count)[index]
-    return lax.rem(place[0] + place[2] * offset + count, count)
-
-
-def split_blocks(refs):
-    blocks = list(refs[:2])
-    for ref in refs[2:]:
-        blocks += [ref.at[0], ref.at[1]]
-    return blocks
-
-
-def lay_rows(place, blocks, rows):
-    count = len(blocks)
+def lay_rows(turn, blocks, offsets, first, rows):
     tiles = rows.shape[1] // LANES
-    for index, block in enumerate(blocks):
+    for block, offset in zip(blocks, offsets):
         per_y = block.shape[0] // tiles
         size = per_y * 8
-        base = pl.multiple_of(block_home(place, index, count) * size, size)
+        base = pl.multiple_of(row_place(turn, offset, first) * size, size)
         for k in range(tiles):
             tile = block[k * per_y : (k + 1) * per_y].astype(jnp.float32)
             rows[pl.ds(base, size), k * LANES : (k + 1) * LANES] = tile.reshape(
                 size, LANES
             ).astype(jnp.bfloat16)
+
+
+def row_place(turn, offset, first):
+    if offset == 0:
+        return 0
+    if offset == -4:
+        return 7 - first
+    ahead = turn if offset > 0 else -turn
+    return 2 * abs(offset) - 1 - first + jnp.where(ahead > 0, 0, 1)
 
 
 def pack_kernel(sub, got, block):
@@ -115,22 +115,21 @@
     block[tiles * per_y] = tags.astype(block.dtype)
 
 
-def part_kernel(place, *refs):
-    *blocks, gate, up, down, part, weight, rows, spread = refs
-    blocks = split_blocks(blocks)
+def part_kernel(picks, offsets, first, place, *refs):
+    *found, gate, up, down, part, weight, rows, spread = refs
+    blocks = [found[i] if j is None else found[i].at[j] for i, j in picks]
     f32 = jnp.float32
-    lay_rows(place, blocks, rows)
+    lay_rows(place[2], blocks, offsets, first, rows)
     mat = rows[...]
-    count = len(blocks)
-    size = rows.shape[0] // count
+    size = rows.shape[0] // len(blocks)
     per_y = size // 8
     shape = (per_y, 8, LANES)
     lane = lax.broadcasted_iota(jnp.int32, shape, 2)
     want = place[1] + lax.broadcasted_iota(jnp.int32, shape, 0) * (LANES // per_y)
-    for index, block in enumerate(blocks):
+    for block, offset in zip(blocks, offsets):
         tags = jnp.broadcast_to(block[block.shape[0] - 1].astype(f32)[None], shape)
         tags = jnp.sum(jnp.where(lane == want, tags, 0.0), axis=2, keepdims=True)
-        base = pl.multiple_of(block_home(place, index, count) * size, size)
+        base = pl.multiple_of(row_place(place[2], offset, first) * size, size)
         spread[pl.ds(base, size), :] = jnp.broadcast_to(tags, shape).reshape(size, LANES)
     weight[...] = first_fours(spread[...])
     for index, mats in enumerate((gate, up)):
@@ -140,18 +139,25 @@
     part[:, 2 * LANES :] = last_fours(out).astype(part.dtype)
 
 
-def grad_kernel(quad, weight, gate, up, back, wide):
+def grad_kernel(place, *refs):
+    *pieces, gate, up, back, wide = refs
     f32, bf16 = jnp.float32, jnp.bfloat16
-    sums = quad[0].astype(f32)
-    for index in range(1, OWNERS):
-        sums = sums + quad[index].astype(f32)
+    quads, weights = pieces[: len(pieces) // 2], pieces[len(pieces) // 2 :]
+    sums = []
+    for quad in quads:
+        total = quad[0].astype(f32)
+        for index in range(1, OWNERS):
+            total = total + quad[index].astype(f32)
+        sums.append(total)
+    sums = jnp.concatenate(sums, axis=0)
+    weight = jnp.concatenate([w[...] for w in weights], axis=0)
     gate_pre = sums[:, :LANES]
     up_pre = sums[:, LANES : 2 * LANES]
     hidden_grad = sums[:, 2 * LANES :]
     sig = jax.nn.sigmoid(gate_pre)
     hidden = (gate_pre * sig * up_pre).astype(bf16).astype(f32)
     route = jnp.sum(hidden * hidden_grad, axis=1, keepdims=True)
-    scaled = weight[...] * hidden_grad
+    scaled = weight * hidden_grad
     gate_grad = (scaled * up_pre * sig * (1.0 + gate_pre * (1.0 - sig))).astype(bf16)
     up_grad = (scaled * gate_pre * sig).astype(bf16)
     route_hi, route_lo = hi_lo(route)
@@ -159,17 +165,28 @@
     groups, tiles, toks, _ = back.shape
     lane = lax.broadcasted_iota(jnp.int32, (slots, LANES), 1)
     tags = jnp.where(lane == 0, route_hi, jnp.where(lane == 1, route_lo, 0.0))
-    back[:, tiles - 1] = tags.reshape(groups, toks, LANES).astype(bf16)
+    count = len(BLOCK_ORDER)
+    per_y = groups // count
+    homes = [
+        pl.multiple_of(lax.rem(place[0] + slot + count, count) * per_y, per_y)
+        for slot in BLOCK_ORDER
+    ]
+
+    def put(k, tile):
+        tile = tile.reshape(groups, toks, LANES).astype(bf16)
+        for index, home in enumerate(homes):
+            back[pl.ds(home, per_y), k] = tile[index * per_y : (index + 1) * per_y]
+
+    put(tiles - 1, tags)
     across = (((1,), (1,)), ((), ()))
     for k in range(0, tiles - 1, 2):
         cols = slice(k * LANES, (k + 2) * LANES)
         out = lax.dot_general(gate_grad, gate[cols], across, preferred_element_type=f32)
         out = out + lax.dot_general(up_grad, up[cols], across, preferred_element_type=f32)
         for j in range(2):
-            tile = out[:, j * LANES : (j + 1) * LANES]
-            back[:, k + j] = tile.reshape(groups, toks, LANES).astype(bf16)
+            put(k + j, out[:, j * LANES : (j + 1) * LANES])
     pairs = slots // 8
-    weighted = (weight[...] * hidden).reshape(pairs, 8, LANES)
+    weighted = (weight * hidden).reshape(pairs, 8, LANES)
     mask = upper(weighted.shape)
     even = jnp.where(mask, swap(weighted), 0.0)
     odd = jnp.where(mask, weighted, 0.0)
@@ -177,9 +194,9 @@
 
 
 def down_kernel(place, *refs):
-    *blocks, wide, out, rows = refs
-    blocks = split_blocks(blocks)
-    lay_rows(place, blocks, rows)
+    *found, wide, out, rows = refs
+    blocks = [found[i] if j is None else found[i].at[j] for i, j in BLOCK_PICKS]
+    lay_rows(place[2], blocks, BLOCK_OFFSETS, 0, rows)
     out[...] = lax.dot_general(
         wide[...], rows[...], (((0,), (0,)), ((), ())), preferred_element_type=jnp.float32
     ).astype(out.dtype)
@@ -248,16 +265,6 @@
     return lax.ppermute(block, ("y", "c"), hops)
 
 
-def y_gather(block):
-    first = swap_with(block, True)
-    pair = swap_with(jnp.stack([block, first]), False)
-    found = [block, first, pair]
-    for step in range(2, lax.axis_size("y") // 2):
-        pair = swap_with(pair, step % 2 == 0)
-        found.append(pair)
-    return found
-
-
 def body(tokens, out_grad, route_weights, expert_ids, w_gate, w_up, w_down):
     f32, bf16 = jnp.float32, jnp.bfloat16
     ny, nxh, nz = lax.axis_size("y"), lax.axis_size("xh"), lax.axis_size("z")
@@ -289,24 +296,40 @@
         groups * tall * LANES,
         1 << 19,
     )(got.reshape(per_y, nz, tall, LANES))
-    blocks = y_gather(block)
-
     smem = pl.BlockSpec(memory_space=pltpu.SMEM)
     slots = groups * toks
-    rows = pltpu.VMEM((groups * tall, nz * sub), bf16)
-    part, weight = call(
-        part_kernel,
-        (
-            jax.ShapeDtypeStruct((slots, 3 * LANES), bf16),
-            jax.ShapeDtypeStruct((slots, LANES), f32),
-        ),
-        [smem] + whole(len(blocks) + 3),
-        [rows, pltpu.VMEM((groups * tall, LANES), f32)],
-        2 * groups * tall * nz * LANES * 3 * LANES,
-        4 << 20,
-    )(place, *blocks, w_gate[0], w_up[0], w_down[0])
-
-    quad = lax.all_gather(part, ("xl", "c"), axis=0, tiled=False)
+    size = per_y * tall
+    width = nz * sub
+
+    def partial_sums(found, low, high, first):
+        picks = BLOCK_PICKS[low:high] if first != 3 else (BLOCK_PICKS[3], BLOCK_PICKS[4])
+        used = sorted({i for i, _ in picks})
+        local = tuple((used.index(i), j) for i, j in picks)
+        n = len(picks)
+        part, weight = call(
+            functools.partial(part_kernel, local, BLOCK_OFFSETS[low:high], first),
+            (
+                jax.ShapeDtypeStruct((n * per_y * toks, 3 * LANES), bf16),
+                jax.ShapeDtypeStruct((n * per_y * toks, LANES), f32),
+            ),
+            [smem] + whole(len(used) + 3),
+            [pltpu.VMEM((n * size, width), bf16), pltpu.VMEM((n * size, LANES), f32)],
+            PART_FLOPS,
+            4 << 20,
+        )(place, *[found[i] for i in used], w_gate[0], w_up[0], w_down[0])
+        return lax.all_gather(part, ("xl", "c"), axis=0, tiled=False), weight
+
+    first = swap_with(block, True)
+    second = swap_with(jnp.stack([block, first]), False)
+    third = swap_with(second, True)
+    quad_a, weight_a = partial_sums([block, first, second], 0, 3, 0)
+    third, quad_a = lax.optimization_barrier((third, quad_a))
+    fourth = swap_with(third, False)
+    found = [block, first, second, third, fourth]
+    quad_b, weight_b = partial_sums(found, 3, 5, 3)
+    fourth, quad_b = lax.optimization_barrier((fourth, quad_b))
+    found[4] = fourth
+    quad_c, weight_c = partial_sums(found, 5, 8, 5)
 
     back, wide = call(
         grad_kernel,
@@ -314,21 +337,21 @@
             jax.ShapeDtypeStruct((groups, tiles + 1, toks, LANES), bf16),
             jax.ShapeDtypeStruct((groups * tall, LANES), bf16),
         ),
-        whole(4),
+        [smem] + whole(8),
         [],
         2 * slots * 2 * LANES * nz * LANES,
         3 << 20,
-    )(quad, weight, w_gate[0], w_up[0])
+    )(place, quad_a, quad_b, quad_c, weight_a, weight_b, weight_c, w_gate[0], w_up[0])
     landed = lax.all_to_all(back, ("y", "xh", "xl", "c"), 0, 0, tiled=True)
 
     down_grad = call(
         down_kernel,
         jax.ShapeDtypeStruct((LANES, nz * sub), bf16),
-        [smem] + whole(len(blocks) + 1),
-        [rows],
+        [smem] + whole(len(found) + 1),
+        [pltpu.VMEM((groups * tall, width), bf16)],
         2 * groups * tall * nz * LANES * LANES,
         4 << 20,
-    )(place, *blocks, wide)
+    )(place, *found, wide)
     pieces = call(
         functools.partial(sum_kernel, sub),
         jax.ShapeDtypeStruct((nz, OWNERS * toks, LANES), bf16),

time: 156 us -> 153 us (0.981)
  waiting for transfers between devices: 34 us -> 20.3 us
  blocking collectives: 93.2 us -> 101 us
  Pallas kernels: 7.24 us -> 9.55 us
    ppermute x4, waiting for transfers between devices: 24.5 us -> 11 us  [swap_with(): return lax.ppermute(block, ('y', 'c'), hops)]
    all_gather x1 -> x3, blocking collectives: 11 us -> 19.7 us  [partial_sums(): return (lax.all_gather(part, ('xl', 'c'), axis=0, tiled=False), weight)]
    pallas_call x1 -> x3, Pallas kernels: 2.43 us -> 3.88 us  [partial_sums(): call(functools.partial(part_kernel, local, BLOCK_OFFSETS[low:high], first...]
  transfers between devices with their start and end apart: 5 -> 5, of which waited for: 5 -> 3; matrix products, arithmetic and copies ran while one was open for 0% -> 0% of each run, Pallas kernels for 1% -> 3%
where the time goes in v6:
time: 153 us; the launch traced here: 151 us
  blocking collectives  101 us (66%)
  waiting for transfers between devices  20.3 us (13%)
  starting transfers between devices  18.5 us (12%)
  Pallas kernels  9.55 us (6%)
    all_to_all x1, blocking collectives, body(): got = lax.all_to_all(send, ('xh', 'xl', 'c', 'z'), 0, 0, tiled=True)  47 us
    all_to_all x1, blocking collectives, body(): landed = lax.all_to_all(back, ('y', 'xh', 'xl', 'c'), 0, 0, tiled=True)  34.1 us
    all_gather x3, blocking collectives, partial_sums(): return (lax.all_gather(part, ('xl', 'c'), axis=0, tiled=False), weight)  19.7 us
    ppermute x4, starting transfers between devices, swap_with(): return lax.ppermute(block, ('y', 'c'), hops)  14.4 us
    ppermute x4, waiting for transfers between devices, swap_with(): return lax.ppermute(block, ('y', 'c'), hops)  11 us
    all_to_all x1, waiting for transfers between devices, body(): final = lax.all_to_all(pieces, 'z', 0, 0, tiled=True)  9.3 us
    all_to_all x1, starting transfers between devices, body(): final = lax.all_to_all(pieces, 'z', 0, 0, tiled=True)  4.09 us
    pallas_call x3, Pallas kernels, partial_sums(): call(functools.partial(part_kernel, local, BLOCK_OFFSETS[low:high], first...  3.88 us
  transfers between devices with their start and end apart: 5, of which 3 were waited for; matrix products, arithmetic and copies ran while one was open for 0% of the time, Pallas kernels for 3%

profile of v6, /device:TPU:1, one launch (start us, length us, event | category | flops | bytes accessed | tf_op | source)
XLA Modules:
  0.0 151.5 jit_solution(13581712762068416936)
XLA Ops:
  0.6 0.0 copy-start.2
  0.6 0.7 convert_element_type.12
  1.3 0.0 copy-done.2
  1.3 0.0 copy-start.5
  1.3 0.1 select_reduce_fusion
  1.4 0.0 copy-start.4
  1.4 0.1 pad.8.clone
  1.5 0.5 copy-done.5
  2.0 0.1 copy-done.4
  2.2 47.0 %all_to_all.15 = bf16[128,8,128]{2,1,0:T(8,128)(2,1)S(1)} all-to-all(bf16[128,8,128]{2,1,0:T(8,128)(2,1)S(1)} %bitcast.35), channel_id=1, replica_groups=mesh['y'=8,'xh'=2,'xl'=2,'c'=2,'z'=16] {'xh','xl','c','z'}, dimensions={0} | all-to-all | bytes 524288 | tf_op jit(solution)/shard_map/all_to_all | solution.py:289
  49.2 0.0 copy-start.3
  49.2 0.2 shard_map.94.refs_0_
  49.4 5.1 %collective-permute-start = (bf16[113,8,128]{2,1,0:T(8,128)(2,1)S(1)}, bf16[113,8,128]{2,1,0:T(8,128)(2,1)S(1)}, u32[]{:S(2)}, u32[]{:S(2)}) collective-permute-start(bf16[113,8,128]{2,1,0:T(8,128)(2,1)S(1)} %shard_map.94.refs_0_), channel_id=1, source_target_pairs={{0,128},{16,912},{128,0},{144,272},{256,384},{272,144},{384,256},{... | collective-permute-start | bytes 694280 | tf_op jit(solution)/shard_map/ppermute | solution.py:265
  54.5 3.4 %collective-permute-done.refs_1_ = bf16[113,8,128]{2,1,0:T(8,128)(2,1)S(1)} collective-permute-done((bf16[113,8,128]{2,1,0:T(8,128)(2,1)S(1)}, bf16[113,8,128]{2,1,0:T(8,128)(2,1)S(1)}, u32[]{:S(2)}, u32[]{:S(2)}) %collective-permute-start) | collective-permute-done | bytes 231456 | tf_op jit(solution)/shard_map/ppermute | solution.py:265
  57.9 0.0 copy-start
  57.9 0.0 copy-start.1
  57.9 2.1 %collective-permute-start.1 = (bf16[2,113,8,128]{3,2,1,0:T(8,128)(2,1)S(1)}, bf16[2,113,8,128]{3,2,1,0:T(8,128)(2,1)S(1)}, u32[]{:S(2)}, u32[]{:S(2)}) collective-permute-start(bf16[2,113,8,128]{3,2,1,0:T(8,128)(2,1)S(1)} %pad_maximum_fusion), channel_id=1, source_target_pairs={{0,896},{16,144},{128,256},{144,16},{256,128},{272,400},{384,512},... | collective-permute-start | bytes 1388552 | tf_op jit(solution)/shard_map/ppermute | solution.py:265
  60.0 0.1 pad_add_fusion.place
  60.1 7.5 %collective-permute-done.1.refs_2_.refs_0_ = bf16[2,113,8,128]{3,2,1,0:T(8,128)(2,1)S(1)} collective-permute-done((bf16[2,113,8,128]{3,2,1,0:T(8,128)(2,1)S(1)}, bf16[2,113,8,128]{3,2,1,0:T(8,128)(2,1)S(1)}, u32[]{:S(2)}, u32[]{:S(2)}) %collective-permute-start.1) | collective-permute-done | bytes 462880 | tf_op jit(solution)/shard_map/ppermute | solution.py:265
  67.6 4.6 %collective-permute-start.2 = (bf16[2,113,8,128]{3,2,1,0:T(8,128)(2,1)S(1)}, bf16[2,113,8,128]{3,2,1,0:T(8,128)(2,1)S(1)}, u32[]{:S(2)}, u32[]{:S(2)}) collective-permute-start(bf16[2,113,8,128]{3,2,1,0:T(8,128)(2,1)S(1)} %collective-permute-done.1.refs_2_.refs_0_), channel_id=1, source_target_pairs={{0,128},{16,912},{128,0},{144,272},{256,384},{272,144},{384,256},{... | collective-permute-start | bytes 1388552 | tf_op jit(solution)/shard_map/ppermute | solution.py:265
  72.2 0.0 copy-done.3
  72.2 0.0 copy-done
  72.2 0.0 copy-done.1
  72.2 1.4 shard_map.95
  73.6 5.3 %all-gather = bf16[384,384]{1,0:T(8,128)(2,1)S(1)} all-gather(bf16[96,384]{1,0:T(8,128)(2,1)S(1)} %get-tuple-element.17), channel_id=2, replica_groups=mesh['y'=8,'xh'=2,'xl'=2,'c'=2,'z'=16] {'xl','c'}, dimensions={0}, use_global_device_ids=true | all-gather | bytes 368640 | tf_op jit(solution)/shard_map/all_gather | solution.py:320
  78.9 0.0 collective-permute-done.2.refs_1_.refs_0_.refs_3_
  78.9 2.7 %collective-permute-start.3 = (bf16[2,113,8,128]{3,2,1,0:T(8,128)(2,1)S(1)}, bf16[2,113,8,128]{3,2,1,0:T(8,128)(2,1)S(1)}, u32[]{:S(2)}, u32[]{:S(2)}) collective-permute-start(bf16[2,113,8,128]{3,2,1,0:T(8,128)(2,1)S(1)} %collective-permute-done.2.refs_1_.refs_0_.refs_3_), channel_id=1, source_target_pairs={{0,896},{16,144},{128,256},{144,16},{256,128},{272,400},{384,512},... | collective-permute-start | bytes 1388552 | tf_op jit(solution)/shard_map/ppermute | solution.py:265
  81.6 1.2 shard_map.96
  82.8 8.3 %all-gather.1 = bf16[256,384]{1,0:T(8,128)(2,1)S(1)} all-gather(bf16[64,384]{1,0:T(8,128)(2,1)S(1)} %get-tuple-element.20), channel_id=3, replica_groups=mesh['y'=8,'xh'=2,'xl'=2,'c'=2,'z'=16] {'xl','c'}, dimensions={0}, use_global_device_ids=true | all-gather | bytes 245760 | tf_op jit(solution)/shard_map/all_gather | solution.py:320
  91.1 0.0 collective-permute-done.3.refs_1_.refs_4_
  91.1 1.3 shard_map.97
  92.4 6.0 %all-gather.2 = bf16[384,384]{1,0:T(8,128)(2,1)S(1)} all-gather(bf16[96,384]{1,0:T(8,128)(2,1)S(1)} %get-tuple-element.23), channel_id=4, replica_groups=mesh['y'=8,'xh'=2,'xl'=2,'c'=2,'z'=16] {'xl','c'}, dimensions={0}, use_global_device_ids=true | all-gather | bytes 368640 | tf_op jit(solution)/shard_map/all_gather | solution.py:320
  98.5 1.4 shard_map.98
  99.9 34.1 %all_to_all.16 = bf16[64,15,4,128]{3,2,1,0:T(4,128)(2,1)S(1)} all-to-all(bf16[64,15,4,128]{3,2,1,0:T(4,128)(2,1)S(1)} %get-tuple-element.27), channel_id=1, replica_groups=mesh['y'=8,'xh'=2,'xl'=2,'c'=2,'z'=16] {'y','xh','xl','c'}, dimensions={0} | all-to-all | bytes 1966080 | tf_op jit(solution)/shard_map/all_to_all | solution.py:345
  134.0 1.1 shard_map.99
  135.0 4.1 %all-to-all-start.2 = ((bf16[16,16,128]{2,1,0:T(8,128)(2,1)}), bf16[16,16,128]{2,1,0:T(8,128)(2,1)S(1)}, u32[]{:S(2)}, u32[]{:S(2)}) async-start(bf16[16,16,128]{2,1,0:T(8,128)(2,1)} %shard_map.99), calls=%async_computation.2 | async-start | bytes 131072 | tf_op jit(solution)/shard_map/all_to_all | solution.py:363
  139.1 2.3 %shard_map.101 = bf16[128,1792]{1,0:T(8,128)(2,1)} custom-call(s32[3]{0:T(128)S(1)} %pad_add_fusion.place, bf16[113,8,128]{2,1,0:T(8,128)(2,1)S(1)} %shard_map.94.refs_0_, bf16[113,8,128]{2,1,0:T(8,128)(2,1)S(1)} %collective-permute-done.refs_1_, bf16[2,113,8,128]{3,2,1,0:T(8,128)(2,1)S(1)} %collective-permute-done.1.refs_2_.refs_0_, ...), custom_call_target="tpu_custom_call" | custom-call | flops 268435456 | bytes 4194304 | tf_op jit(solution)/shard_map/pallas_call | solution.py:347
  141.4 9.3 %all-to-all-done.2.final = bf16[16,16,128]{2,1,0:T(8,128)(2,1)S(1)} async-done(((bf16[16,16,128]{2,1,0:T(8,128)(2,1)}), bf16[16,16,128]{2,1,0:T(8,128)(2,1)S(1)}, u32[]{:S(2)}, u32[]{:S(2)}) %all-to-all-start.2) | async-done | bytes 65568 | tf_op jit(solution)/shard_map/all_to_all | solution.py:363
  150.7 0.7 shard_map.100
  (4 shorter events, 0.1 us)
Async XLA Ops:
  0.6 0.7 copy-start.2
  1.3 0.7 copy-start.5
  1.4 0.7 copy-start.4
  49.2 23.0 %copy-start.3 = (bf16[1,128,1792]{2,1,0:T(8,128)(2,1)S(1)}, bf16[1,128,1792]{2,1,0:T(8,128)(2,1)}, u32[]{:S(2)}) copy-start(bf16[1,128,1792]{2,1,0:T(8,128)(2,1)} %param.13) | copy-start | bytes 1376260
  49.4 8.5 %collective-permute-start = (bf16[113,8,128]{2,1,0:T(8,128)(2,1)S(1)}, bf16[113,8,128]{2,1,0:T(8,128)(2,1)S(1)}, u32[]{:S(2)}, u32[]{:S(2)}) collective-permute-start(bf16[113,8,128]{2,1,0:T(8,128)(2,1)S(1)} %shard_map.94.refs_0_), channel_id=1, source_target_pairs={{0,128},{16,912},{128,0},{144,272},{256,384},{272,144},{384,256},{... | collective-permute-start | bytes 694280 | tf_op jit(solution)/shard_map/ppermute | solution.py:265
  57.9 14.3 %copy-start = (bf16[1,1792,128]{2,1,0:T(8,128)(2,1)S(1)}, bf16[1,1792,128]{2,1,0:T(8,128)(2,1)}, u32[]{:S(2)}) copy-start(bf16[1,1792,128]{2,1,0:T(8,128)(2,1)} %param.11) | copy-start | bytes 1376260
  57.9 14.3 %copy-start.1 = (bf16[1,1792,128]{2,1,0:T(8,128)(2,1)S(1)}, bf16[1,1792,128]{2,1,0:T(8,128)(2,1)}, u32[]{:S(2)}) copy-start(bf16[1,1792,128]{2,1,0:T(8,128)(2,1)} %param.12) | copy-start | bytes 1376260
  57.9 9.7 %collective-permute-start.1 = (bf16[2,113,8,128]{3,2,1,0:T(8,128)(2,1)S(1)}, bf16[2,113,8,128]{3,2,1,0:T(8,128)(2,1)S(1)}, u32[]{:S(2)}, u32[]{:S(2)}) collective-permute-start(bf16[2,113,8,128]{3,2,1,0:T(8,128)(2,1)S(1)} %pad_maximum_fusion), channel_id=1, source_target_pairs={{0,896},{16,144},{128,256},{144,16},{256,128},{272,400},{384,512},... | collective-permute-start | bytes 1388552 | tf_op jit(solution)/shard_map/ppermute | solution.py:265
  67.6 11.3 %collective-permute-start.2 = (bf16[2,113,8,128]{3,2,1,0:T(8,128)(2,1)S(1)}, bf16[2,113,8,128]{3,2,1,0:T(8,128)(2,1)S(1)}, u32[]{:S(2)}, u32[]{:S(2)}) collective-permute-start(bf16[2,113,8,128]{3,2,1,0:T(8,128)(2,1)S(1)} %collective-permute-done.1.refs_2_.refs_0_), channel_id=1, source_target_pairs={{0,128},{16,912},{128,0},{144,272},{256,384},{272,144},{384,256},{... | collective-permute-start | bytes 1388552 | tf_op jit(solution)/shard_map/ppermute | solution.py:265
  78.9 12.2 %collective-permute-start.3 = (bf16[2,113,8,128]{3,2,1,0:T(8,128)(2,1)S(1)}, bf16[2,113,8,128]{3,2,1,0:T(8,128)(2,1)S(1)}, u32[]{:S(2)}, u32[]{:S(2)}) collective-permute-start(bf16[2,113,8,128]{3,2,1,0:T(8,128)(2,1)S(1)} %collective-permute-done.2.refs_1_.refs_0_.refs_3_), channel_id=1, source_target_pairs={{0,896},{16,144},{128,256},{144,16},{256,128},{272,400},{384,512},... | collective-permute-start | bytes 1388552 | tf_op jit(solution)/shard_map/ppermute | solution.py:265
  135.0 15.7 %all-to-all-start.2 = ((bf16[16,16,128]{2,1,0:T(8,128)(2,1)}), bf16[16,16,128]{2,1,0:T(8,128)(2,1)S(1)}, u32[]{:S(2)}, u32[]{:S(2)}) async-start(bf16[16,16,128]{2,1,0:T(8,128)(2,1)} %shard_map.99), calls=%async_computation.2 | async-start | bytes 131072 | tf_op jit(solution)/shard_map/all_to_all | solution.py:363

commit v7 on v6

--- a/solution.py
+++ b/solution.py
@@ -12,7 +12,7 @@
 
 
 VMEM_LIMIT = 40 * 1024 * 1024
-BLOCK_PICKS = ((0, None), (1, None), (2, 0), (2, 1), (3, 0), (3, 1), (4, 0), (4, 1))
+BLOCK_PICKS = ((0, None), (1, None), (2, None), (3, None), (4, 0), (4, 1), (5, 0), (5, 1))
 BLOCK_OFFSETS = (0, 1, -1, -2, 2, 3, -3, -4)
 BLOCK_ORDER = (0, 1, -1, 2, -2, 3, -3, 4)
 PART_FLOPS = 4 * 10**9
@@ -302,7 +302,7 @@
     width = nz * sub
 
     def partial_sums(found, low, high, first):
-        picks = BLOCK_PICKS[low:high] if first != 3 else (BLOCK_PICKS[3], BLOCK_PICKS[4])
+        picks = BLOCK_PICKS[low:high]
         used = sorted({i for i, _ in picks})
         local = tuple((used.index(i), j) for i, j in picks)
         n = len(picks)
@@ -320,15 +320,17 @@
         return lax.all_gather(part, ("xl", "c"), axis=0, tiled=False), weight
 
     first = swap_with(block, True)
-    second = swap_with(jnp.stack([block, first]), False)
-    third = swap_with(second, True)
-    quad_a, weight_a = partial_sums([block, first, second], 0, 3, 0)
+    other = swap_with(block, False)
+    beyond = swap_with(first, False)
+    third = swap_with(jnp.stack([other, beyond]), True)
+    found = [block, first, other, beyond, third]
+    quad_a, weight_a = partial_sums(found, 0, 3, 0)
     third, quad_a = lax.optimization_barrier((third, quad_a))
+    found[4] = third
     fourth = swap_with(third, False)
-    found = [block, first, second, third, fourth]
     quad_b, weight_b = partial_sums(found, 3, 5, 3)
     fourth, quad_b = lax.optimization_barrier((fourth, quad_b))
-    found[4] = fourth
+    found.append(fourth)
     quad_c, weight_c = partial_sums(found, 5, 8, 5)
 
     back, wide = call(

time: 153 us -> 153 us (level)
  waiting for transfers between devices: 20.3 us -> 15.9 us
  starting transfers between devices: 18.5 us -> 22 us
    ppermute x4 -> x5, waiting for transfers between devices: 11 us -> 6.56 us  [swap_with(): return lax.ppermute(block, ('y', 'c'), hops)]
    ppermute x4 -> x5, starting transfers between devices: 14.4 us -> 16.7 us  [swap_with(): return lax.ppermute(block, ('y', 'c'), hops)]
  transfers between devices with their start and end apart: 5 -> 6, of which waited for: 3 -> 4; matrix products, arithmetic and copies ran while one was open for 0% -> 0% of each run, Pallas kernels for 3% -> 3%
where the time goes in v7:
time: 153 us; the launch traced here: 151 us
  blocking collectives  101 us (66%)
  starting transfers between devices  22 us (14%)
  waiting for transfers between devices  15.9 us (10%)
  Pallas kernels  9.53 us (6%)
    all_to_all x1, blocking collectives, body(): got = lax.all_to_all(send, ('xh', 'xl', 'c', 'z'), 0, 0, tiled=True)  47 us
    all_to_all x1, blocking collectives, body(): landed = lax.all_to_all(back, ('y', 'xh', 'xl', 'c'), 0, 0, tiled=True)  34.8 us
    all_gather x3, blocking collectives, partial_sums(): return (lax.all_gather(part, ('xl', 'c'), axis=0, tiled=False), weight)  19.3 us
    ppermute x5, starting transfers between devices, swap_with(): return lax.ppermute(block, ('y', 'c'), hops)  16.7 us
    all_to_all x1, waiting for transfers between devices, body(): final = lax.all_to_all(pieces, 'z', 0, 0, tiled=True)  9.3 us
    ppermute x5, waiting for transfers between devices, swap_with(): return lax.ppermute(block, ('y', 'c'), hops)  6.56 us
    all_to_all x1, starting transfers between devices, body(): final = lax.all_to_all(pieces, 'z', 0, 0, tiled=True)  5.24 us
    pallas_call x3, Pallas kernels, partial_sums(): call(functools.partial(part_kernel, local, BLOCK_OFFSETS[low:high], first...  3.86 us
  transfers between devices with their start and end apart: 6, of which 4 were waited for; matrix products, arithmetic and copies ran while one was open for 0% of the time, Pallas kernels for 3%

profile of v7, /device:TPU:1, one launch (start us, length us, event | category | flops | bytes accessed | tf_op | source)
XLA Modules:
  0.0 150.8 jit_solution(12509350902772243045)
XLA Ops:
  0.6 0.0 copy-start.2
  0.6 0.7 convert_element_type.12
  1.3 0.0 copy-done.2
  1.3 0.0 copy-start.5
  1.3 0.1 select_reduce_fusion
  1.4 0.0 copy-start.4
  1.4 0.1 pad.8.clone
  1.5 0.5 copy-done.5
  2.0 0.1 copy-done.4
  2.2 47.0 %all_to_all.15 = bf16[128,8,128]{2,1,0:T(8,128)(2,1)S(1)} all-to-all(bf16[128,8,128]{2,1,0:T(8,128)(2,1)S(1)} %bitcast.35), channel_id=1, replica_groups=mesh['y'=8,'xh'=2,'xl'=2,'c'=2,'z'=16] {'xh','xl','c','z'}, dimensions={0} | all-to-all | bytes 524288 | tf_op jit(solution)/shard_map/all_to_all | solution.py:289
  49.2 0.0 copy-start.3
  49.2 0.2 shard_map.94.refs_0_
  49.4 5.1 %collective-permute-start.1 = (bf16[113,8,128]{2,1,0:T(8,128)(2,1)S(1)}, bf16[113,8,128]{2,1,0:T(8,128)(2,1)S(1)}, u32[]{:S(2)}, u32[]{:S(2)}) collective-permute-start(bf16[113,8,128]{2,1,0:T(8,128)(2,1)S(1)} %shard_map.94.refs_0_), channel_id=1, source_target_pairs={{0,128},{16,912},{128,0},{144,272},{256,384},{272,144},{384,256},{... | collective-permute-start | bytes 694280 | tf_op jit(solution)/shard_map/ppermute | solution.py:265
  54.5 1.9 %collective-permute-start = (bf16[113,8,128]{2,1,0:T(8,128)(2,1)S(1)}, bf16[113,8,128]{2,1,0:T(8,128)(2,1)S(1)}, u32[]{:S(2)}, u32[]{:S(2)}) collective-permute-start(bf16[113,8,128]{2,1,0:T(8,128)(2,1)S(1)} %shard_map.94.refs_0_), channel_id=1, source_target_pairs={{0,896},{16,144},{128,256},{144,16},{256,128},{272,400},{384,512},... | collective-permute-start | bytes 694280 | tf_op jit(solution)/shard_map/ppermute | solution.py:265
  56.4 1.5 collective-permute-done.1.refs_1_
  57.9 1.9 %collective-permute-start.2 = (bf16[113,8,128]{2,1,0:T(8,128)(2,1)S(1)}, bf16[113,8,128]{2,1,0:T(8,128)(2,1)S(1)}, u32[]{:S(2)}, u32[]{:S(2)}) collective-permute-start(bf16[113,8,128]{2,1,0:T(8,128)(2,1)S(1)} %collective-permute-done.1.refs_1_), channel_id=1, source_target_pairs={{0,896},{16,144},{128,256},{144,16},{256,128},{272,400},{384,512},... | collective-permute-start | bytes 694280 | tf_op jit(solution)/shard_map/ppermute | solution.py:265
  59.8 0.1 pad_add_fusion.place
  59.9 1.4 collective-permute-done.refs_2_
  61.3 3.7 %collective-permute-done.2.refs_0_.refs_3_ = bf16[113,8,128]{2,1,0:T(8,128)(2,1)S(1)} collective-permute-done((bf16[113,8,128]{2,1,0:T(8,128)(2,1)S(1)}, bf16[113,8,128]{2,1,0:T(8,128)(2,1)S(1)}, u32[]{:S(2)}, u32[]{:S(2)}) %collective-permute-start.2) | collective-permute-done | bytes 231456 | tf_op jit(solution)/shard_map/ppermute | solution.py:265
  65.0 0.0 copy-start
  65.0 0.0 copy-start.1
  65.0 4.7 %collective-permute-start.3 = (bf16[2,113,8,128]{3,2,1,0:T(8,128)(2,1)S(1)}, bf16[2,113,8,128]{3,2,1,0:T(8,128)(2,1)S(1)}, u32[]{:S(2)}, u32[]{:S(2)}) collective-permute-start(bf16[2,113,8,128]{3,2,1,0:T(8,128)(2,1)S(1)} %pad_maximum_fusion), channel_id=1, source_target_pairs={{0,128},{16,912},{128,0},{144,272},{256,384},{272,144},{384,256},{... | collective-permute-start | bytes 1388552 | tf_op jit(solution)/shard_map/ppermute | solution.py:265
  69.7 0.0 copy-done.3
  69.7 0.0 copy-done
  69.7 0.0 copy-done.1
  69.8 1.4 shard_map.95
  71.1 5.4 %all-gather = bf16[384,384]{1,0:T(8,128)(2,1)S(1)} all-gather(bf16[96,384]{1,0:T(8,128)(2,1)S(1)} %get-tuple-element.17), channel_id=2, replica_groups=mesh['y'=8,'xh'=2,'xl'=2,'c'=2,'z'=16] {'xl','c'}, dimensions={0}, use_global_device_ids=true | all-gather | bytes 368640 | tf_op jit(solution)/shard_map/all_gather | solution.py:320
  76.5 0.0 collective-permute-done.3.refs_1_.refs_0_.refs_4_
  76.5 3.1 %collective-permute-start.4 = (bf16[2,113,8,128]{3,2,1,0:T(8,128)(2,1)S(1)}, bf16[2,113,8,128]{3,2,1,0:T(8,128)(2,1)S(1)}, u32[]{:S(2)}, u32[]{:S(2)}) collective-permute-start(bf16[2,113,8,128]{3,2,1,0:T(8,128)(2,1)S(1)} %collective-permute-done.3.refs_1_.refs_0_.refs_4_), channel_id=1, source_target_pairs={{0,896},{16,144},{128,256},{144,16},{256,128},{272,400},{384,512},... | collective-permute-start | bytes 1388552 | tf_op jit(solution)/shard_map/ppermute | solution.py:265
  79.6 1.2 shard_map.96
  80.7 7.8 %all-gather.1 = bf16[256,384]{1,0:T(8,128)(2,1)S(1)} all-gather(bf16[64,384]{1,0:T(8,128)(2,1)S(1)} %get-tuple-element.20), channel_id=3, replica_groups=mesh['y'=8,'xh'=2,'xl'=2,'c'=2,'z'=16] {'xl','c'}, dimensions={0}, use_global_device_ids=true | all-gather | bytes 245760 | tf_op jit(solution)/shard_map/all_gather | solution.py:320
  88.6 0.0 collective-permute-done.4.refs_1_.refs_5_
  88.6 1.3 shard_map.97
  89.9 6.1 %all-gather.2 = bf16[384,384]{1,0:T(8,128)(2,1)S(1)} all-gather(bf16[96,384]{1,0:T(8,128)(2,1)S(1)} %get-tuple-element.23), channel_id=4, replica_groups=mesh['y'=8,'xh'=2,'xl'=2,'c'=2,'z'=16] {'xl','c'}, dimensions={0}, use_global_device_ids=true | all-gather | bytes 368640 | tf_op jit(solution)/shard_map/all_gather | solution.py:320
  96.0 1.4 shard_map.98
  97.4 34.8 %all_to_all.16 = bf16[64,15,4,128]{3,2,1,0:T(4,128)(2,1)S(1)} all-to-all(bf16[64,15,4,128]{3,2,1,0:T(4,128)(2,1)S(1)} %get-tuple-element.27), channel_id=1, replica_groups=mesh['y'=8,'xh'=2,'xl'=2,'c'=2,'z'=16] {'y','xh','xl','c'}, dimensions={0} | all-to-all | bytes 1966080 | tf_op jit(solution)/shard_map/all_to_all | solution.py:347
  132.2 1.1 shard_map.99
  133.3 5.2 %all-to-all-start.2 = ((bf16[16,16,128]{2,1,0:T(8,128)(2,1)}), bf16[16,16,128]{2,1,0:T(8,128)(2,1)S(1)}, u32[]{:S(2)}, u32[]{:S(2)}) async-start(bf16[16,16,128]{2,1,0:T(8,128)(2,1)} %shard_map.99), calls=%async_computation.2 | async-start | bytes 131072 | tf_op jit(solution)/shard_map/all_to_all | solution.py:365
  138.5 2.3 %shard_map.101 = bf16[128,1792]{1,0:T(8,128)(2,1)} custom-call(s32[3]{0:T(128)S(1)} %pad_add_fusion.place, bf16[113,8,128]{2,1,0:T(8,128)(2,1)S(1)} %shard_map.94.refs_0_, bf16[113,8,128]{2,1,0:T(8,128)(2,1)S(1)} %collective-permute-done.1.refs_1_, bf16[113,8,128]{2,1,0:T(8,128)(2,1)S(1)} %collective-permute-done.refs_2_, ...), custom_call_target="tpu_custom_call" | custom-call | flops 268435456 | bytes 4194304 | tf_op jit(solution)/shard_map/pallas_call | solution.py:349
  140.8 9.3 %all-to-all-done.2.final = bf16[16,16,128]{2,1,0:T(8,128)(2,1)S(1)} async-done(((bf16[16,16,128]{2,1,0:T(8,128)(2,1)}), bf16[16,16,128]{2,1,0:T(8,128)(2,1)S(1)}, u32[]{:S(2)}, u32[]{:S(2)}) %all-to-all-start.2) | async-done | bytes 65568 | tf_op jit(solution)/shard_map/all_to_all | solution.py:365
  150.1 0.7 shard_map.100
  (4 shorter events, 0.1 us)
Async XLA Ops:
  0.6 0.7 copy-start.2
  1.3 0.7 copy-start.5
  1.4 0.7 copy-start.4
  49.2 20.6 %copy-start.3 = (bf16[1,128,1792]{2,1,0:T(8,128)(2,1)S(1)}, bf16[1,128,1792]{2,1,0:T(8,128)(2,1)}, u32[]{:S(2)}) copy-start(bf16[1,128,1792]{2,1,0:T(8,128)(2,1)} %param.13) | copy-start | bytes 1376260
  49.4 8.5 %collective-permute-start.1 = (bf16[113,8,128]{2,1,0:T(8,128)(2,1)S(1)}, bf16[113,8,128]{2,1,0:T(8,128)(2,1)S(1)}, u32[]{:S(2)}, u32[]{:S(2)}) collective-permute-start(bf16[113,8,128]{2,1,0:T(8,128)(2,1)S(1)} %shard_map.94.refs_0_), channel_id=1, source_target_pairs={{0,128},{16,912},{128,0},{144,272},{256,384},{272,144},{384,256},{... | collective-permute-start | bytes 694280 | tf_op jit(solution)/shard_map/ppermute | solution.py:265
  54.5 6.8 %collective-permute-start = (bf16[113,8,128]{2,1,0:T(8,128)(2,1)S(1)}, bf16[113,8,128]{2,1,0:T(8,128)(2,1)S(1)}, u32[]{:S(2)}, u32[]{:S(2)}) collective-permute-start(bf16[113,8,128]{2,1,0:T(8,128)(2,1)S(1)} %shard_map.94.refs_0_), channel_id=1, source_target_pairs={{0,896},{16,144},{128,256},{144,16},{256,128},{272,400},{384,512},... | collective-permute-start | bytes 694280 | tf_op jit(solution)/shard_map/ppermute | solution.py:265
  57.9 7.1 %collective-permute-start.2 = (bf16[113,8,128]{2,1,0:T(8,128)(2,1)S(1)}, bf16[113,8,128]{2,1,0:T(8,128)(2,1)S(1)}, u32[]{:S(2)}, u32[]{:S(2)}) collective-permute-start(bf16[113,8,128]{2,1,0:T(8,128)(2,1)S(1)} %collective-permute-done.1.refs_1_), channel_id=1, source_target_pairs={{0,896},{16,144},{128,256},{144,16},{256,128},{272,400},{384,512},... | collective-permute-start | bytes 694280 | tf_op jit(solution)/shard_map/ppermute | solution.py:265
  65.0 4.8 %copy-start = (bf16[1,1792,128]{2,1,0:T(8,128)(2,1)S(1)}, bf16[1,1792,128]{2,1,0:T(8,128)(2,1)}, u32[]{:S(2)}) copy-start(bf16[1,1792,128]{2,1,0:T(8,128)(2,1)} %param.11) | copy-start | bytes 1376260
  65.0 4.8 %copy-start.1 = (bf16[1,1792,128]{2,1,0:T(8,128)(2,1)S(1)}, bf16[1,1792,128]{2,1,0:T(8,128)(2,1)}, u32[]{:S(2)}) copy-start(bf16[1,1792,128]{2,1,0:T(8,128)(2,1)} %param.12) | copy-start | bytes 1376260
  65.0 11.5 %collective-permute-start.3 = (bf16[2,113,8,128]{3,2,1,0:T(8,128)(2,1)S(1)}, bf16[2,113,8,128]{3,2,1,0:T(8,128)(2,1)S(1)}, u32[]{:S(2)}, u32[]{:S(2)}) collective-permute-start(bf16[2,113,8,128]{3,2,1,0:T(8,128)(2,1)S(1)} %pad_maximum_fusion), channel_id=1, source_target_pairs={{0,128},{16,912},{128,0},{144,272},{256,384},{272,144},{384,256},{... | collective-permute-start | bytes 1388552 | tf_op jit(solution)/shard_map/ppermute | solution.py:265
  76.5 12.1 %collective-permute-start.4 = (bf16[2,113,8,128]{3,2,1,0:T(8,128)(2,1)S(1)}, bf16[2,113,8,128]{3,2,1,0:T(8,128)(2,1)S(1)}, u32[]{:S(2)}, u32[]{:S(2)}) collective-permute-start(bf16[2,113,8,128]{3,2,1,0:T(8,128)(2,1)S(1)} %collective-permute-done.3.refs_1_.refs_0_.refs_4_), channel_id=1, source_target_pairs={{0,896},{16,144},{128,256},{144,16},{256,128},{272,400},{384,512},... | collective-permute-start | bytes 1388552 | tf_op jit(solution)/shard_map/ppermute | solution.py:265
  133.3 16.8 %all-to-all-start.2 = ((bf16[16,16,128]{2,1,0:T(8,128)(2,1)}), bf16[16,16,128]{2,1,0:T(8,128)(2,1)S(1)}, u32[]{:S(2)}, u32[]{:S(2)}) async-start(bf16[16,16,128]{2,1,0:T(8,128)(2,1)} %shard_map.99), calls=%async_computation.2 | async-start | bytes 131072 | tf_op jit(solution)/shard_map/all_to_all | solution.py:365

commit v8 on v7

--- a/solution.py
+++ b/solution.py
@@ -140,7 +140,7 @@
 
 
 def grad_kernel(place, *refs):
-    *pieces, gate, up, back, wide = refs
+    *pieces, gate, up, back, wide, moved = refs
     f32, bf16 = jnp.float32, jnp.bfloat16
     quads, weights = pieces[: len(pieces) // 2], pieces[len(pieces) // 2 :]
     sums = []
@@ -166,18 +166,19 @@
     lane = lax.broadcasted_iota(jnp.int32, (slots, LANES), 1)
     tags = jnp.where(lane == 0, route_hi, jnp.where(lane == 1, route_lo, 0.0))
     count = len(BLOCK_ORDER)
-    per_y = groups // count
-    homes = [
-        pl.multiple_of(lax.rem(place[0] + slot + count, count) * per_y, per_y)
-        for slot in BLOCK_ORDER
-    ]
+    tall = slots // count
+    for index, slot in enumerate(BLOCK_ORDER):
+        home = pl.multiple_of(lax.rem(place[0] + slot + count, count) * tall, tall)
+        own = slice(index * tall, (index + 1) * tall)
+        moved[pl.ds(home, tall), :LANES] = gate_grad[own]
+        moved[pl.ds(home, tall), LANES : 2 * LANES] = up_grad[own]
+        moved[pl.ds(home, tall), 2 * LANES :] = tags[own].astype(bf16)
+    gate_grad, up_grad = moved[:, :LANES], moved[:, LANES : 2 * LANES]
 
     def put(k, tile):
-        tile = tile.reshape(groups, toks, LANES).astype(bf16)
-        for index, home in enumerate(homes):
-            back[pl.ds(home, per_y), k] = tile[index * per_y : (index + 1) * per_y]
-
-    put(tiles - 1, tags)
+        back[:, k] = tile.reshape(groups, toks, LANES).astype(bf16)
+
+    put(tiles - 1, moved[:, 2 * LANES :].astype(f32))
     across = (((1,), (1,)), ((), ()))
     for k in range(0, tiles - 1, 2):
         cols = slice(k * LANES, (k + 2) * LANES)
@@ -248,10 +249,25 @@
     route_grad[...] = out
 
 
-def weight_table(expert_ids, route_weights, experts):
-    onehot = expert_ids[:, :, None] == jnp.arange(experts, dtype=jnp.int32)[None, None, :]
-    weights = jnp.where(onehot, route_weights.astype(jnp.float32)[:, :, None], 0.0)
-    return jnp.sum(weights, axis=1).astype(jnp.bfloat16)
+def send_kernel(tokens, out_grad, weights, ids, send, acc):
+    f32 = jnp.float32
+    toks, owners, sub = tokens.shape
+    x_rows = tokens[...].astype(f32)
+    g_rows = out_grad[...].astype(f32)
+    acc[...] = jnp.zeros_like(acc)
+    for q in range(owners):
+        acc[q, :toks, :sub] = x_rows[:, q, :]
+        acc[q, toks : 2 * toks, :sub] = g_rows[:, q, :]
+    route = weights[...].astype(f32)
+    lane = lax.broadcasted_iota(jnp.int32, (toks, LANES), 1) - sub
+    table = jnp.zeros((toks, LANES), f32)
+    for k in range(ids.shape[1]):
+        table = jnp.where(lane == ids[:, k : k + 1], route[:, k : k + 1], table)
+    acc[owners, :toks, :] = table
+    for q in range(owners):
+        tile = (acc[q] + acc[owners]).astype(send.dtype)
+        for top in range(q, send.shape[0], owners):
+            send[top] = jnp.broadcast_to(tile[None], send.shape[1:])
 
 
 def swap_with(block, toward):
@@ -278,13 +294,14 @@
     turn = 1 - 2 * lax.rem(my_y + lax.axis_index("c"), 2)
     place = jnp.stack([my_y, expert, turn]).astype(jnp.int32)
 
-    table = weight_table(expert_ids, route_weights, experts)
-    x_rows = jnp.concatenate(
-        [tokens.transpose(1, 0, 2), jnp.broadcast_to(table[None], (OWNERS, toks, experts))], axis=2
-    )
-    g_rows = jnp.pad(out_grad.transpose(1, 0, 2), ((0, 0), (0, 0), (0, LANES - sub)))
-    send = jnp.concatenate([x_rows, g_rows], axis=1)
-    send = jnp.broadcast_to(send[None, :, None], (nxh, OWNERS, nz, tall, LANES))
+    send = call(
+        send_kernel,
+        jax.ShapeDtypeStruct((nxh * OWNERS, nz, tall, LANES), bf16),
+        whole(4),
+        [pltpu.VMEM((OWNERS + 1, tall, LANES), f32)],
+        per_y * nz * tall * LANES,
+        1 << 19,
+    )(tokens, out_grad, route_weights, expert_ids)
     send = send.reshape(nxh * OWNERS * nz, tall, LANES)
     got = lax.all_to_all(send, ("xh", "xl", "c", "z"), 0, 0, tiled=True)
     tiles = nz * sub // LANES
@@ -340,7 +357,7 @@
             jax.ShapeDtypeStruct((groups * tall, LANES), bf16),
         ),
         [smem] + whole(8),
-        [],
+        [pltpu.VMEM((slots, 3 * LANES), bf16)],
         2 * slots * 2 * LANES * nz * LANES,
         3 << 20,
     )(place, quad_a, quad_b, quad_c, weight_a, weight_b, weight_c, w_gate[0], w_up[0])

time: 153 us -> 154 us (level)
  local copies, waits for them, and re-layouts: 0.74 us -> 2.75 us
    unnamed x12 -> x16, local copies, waits for them, and re-layouts: 0.63 us -> 2.75 us
where the time goes in v8:
time: 154 us; the launch traced here: 152 us
  blocking collectives  101 us (66%)
  starting transfers between devices  22 us (14%)
  waiting for transfers between devices  15.9 us (10%)
  Pallas kernels  9.7 us (6%)
  local copies, waits for them, and re-layouts  2.75 us (2%)
    all_to_all x1, blocking collectives, body(): got = lax.all_to_all(send, ('xh', 'xl', 'c', 'z'), 0, 0, tiled=True)  47 us
    all_to_all x1, blocking collectives, body(): landed = lax.all_to_all(back, ('y', 'xh', 'xl', 'c'), 0, 0, tiled=True)  34.8 us
    all_gather x3, blocking collectives, partial_sums(): return (lax.all_gather(part, ('xl', 'c'), axis=0, tiled=False), weight)  19.3 us
    ppermute x5, starting transfers between devices, swap_with(): return lax.ppermute(block, ('y', 'c'), hops)  16.7 us
    all_to_all x1, waiting for transfers between devices, body(): final = lax.all_to_all(pieces, 'z', 0, 0, tiled=True)  9.29 us
    ppermute x5, waiting for transfers between devices, swap_with(): return lax.ppermute(block, ('y', 'c'), hops)  6.56 us
    all_to_all x1, starting transfers between devices, body(): final = lax.all_to_all(pieces, 'z', 0, 0, tiled=True)  5.23 us
    pallas_call x3, Pallas kernels, partial_sums(): call(functools.partial(part_kernel, local, BLOCK_OFFSETS[low:high], first...  3.86 us
  transfers between devices with their start and end apart: 6, of which 4 were waited for; matrix products, arithmetic and copies ran while one was open for 0% of the time, Pallas kernels for 3%

profile of v8, /device:TPU:1, one launch (start us, length us, event | category | flops | bytes accessed | tf_op | source)
XLA Modules:
  0.0 152.2 jit_solution(12034659753620919997)
XLA Ops:
  0.6 0.0 copy-start.2
  0.6 0.7 copy-done.2
  1.3 0.0 copy-start.4
  1.3 0.7 copy-done.4
  2.0 0.0 copy-start.5
  2.0 0.7 copy-done.5
  2.7 0.0 copy-start.6
  2.7 0.7 copy-done.6
  3.4 0.1 shard_map.94
  3.5 47.0 %all_to_all.15 = bf16[128,8,128]{2,1,0:T(8,128)(2,1)S(1)} all-to-all(bf16[128,8,128]{2,1,0:T(8,128)(2,1)S(1)} %bitcast.18), channel_id=1, replica_groups=mesh['y'=8,'xh'=2,'xl'=2,'c'=2,'z'=16] {'xh','xl','c','z'}, dimensions={0} | all-to-all | bytes 524288 | tf_op jit(solution)/shard_map/all_to_all | solution.py:306
  50.5 0.0 copy-start.7
  50.5 0.2 shard_map.95.refs_0_
  50.7 5.1 %collective-permute-start.1 = (bf16[113,8,128]{2,1,0:T(8,128)(2,1)S(1)}, bf16[113,8,128]{2,1,0:T(8,128)(2,1)S(1)}, u32[]{:S(2)}, u32[]{:S(2)}) collective-permute-start(bf16[113,8,128]{2,1,0:T(8,128)(2,1)S(1)} %shard_map.95.refs_0_), channel_id=1, source_target_pairs={{0,128},{16,912},{128,0},{144,272},{256,384},{272,144},{384,256},{... | collective-permute-start | bytes 694280 | tf_op jit(solution)/shard_map/ppermute | solution.py:281
  55.8 1.9 %collective-permute-start = (bf16[113,8,128]{2,1,0:T(8,128)(2,1)S(1)}, bf16[113,8,128]{2,1,0:T(8,128)(2,1)S(1)}, u32[]{:S(2)}, u32[]{:S(2)}) collective-permute-start(bf16[113,8,128]{2,1,0:T(8,128)(2,1)S(1)} %shard_map.95.refs_0_), channel_id=1, source_target_pairs={{0,896},{16,144},{128,256},{144,16},{256,128},{272,400},{384,512},... | collective-permute-start | bytes 694280 | tf_op jit(solution)/shard_map/ppermute | solution.py:281
  57.7 1.5 collective-permute-done.1.refs_1_
  59.2 1.9 %collective-permute-start.2 = (bf16[113,8,128]{2,1,0:T(8,128)(2,1)S(1)}, bf16[113,8,128]{2,1,0:T(8,128)(2,1)S(1)}, u32[]{:S(2)}, u32[]{:S(2)}) collective-permute-start(bf16[113,8,128]{2,1,0:T(8,128)(2,1)S(1)} %collective-permute-done.1.refs_1_), channel_id=1, source_target_pairs={{0,896},{16,144},{128,256},{144,16},{256,128},{272,400},{384,512},... | collective-permute-start | bytes 694280 | tf_op jit(solution)/shard_map/ppermute | solution.py:281
  61.1 0.1 pad_add_fusion.place
  61.2 1.4 collective-permute-done.refs_2_
  62.6 3.7 %collective-permute-done.2.refs_0_.refs_3_ = bf16[113,8,128]{2,1,0:T(8,128)(2,1)S(1)} collective-permute-done((bf16[113,8,128]{2,1,0:T(8,128)(2,1)S(1)}, bf16[113,8,128]{2,1,0:T(8,128)(2,1)S(1)}, u32[]{:S(2)}, u32[]{:S(2)}) %collective-permute-start.2) | collective-permute-done | bytes 231456 | tf_op jit(solution)/shard_map/ppermute | solution.py:281
  66.3 0.0 copy-start
  66.3 0.0 copy-start.1
  66.3 4.7 %collective-permute-start.3 = (bf16[2,113,8,128]{3,2,1,0:T(8,128)(2,1)S(1)}, bf16[2,113,8,128]{3,2,1,0:T(8,128)(2,1)S(1)}, u32[]{:S(2)}, u32[]{:S(2)}) collective-permute-start(bf16[2,113,8,128]{3,2,1,0:T(8,128)(2,1)S(1)} %pad_maximum_fusion), channel_id=1, source_target_pairs={{0,128},{16,912},{128,0},{144,272},{256,384},{272,144},{384,256},{... | collective-permute-start | bytes 1388552 | tf_op jit(solution)/shard_map/ppermute | solution.py:281
  71.0 0.0 copy-done.7
  71.0 0.0 copy-done
  71.0 0.0 copy-done.1
  71.1 1.4 shard_map.96
  72.4 5.4 %all-gather = bf16[384,384]{1,0:T(8,128)(2,1)S(1)} all-gather(bf16[96,384]{1,0:T(8,128)(2,1)S(1)} %get-tuple-element.17), channel_id=2, replica_groups=mesh['y'=8,'xh'=2,'xl'=2,'c'=2,'z'=16] {'xl','c'}, dimensions={0}, use_global_device_ids=true | all-gather | bytes 368640 | tf_op jit(solution)/shard_map/all_gather | solution.py:337
  77.8 0.0 collective-permute-done.3.refs_1_.refs_0_.refs_4_
  77.8 3.1 %collective-permute-start.4 = (bf16[2,113,8,128]{3,2,1,0:T(8,128)(2,1)S(1)}, bf16[2,113,8,128]{3,2,1,0:T(8,128)(2,1)S(1)}, u32[]{:S(2)}, u32[]{:S(2)}) collective-permute-start(bf16[2,113,8,128]{3,2,1,0:T(8,128)(2,1)S(1)} %collective-permute-done.3.refs_1_.refs_0_.refs_4_), channel_id=1, source_target_pairs={{0,896},{16,144},{128,256},{144,16},{256,128},{272,400},{384,512},... | collective-permute-start | bytes 1388552 | tf_op jit(solution)/shard_map/ppermute | solution.py:281
  80.9 1.2 shard_map.97
  82.1 7.8 %all-gather.1 = bf16[256,384]{1,0:T(8,128)(2,1)S(1)} all-gather(bf16[64,384]{1,0:T(8,128)(2,1)S(1)} %get-tuple-element.20), channel_id=3, replica_groups=mesh['y'=8,'xh'=2,'xl'=2,'c'=2,'z'=16] {'xl','c'}, dimensions={0}, use_global_device_ids=true | all-gather | bytes 245760 | tf_op jit(solution)/shard_map/all_gather | solution.py:337
  89.9 0.0 collective-permute-done.4.refs_1_.refs_5_
  89.9 1.4 shard_map.98
  91.2 6.1 %all-gather.2 = bf16[384,384]{1,0:T(8,128)(2,1)S(1)} all-gather(bf16[96,384]{1,0:T(8,128)(2,1)S(1)} %get-tuple-element.23), channel_id=4, replica_groups=mesh['y'=8,'xh'=2,'xl'=2,'c'=2,'z'=16] {'xl','c'}, dimensions={0}, use_global_device_ids=true | all-gather | bytes 368640 | tf_op jit(solution)/shard_map/all_gather | solution.py:337
  97.3 1.4 shard_map.99
  98.7 34.8 %all_to_all.16 = bf16[64,15,4,128]{3,2,1,0:T(4,128)(2,1)S(1)} all-to-all(bf16[64,15,4,128]{3,2,1,0:T(4,128)(2,1)S(1)} %get-tuple-element.27), channel_id=1, replica_groups=mesh['y'=8,'xh'=2,'xl'=2,'c'=2,'z'=16] {'y','xh','xl','c'}, dimensions={0} | all-to-all | bytes 1966080 | tf_op jit(solution)/shard_map/all_to_all | solution.py:364
  133.5 1.1 shard_map.100
  134.6 5.2 %all-to-all-start.2 = ((bf16[16,16,128]{2,1,0:T(8,128)(2,1)}), bf16[16,16,128]{2,1,0:T(8,128)(2,1)S(1)}, u32[]{:S(2)}, u32[]{:S(2)}) async-start(bf16[16,16,128]{2,1,0:T(8,128)(2,1)} %shard_map.100), calls=%async_computation.2 | async-start | bytes 131072 | tf_op jit(solution)/shard_map/all_to_all | solution.py:382
  139.8 0.0 copy-start.3
  139.9 2.3 %shard_map.102 = bf16[128,1792]{1,0:T(8,128)(2,1)} custom-call(s32[3]{0:T(128)S(1)} %pad_add_fusion.place, bf16[113,8,128]{2,1,0:T(8,128)(2,1)S(1)} %shard_map.95.refs_0_, bf16[113,8,128]{2,1,0:T(8,128)(2,1)S(1)} %collective-permute-done.1.refs_1_, bf16[113,8,128]{2,1,0:T(8,128)(2,1)S(1)} %collective-permute-done.refs_2_, ...), custom_call_target="tpu_custom_call" | custom-call | flops 268435456 | bytes 4194304 | tf_op jit(solution)/shard_map/pallas_call | solution.py:366
  142.1 9.3 %all-to-all-done.2.final = bf16[16,16,128]{2,1,0:T(8,128)(2,1)S(1)} async-done(((bf16[16,16,128]{2,1,0:T(8,128)(2,1)}), bf16[16,16,128]{2,1,0:T(8,128)(2,1)S(1)}, u32[]{:S(2)}, u32[]{:S(2)}) %all-to-all-start.2) | async-done | bytes 65568 | tf_op jit(solution)/shard_map/all_to_all | solution.py:382
  151.4 0.0 copy-done.3
  151.4 0.7 shard_map.101
  (1 shorter events, 0.0 us)
Async XLA Ops:
  0.6 0.7 copy-start.2
  1.3 0.7 copy-start.4
  2.0 0.7 copy-start.5
  2.7 0.7 copy-start.6
  50.5 20.6 %copy-start.7 = (bf16[1,128,1792]{2,1,0:T(8,128)(2,1)S(1)}, bf16[1,128,1792]{2,1,0:T(8,128)(2,1)}, u32[]{:S(2)}) copy-start(bf16[1,128,1792]{2,1,0:T(8,128)(2,1)} %param.13) | copy-start | bytes 1376260
  50.7 8.5 %collective-permute-start.1 = (bf16[113,8,128]{2,1,0:T(8,128)(2,1)S(1)}, bf16[113,8,128]{2,1,0:T(8,128)(2,1)S(1)}, u32[]{:S(2)}, u32[]{:S(2)}) collective-permute-start(bf16[113,8,128]{2,1,0:T(8,128)(2,1)S(1)} %shard_map.95.refs_0_), channel_id=1, source_target_pairs={{0,128},{16,912},{128,0},{144,272},{256,384},{272,144},{384,256},{... | collective-permute-start | bytes 694280 | tf_op jit(solution)/shard_map/ppermute | solution.py:281
  55.8 6.8 %collective-permute-start = (bf16[113,8,128]{2,1,0:T(8,128)(2,1)S(1)}, bf16[113,8,128]{2,1,0:T(8,128)(2,1)S(1)}, u32[]{:S(2)}, u32[]{:S(2)}) collective-permute-start(bf16[113,8,128]{2,1,0:T(8,128)(2,1)S(1)} %shard_map.95.refs_0_), channel_id=1, source_target_pairs={{0,896},{16,144},{128,256},{144,16},{256,128},{272,400},{384,512},... | collective-permute-start | bytes 694280 | tf_op jit(solution)/shard_map/ppermute | solution.py:281
  59.2 7.1 %collective-permute-start.2 = (bf16[113,8,128]{2,1,0:T(8,128)(2,1)S(1)}, bf16[113,8,128]{2,1,0:T(8,128)(2,1)S(1)}, u32[]{:S(2)}, u32[]{:S(2)}) collective-permute-start(bf16[113,8,128]{2,1,0:T(8,128)(2,1)S(1)} %collective-permute-done.1.refs_1_), channel_id=1, source_target_pairs={{0,896},{16,144},{128,256},{144,16},{256,128},{272,400},{384,512},... | collective-permute-start | bytes 694280 | tf_op jit(solution)/shard_map/ppermute | solution.py:281
  66.3 4.8 %copy-start = (bf16[1,1792,128]{2,1,0:T(8,128)(2,1)S(1)}, bf16[1,1792,128]{2,1,0:T(8,128)(2,1)}, u32[]{:S(2)}) copy-start(bf16[1,1792,128]{2,1,0:T(8,128)(2,1)} %param.11) | copy-start | bytes 1376260
  66.3 4.8 %copy-start.1 = (bf16[1,1792,128]{2,1,0:T(8,128)(2,1)S(1)}, bf16[1,1792,128]{2,1,0:T(8,128)(2,1)}, u32[]{:S(2)}) copy-start(bf16[1,1792,128]{2,1,0:T(8,128)(2,1)} %param.12) | copy-start | bytes 1376260
  66.3 11.5 %collective-permute-start.3 = (bf16[2,113,8,128]{3,2,1,0:T(8,128)(2,1)S(1)}, bf16[2,113,8,128]{3,2,1,0:T(8,128)(2,1)S(1)}, u32[]{:S(2)}, u32[]{:S(2)}) collective-permute-start(bf16[2,113,8,128]{3,2,1,0:T(8,128)(2,1)S(1)} %pad_maximum_fusion), channel_id=1, source_target_pairs={{0,128},{16,912},{128,0},{144,272},{256,384},{272,144},{384,256},{... | collective-permute-start | bytes 1388552 | tf_op jit(solution)/shard_map/ppermute | solution.py:281
  77.8 12.1 %collective-permute-start.4 = (bf16[2,113,8,128]{3,2,1,0:T(8,128)(2,1)S(1)}, bf16[2,113,8,128]{3,2,1,0:T(8,128)(2,1)S(1)}, u32[]{:S(2)}, u32[]{:S(2)}) collective-permute-start(bf16[2,113,8,128]{3,2,1,0:T(8,128)(2,1)S(1)} %collective-permute-done.3.refs_1_.refs_0_.refs_4_), channel_id=1, source_target_pairs={{0,896},{16,144},{128,256},{144,16},{256,128},{272,400},{384,512},... | collective-permute-start | bytes 1388552 | tf_op jit(solution)/shard_map/ppermute | solution.py:281
  134.6 16.8 %all-to-all-start.2 = ((bf16[16,16,128]{2,1,0:T(8,128)(2,1)}), bf16[16,16,128]{2,1,0:T(8,128)(2,1)S(1)}, u32[]{:S(2)}, u32[]{:S(2)}) async-start(bf16[16,16,128]{2,1,0:T(8,128)(2,1)} %shard_map.100), calls=%async_computation.2 | async-start | bytes 131072 | tf_op jit(solution)/shard_map/all_to_all | solution.py:382
  139.8 11.6 %copy-start.3 = (s32[4,8]{1,0:T(4,128)S(1)}, s32[4,8]{1,0:T(4,128)}, u32[]{:S(2)}) copy-start(s32[4,8]{1,0:T(4,128)} %ids.3) | copy-start | bytes 388

commit v9 on v8

--- a/solution.py
+++ b/solution.py
@@ -115,7 +115,14 @@
     block[tiles * per_y] = tags.astype(block.dtype)
 
 
-def part_kernel(picks, offsets, first, place, *refs):
+def position():
+    my_y = lax.axis_index("y")
+    expert = my_y * lax.axis_size("xh") + lax.axis_index("xh")
+    return my_y, expert, 1 - 2 * lax.rem(my_y + lax.axis_index("c"), 2)
+
+
+def part_kernel(picks, offsets, first, *refs):
+    place = position()
     *found, gate, up, down, part, weight, rows, spread = refs
     blocks = [found[i] if j is None else found[i].at[j] for i, j in picks]
     f32 = jnp.float32
@@ -139,7 +146,8 @@
     part[:, 2 * LANES :] = last_fours(out).astype(part.dtype)
 
 
-def grad_kernel(place, *refs):
+def grad_kernel(*refs):
+    place = position()
     *pieces, gate, up, back, wide, moved = refs
     f32, bf16 = jnp.float32, jnp.bfloat16
     quads, weights = pieces[: len(pieces) // 2], pieces[len(pieces) // 2 :]
@@ -194,7 +202,8 @@
     wide[...] = jnp.stack([even, odd], axis=1).reshape(pairs * 16, LANES).astype(bf16)
 
 
-def down_kernel(place, *refs):
+def down_kernel(*refs):
+    place = position()
     *found, wide, out, rows = refs
     blocks = [found[i] if j is None else found[i].at[j] for i, j in BLOCK_PICKS]
     lay_rows(place[2], blocks, BLOCK_OFFSETS, 0, rows)
@@ -249,8 +258,15 @@
     route_grad[...] = out
 
 
-def send_kernel(tokens, out_grad, weights, ids, send, acc):
+def send_kernel(*refs):
     f32 = jnp.float32
+    far, send, acc, near, sems = refs[:4], refs[4], refs[5], refs[6:10], refs[10]
+    copies = [pltpu.make_async_copy(a, b, sems.at[i]) for i, (a, b) in enumerate(zip(far, near))]
+    for copy in copies:
+        copy.start()
+    for copy in copies:
+        copy.wait()
+    tokens, out_grad, weights, ids = near
     toks, owners, sub = tokens.shape
     x_rows = tokens[...].astype(f32)
     g_rows = out_grad[...].astype(f32)
@@ -289,16 +305,18 @@
     per_y = nxh * OWNERS
     groups = ny * per_y
     tall = 2 * toks
-    my_y = lax.axis_index("y")
-    expert = my_y * nxh + lax.axis_index("xh")
-    turn = 1 - 2 * lax.rem(my_y + lax.axis_index("c"), 2)
-    place = jnp.stack([my_y, expert, turn]).astype(jnp.int32)
-
     send = call(
         send_kernel,
         jax.ShapeDtypeStruct((nxh * OWNERS, nz, tall, LANES), bf16),
-        whole(4),
-        [pltpu.VMEM((OWNERS + 1, tall, LANES), f32)],
+        [pl.BlockSpec(memory_space=pltpu.HBM)] * 4,
+        [
+            pltpu.VMEM((OWNERS + 1, tall, LANES), f32),
+            pltpu.VMEM(tokens.shape, bf16),
+            pltpu.VMEM(out_grad.shape, bf16),
+            pltpu.VMEM(route_weights.shape, bf16),
+            pltpu.VMEM(expert_ids.shape, jnp.int32),
+            pltpu.SemaphoreType.DMA((4,)),
+        ],
         per_y * nz * tall * LANES,
         1 << 19,
     )(tokens, out_grad, route_weights, expert_ids)
@@ -313,7 +331,6 @@
         groups * tall * LANES,
         1 << 19,
     )(got.reshape(per_y, nz, tall, LANES))
-    smem = pl.BlockSpec(memory_space=pltpu.SMEM)
     slots = groups * toks
     size = per_y * tall
     width = nz * sub
@@ -329,11 +346,11 @@
                 jax.ShapeDtypeStruct((n * per_y * toks, 3 * LANES), bf16),
                 jax.ShapeDtypeStruct((n * per_y * toks, LANES), f32),
             ),
-            [smem] + whole(len(used) + 3),
+            whole(len(used) + 3),
             [pltpu.VMEM((n * size, width), bf16), pltpu.VMEM((n * size, LANES), f32)],
             PART_FLOPS,
             4 << 20,
-        )(place, *[found[i] for i in used], w_gate[0], w_up[0], w_down[0])
+        )(*[found[i] for i in used], w_gate[0], w_up[0], w_down[0])
         return lax.all_gather(part, ("xl", "c"), axis=0, tiled=False), weight
 
     first = swap_with(block, True)
@@ -356,21 +373,21 @@
             jax.ShapeDtypeStruct((groups, tiles + 1, toks, LANES), bf16),
             jax.ShapeDtypeStruct((groups * tall, LANES), bf16),
         ),
-        [smem] + whole(8),
+        whole(8),
         [pltpu.VMEM((slots, 3 * LANES), bf16)],
         2 * slots * 2 * LANES * nz * LANES,
         3 << 20,
-    )(place, quad_a, quad_b, quad_c, weight_a, weight_b, weight_c, w_gate[0], w_up[0])
+    )(quad_a, quad_b, quad_c, weight_a, weight_b, weight_c, w_gate[0], w_up[0])
     landed = lax.all_to_all(back, ("y", "xh", "xl", "c"), 0, 0, tiled=True)
 
     down_grad = call(
         down_kernel,
         jax.ShapeDtypeStruct((LANES, nz * sub), bf16),
-        [smem] + whole(len(found) + 1),
+        whole(len(found) + 1),
         [pltpu.VMEM((groups * tall, width), bf16)],
         2 * groups * tall * nz * LANES * LANES,
         4 << 20,
-    )(place, *found, wide)
+    )(*found, wide)
     pieces = call(
         functools.partial(sum_kernel, sub),
         jax.ShapeDtypeStruct((nz, OWNERS * toks, LANES), bf16),

time: 154 us -> 153 us (level)
  Pallas kernels: 9.7 us -> 7.06 us
    pallas_call x3, Pallas kernels: 3.86 us -> 2.26 us  [partial_sums(): call(functools.partial(part_kernel, local, BLOCK_OFFSETS[low:high], first...]
  transfers between devices with their start and end apart: 6 -> 6, of which waited for: 4 -> 4; matrix products, arithmetic and copies ran while one was open for 0% -> 0% of each run, Pallas kernels for 3% -> 2%
where the time goes in v9:
time: 153 us; the launch traced here: 151 us
  blocking collectives  102 us (67%)
  starting transfers between devices  21.9 us (14%)
  waiting for transfers between devices  16.5 us (11%)
  Pallas kernels  7.06 us (5%)
  local copies, waits for them, and re-layouts  2.75 us (2%)
    all_to_all x1, blocking collectives, body(): got = lax.all_to_all(send, ('xh', 'xl', 'c', 'z'), 0, 0, tiled=True)  47 us
    all_to_all x1, blocking collectives, body(): landed = lax.all_to_all(back, ('y', 'xh', 'xl', 'c'), 0, 0, tiled=True)  34.8 us
    all_gather x3, blocking collectives, partial_sums(): return (lax.all_gather(part, ('xl', 'c'), axis=0, tiled=False), weight)  20.3 us
    ppermute x5, starting transfers between devices, swap_with(): return lax.ppermute(block, ('y', 'c'), hops)  16.7 us
    all_to_all x1, waiting for transfers between devices, body(): final = lax.all_to_all(pieces, 'z', 0, 0, tiled=True)  9.84 us
    ppermute x5, waiting for transfers between devices, swap_with(): return lax.ppermute(block, ('y', 'c'), hops)  6.65 us
    all_to_all x1, starting transfers between devices, body(): final = lax.all_to_all(pieces, 'z', 0, 0, tiled=True)  5.23 us
  transfers between devices with their start and end apart: 6, of which 4 were waited for; matrix products, arithmetic and copies ran while one was open for 0% of the time, Pallas kernels for 2%

profile of v9, /device:TPU:1, one launch (start us, length us, event | category | flops | bytes accessed | tf_op | source)
XLA Modules:
  0.0 151.1 jit_solution(14227412049797848475)
XLA Ops:
  0.6 0.0 copy-start.2
  0.6 0.7 copy-done.2
  1.3 0.0 copy-start.4
  1.3 0.7 copy-done.4
  2.0 0.0 copy-start.5
  2.0 0.7 copy-done.5
  2.7 0.0 copy-start.6
  2.7 0.7 copy-done.6
  3.4 0.2 shard_map.94
  3.5 47.0 %all_to_all.15 = bf16[128,8,128]{2,1,0:T(8,128)(2,1)S(1)} all-to-all(bf16[128,8,128]{2,1,0:T(8,128)(2,1)S(1)} %bitcast.15), channel_id=1, replica_groups=mesh['y'=8,'xh'=2,'xl'=2,'c'=2,'z'=16] {'xh','xl','c','z'}, dimensions={0} | all-to-all | bytes 524288 | tf_op jit(solution)/shard_map/all_to_all | solution.py:324
  50.5 0.0 copy-start.7
  50.5 0.2 shard_map.95.refs_0_
  50.7 5.1 %collective-permute-start.1 = (bf16[113,8,128]{2,1,0:T(8,128)(2,1)S(1)}, bf16[113,8,128]{2,1,0:T(8,128)(2,1)S(1)}, u32[]{:S(2)}, u32[]{:S(2)}) collective-permute-start(bf16[113,8,128]{2,1,0:T(8,128)(2,1)S(1)} %shard_map.95.refs_0_), channel_id=1, source_target_pairs={{0,128},{16,912},{128,0},{144,272},{256,384},{272,144},{384,256},{... | collective-permute-start | bytes 694280 | tf_op jit(solution)/shard_map/ppermute | solution.py:297
  55.8 1.9 %collective-permute-start = (bf16[113,8,128]{2,1,0:T(8,128)(2,1)S(1)}, bf16[113,8,128]{2,1,0:T(8,128)(2,1)S(1)}, u32[]{:S(2)}, u32[]{:S(2)}) collective-permute-start(bf16[113,8,128]{2,1,0:T(8,128)(2,1)S(1)} %shard_map.95.refs_0_), channel_id=1, source_target_pairs={{0,896},{16,144},{128,256},{144,16},{256,128},{272,400},{384,512},... | collective-permute-start | bytes 694280 | tf_op jit(solution)/shard_map/ppermute | solution.py:297
  57.8 1.5 collective-permute-done.1.refs_1_
  59.2 1.9 %collective-permute-start.2 = (bf16[113,8,128]{2,1,0:T(8,128)(2,1)S(1)}, bf16[113,8,128]{2,1,0:T(8,128)(2,1)S(1)}, u32[]{:S(2)}, u32[]{:S(2)}) collective-permute-start(bf16[113,8,128]{2,1,0:T(8,128)(2,1)S(1)} %collective-permute-done.1.refs_1_), channel_id=1, source_target_pairs={{0,896},{16,144},{128,256},{144,16},{256,128},{272,400},{384,512},... | collective-permute-start | bytes 694280 | tf_op jit(solution)/shard_map/ppermute | solution.py:297
  61.2 1.5 collective-permute-done.refs_2_
  62.6 3.7 %collective-permute-done.2.refs_0_.refs_3_ = bf16[113,8,128]{2,1,0:T(8,128)(2,1)S(1)} collective-permute-done((bf16[113,8,128]{2,1,0:T(8,128)(2,1)S(1)}, bf16[113,8,128]{2,1,0:T(8,128)(2,1)S(1)}, u32[]{:S(2)}, u32[]{:S(2)}) %collective-permute-start.2) | collective-permute-done | bytes 231456 | tf_op jit(solution)/shard_map/ppermute | solution.py:297
  66.3 0.0 copy-start
  66.3 0.0 copy-start.1
  66.4 4.7 %collective-permute-start.3 = (bf16[2,113,8,128]{3,2,1,0:T(8,128)(2,1)S(1)}, bf16[2,113,8,128]{3,2,1,0:T(8,128)(2,1)S(1)}, u32[]{:S(2)}, u32[]{:S(2)}) collective-permute-start(bf16[2,113,8,128]{3,2,1,0:T(8,128)(2,1)S(1)} %pad_maximum_fusion), channel_id=1, source_target_pairs={{0,128},{16,912},{128,0},{144,272},{256,384},{272,144},{384,256},{... | collective-permute-start | bytes 1388552 | tf_op jit(solution)/shard_map/ppermute | solution.py:297
  71.1 0.0 copy-done.7
  71.1 0.0 copy-done
  71.1 0.0 copy-done.1
  71.1 0.8 shard_map.96
  71.9 5.4 %all-gather = bf16[384,384]{1,0:T(8,128)(2,1)S(1)} all-gather(bf16[96,384]{1,0:T(8,128)(2,1)S(1)} %get-tuple-element.17), channel_id=2, replica_groups=mesh['y'=8,'xh'=2,'xl'=2,'c'=2,'z'=16] {'xl','c'}, dimensions={0}, use_global_device_ids=true | all-gather | bytes 368640 | tf_op jit(solution)/shard_map/all_gather | solution.py:354
  77.3 0.0 collective-permute-done.3.refs_1_.refs_0_.refs_4_
  77.3 3.1 %collective-permute-start.4 = (bf16[2,113,8,128]{3,2,1,0:T(8,128)(2,1)S(1)}, bf16[2,113,8,128]{3,2,1,0:T(8,128)(2,1)S(1)}, u32[]{:S(2)}, u32[]{:S(2)}) collective-permute-start(bf16[2,113,8,128]{3,2,1,0:T(8,128)(2,1)S(1)} %collective-permute-done.3.refs_1_.refs_0_.refs_4_), channel_id=1, source_target_pairs={{0,896},{16,144},{128,256},{144,16},{256,128},{272,400},{384,512},... | collective-permute-start | bytes 1388552 | tf_op jit(solution)/shard_map/ppermute | solution.py:297
  80.4 0.6 shard_map.97
  81.0 8.4 %all-gather.1 = bf16[256,384]{1,0:T(8,128)(2,1)S(1)} all-gather(bf16[64,384]{1,0:T(8,128)(2,1)S(1)} %get-tuple-element.20), channel_id=3, replica_groups=mesh['y'=8,'xh'=2,'xl'=2,'c'=2,'z'=16] {'xl','c'}, dimensions={0}, use_global_device_ids=true | all-gather | bytes 245760 | tf_op jit(solution)/shard_map/all_gather | solution.py:354
  89.4 0.0 collective-permute-done.4.refs_1_.refs_5_
  89.4 0.8 shard_map.98
  90.2 6.6 %all-gather.2 = bf16[384,384]{1,0:T(8,128)(2,1)S(1)} all-gather(bf16[96,384]{1,0:T(8,128)(2,1)S(1)} %get-tuple-element.23), channel_id=4, replica_groups=mesh['y'=8,'xh'=2,'xl'=2,'c'=2,'z'=16] {'xl','c'}, dimensions={0}, use_global_device_ids=true | all-gather | bytes 368640 | tf_op jit(solution)/shard_map/all_gather | solution.py:354
  96.8 0.9 shard_map.99
  97.7 34.8 %all_to_all.16 = bf16[64,15,4,128]{3,2,1,0:T(4,128)(2,1)S(1)} all-to-all(bf16[64,15,4,128]{3,2,1,0:T(4,128)(2,1)S(1)} %get-tuple-element.27), channel_id=1, replica_groups=mesh['y'=8,'xh'=2,'xl'=2,'c'=2,'z'=16] {'y','xh','xl','c'}, dimensions={0} | all-to-all | bytes 1966080 | tf_op jit(solution)/shard_map/all_to_all | solution.py:381
  132.5 1.1 shard_map.100
  133.6 5.2 %all-to-all-start.2 = ((bf16[16,16,128]{2,1,0:T(8,128)(2,1)}), bf16[16,16,128]{2,1,0:T(8,128)(2,1)S(1)}, u32[]{:S(2)}, u32[]{:S(2)}) async-start(bf16[16,16,128]{2,1,0:T(8,128)(2,1)} %shard_map.100), calls=%async_computation.2 | async-start | bytes 131072 | tf_op jit(solution)/shard_map/all_to_all | solution.py:399
  138.8 0.0 copy-start.3
  138.8 1.7 %shard_map.102 = bf16[128,1792]{1,0:T(8,128)(2,1)} custom-call(bf16[113,8,128]{2,1,0:T(8,128)(2,1)S(1)} %shard_map.95.refs_0_, bf16[113,8,128]{2,1,0:T(8,128)(2,1)S(1)} %collective-permute-done.1.refs_1_, bf16[113,8,128]{2,1,0:T(8,128)(2,1)S(1)} %collective-permute-done.refs_2_, bf16[113,8,128]{2,1,0:T(8,128)(2,1)S(1)} %collective-permute-done.2.refs_0_.refs_3_, ...), custom_call_target="tpu_custom_call" | custom-call | flops 268435456 | bytes 4194304 | tf_op jit(solution)/shard_map/pallas_call | solution.py:383
  140.6 9.8 %all-to-all-done.2.final = bf16[16,16,128]{2,1,0:T(8,128)(2,1)S(1)} async-done(((bf16[16,16,128]{2,1,0:T(8,128)(2,1)}), bf16[16,16,128]{2,1,0:T(8,128)(2,1)S(1)}, u32[]{:S(2)}, u32[]{:S(2)}) %all-to-all-start.2) | async-done | bytes 65568 | tf_op jit(solution)/shard_map/all_to_all | solution.py:399
  150.4 0.0 copy-done.3
  150.4 0.7 shard_map.101
  (1 shorter events, 0.0 us)
Async XLA Ops:
  0.6 0.7 copy-start.2
  1.3 0.7 copy-start.4
  2.0 0.7 copy-start.5
  2.7 0.7 copy-start.6
  50.5 20.6 %copy-start.7 = (bf16[1,128,1792]{2,1,0:T(8,128)(2,1)S(1)}, bf16[1,128,1792]{2,1,0:T(8,128)(2,1)}, u32[]{:S(2)}) copy-start(bf16[1,128,1792]{2,1,0:T(8,128)(2,1)} %param.13) | copy-start | bytes 1376260
  50.7 8.5 %collective-permute-start.1 = (bf16[113,8,128]{2,1,0:T(8,128)(2,1)S(1)}, bf16[113,8,128]{2,1,0:T(8,128)(2,1)S(1)}, u32[]{:S(2)}, u32[]{:S(2)}) collective-permute-start(bf16[113,8,128]{2,1,0:T(8,128)(2,1)S(1)} %shard_map.95.refs_0_), channel_id=1, source_target_pairs={{0,128},{16,912},{128,0},{144,272},{256,384},{272,144},{384,256},{... | collective-permute-start | bytes 694280 | tf_op jit(solution)/shard_map/ppermute | solution.py:297
  55.8 6.8 %collective-permute-start = (bf16[113,8,128]{2,1,0:T(8,128)(2,1)S(1)}, bf16[113,8,128]{2,1,0:T(8,128)(2,1)S(1)}, u32[]{:S(2)}, u32[]{:S(2)}) collective-permute-start(bf16[113,8,128]{2,1,0:T(8,128)(2,1)S(1)} %shard_map.95.refs_0_), channel_id=1, source_target_pairs={{0,896},{16,144},{128,256},{144,16},{256,128},{272,400},{384,512},... | collective-permute-start | bytes 694280 | tf_op jit(solution)/shard_map/ppermute | solution.py:297
  59.2 7.1 %collective-permute-start.2 = (bf16[113,8,128]{2,1,0:T(8,128)(2,1)S(1)}, bf16[113,8,128]{2,1,0:T(8,128)(2,1)S(1)}, u32[]{:S(2)}, u32[]{:S(2)}) collective-permute-start(bf16[113,8,128]{2,1,0:T(8,128)(2,1)S(1)} %collective-permute-done.1.refs_1_), channel_id=1, source_target_pairs={{0,896},{16,144},{128,256},{144,16},{256,128},{272,400},{384,512},... | collective-permute-start | bytes 694280 | tf_op jit(solution)/shard_map/ppermute | solution.py:297
  66.3 4.8 %copy-start = (bf16[1,1792,128]{2,1,0:T(8,128)(2,1)S(1)}, bf16[1,1792,128]{2,1,0:T(8,128)(2,1)}, u32[]{:S(2)}) copy-start(bf16[1,1792,128]{2,1,0:T(8,128)(2,1)} %param.11) | copy-start | bytes 1376260
  66.3 4.8 %copy-start.1 = (bf16[1,1792,128]{2,1,0:T(8,128)(2,1)S(1)}, bf16[1,1792,128]{2,1,0:T(8,128)(2,1)}, u32[]{:S(2)}) copy-start(bf16[1,1792,128]{2,1,0:T(8,128)(2,1)} %param.12) | copy-start | bytes 1376260
  66.4 10.9 %collective-permute-start.3 = (bf16[2,113,8,128]{3,2,1,0:T(8,128)(2,1)S(1)}, bf16[2,113,8,128]{3,2,1,0:T(8,128)(2,1)S(1)}, u32[]{:S(2)}, u32[]{:S(2)}) collective-permute-start(bf16[2,113,8,128]{3,2,1,0:T(8,128)(2,1)S(1)} %pad_maximum_fusion), channel_id=1, source_target_pairs={{0,128},{16,912},{128,0},{144,272},{256,384},{272,144},{384,256},{... | collective-permute-start | bytes 1388552 | tf_op jit(solution)/shard_map/ppermute | solution.py:297
  77.3 12.1 %collective-permute-start.4 = (bf16[2,113,8,128]{3,2,1,0:T(8,128)(2,1)S(1)}, bf16[2,113,8,128]{3,2,1,0:T(8,128)(2,1)S(1)}, u32[]{:S(2)}, u32[]{:S(2)}) collective-permute-start(bf16[2,113,8,128]{3,2,1,0:T(8,128)(2,1)S(1)} %collective-permute-done.3.refs_1_.refs_0_.refs_4_), channel_id=1, source_target_pairs={{0,896},{16,144},{128,256},{144,16},{256,128},{272,400},{384,512},... | collective-permute-start | bytes 1388552 | tf_op jit(solution)/shard_map/ppermute | solution.py:297
  133.6 16.8 %all-to-all-start.2 = ((bf16[16,16,128]{2,1,0:T(8,128)(2,1)}), bf16[16,16,128]{2,1,0:T(8,128)(2,1)S(1)}, u32[]{:S(2)}, u32[]{:S(2)}) async-start(bf16[16,16,128]{2,1,0:T(8,128)(2,1)} %shard_map.100), calls=%async_computation.2 | async-start | bytes 131072 | tf_op jit(solution)/shard_map/all_to_all | solution.py:399
  138.8 11.6 %copy-start.3 = (s32[4,8]{1,0:T(4,128)S(1)}, s32[4,8]{1,0:T(4,128)}, u32[]{:S(2)}) copy-start(s32[4,8]{1,0:T(4,128)} %ids.1) | copy-start | bytes 388

commit v10 on v9

--- a/solution.py
+++ b/solution.py
@@ -258,32 +258,10 @@
     route_grad[...] = out
 
 
-def send_kernel(*refs):
-    f32 = jnp.float32
-    far, send, acc, near, sems = refs[:4], refs[4], refs[5], refs[6:10], refs[10]
-    copies = [pltpu.make_async_copy(a, b, sems.at[i]) for i, (a, b) in enumerate(zip(far, near))]
-    for copy in copies:
-        copy.start()
-    for copy in copies:
-        copy.wait()
-    tokens, out_grad, weights, ids = near
-    toks, owners, sub = tokens.shape
-    x_rows = tokens[...].astype(f32)
-    g_rows = out_grad[...].astype(f32)
-    acc[...] = jnp.zeros_like(acc)
-    for q in range(owners):
-        acc[q, :toks, :sub] = x_rows[:, q, :]
-        acc[q, toks : 2 * toks, :sub] = g_rows[:, q, :]
-    route = weights[...].astype(f32)
-    lane = lax.broadcasted_iota(jnp.int32, (toks, LANES), 1) - sub
-    table = jnp.zeros((toks, LANES), f32)
-    for k in range(ids.shape[1]):
-        table = jnp.where(lane == ids[:, k : k + 1], route[:, k : k + 1], table)
-    acc[owners, :toks, :] = table
-    for q in range(owners):
-        tile = (acc[q] + acc[owners]).astype(send.dtype)
-        for top in range(q, send.shape[0], owners):
-            send[top] = jnp.broadcast_to(tile[None], send.shape[1:])
+def weight_table(expert_ids, route_weights, experts):
+    onehot = expert_ids[:, :, None] == jnp.arange(experts, dtype=jnp.int32)[None, None, :]
+    weights = jnp.where(onehot, route_weights.astype(jnp.float32)[:, :, None], 0.0)
+    return jnp.sum(weights, axis=1).astype(jnp.bfloat16)
 
 
 def swap_with(block, toward):
@@ -305,21 +283,13 @@
     per_y = nxh * OWNERS
     groups = ny * per_y
     tall = 2 * toks
-    send = call(
-        send_kernel,
-        jax.ShapeDtypeStruct((nxh * OWNERS, nz, tall, LANES), bf16),
-        [pl.BlockSpec(memory_space=pltpu.HBM)] * 4,
-        [
-            pltpu.VMEM((OWNERS + 1, tall, LANES), f32),
-            pltpu.VMEM(tokens.shape, bf16),
-            pltpu.VMEM(out_grad.shape, bf16),
-            pltpu.VMEM(route_weights.shape, bf16),
-            pltpu.VMEM(expert_ids.shape, jnp.int32),
-            pltpu.SemaphoreType.DMA((4,)),
-        ],
-        per_y * nz * tall * LANES,
-        1 << 19,
-    )(tokens, out_grad, route_weights, expert_ids)
+    table = weight_table(expert_ids, route_weights, experts)
+    x_rows = jnp.concatenate(
+        [tokens.transpose(1, 0, 2), jnp.broadcast_to(table[None], (OWNERS, toks, experts))], axis=2
+    )
+    g_rows = jnp.pad(out_grad.transpose(1, 0, 2), ((0, 0), (0, 0), (0, LANES - sub)))
+    send = jnp.concatenate([x_rows, g_rows], axis=1)
+    send = jnp.broadcast_to(send[None, :, None], (nxh, OWNERS, nz, tall, LANES))
     send = send.reshape(nxh * OWNERS * nz, tall, LANES)
     got = lax.all_to_all(send, ("xh", "xl", "c", "z"), 0, 0, tiled=True)
     tiles = nz * sub // LANES

time: 153 us -> 152 us (level)
  local copies, waits for them, and re-layouts: 2.75 us -> 0.74 us
    unnamed x16 -> x12, local copies, waits for them, and re-layouts: 2.75 us -> 0.63 us
where the time goes in v10:
time: 152 us; the launch traced here: 150 us
  blocking collectives  102 us (67%)
  starting transfers between devices  21.9 us (14%)
  waiting for transfers between devices  16.5 us (11%)
  Pallas kernels  6.88 us (5%)
    all_to_all x1, blocking collectives, body(): got = lax.all_to_all(send, ('xh', 'xl', 'c', 'z'), 0, 0, tiled=True)  47 us
    all_to_all x1, blocking collectives, body(): landed = lax.all_to_all(back, ('y', 'xh', 'xl', 'c'), 0, 0, tiled=True)  34.8 us
    all_gather x3, blocking collectives, partial_sums(): return (lax.all_gather(part, ('xl', 'c'), axis=0, tiled=False), weight)  20.3 us
    ppermute x5, starting transfers between devices, swap_with(): return lax.ppermute(block, ('y', 'c'), hops)  16.7 us
    all_to_all x1, waiting for transfers between devices, body(): final = lax.all_to_all(pieces, 'z', 0, 0, tiled=True)  9.85 us
    ppermute x5, waiting for transfers between devices, swap_with(): return lax.ppermute(block, ('y', 'c'), hops)  6.65 us
    all_to_all x1, starting transfers between devices, body(): final = lax.all_to_all(pieces, 'z', 0, 0, tiled=True)  5.23 us
  transfers between devices with their start and end apart: 6, of which 4 were waited for; matrix products, arithmetic and copies ran while one was open for 0% of the time, Pallas kernels for 2%

profile of v10, /device:TPU:1, one launch (start us, length us, event | category | flops | bytes accessed | tf_op | source)
XLA Modules:
  0.0 149.8 jit_solution(6477081330340897867)
XLA Ops:
  0.6 0.0 copy-start.2
  0.6 0.7 convert_element_type.12
  1.3 0.0 copy-done.2
  1.3 0.0 copy-start.5
  1.3 0.1 select_reduce_fusion
  1.4 0.0 copy-start.4
  1.4 0.1 pad.8.clone
  1.5 0.5 copy-done.5
  2.0 0.1 copy-done.4
  2.2 47.0 %all_to_all.15 = bf16[128,8,128]{2,1,0:T(8,128)(2,1)S(1)} all-to-all(bf16[128,8,128]{2,1,0:T(8,128)(2,1)S(1)} %bitcast.32), channel_id=1, replica_groups=mesh['y'=8,'xh'=2,'xl'=2,'c'=2,'z'=16] {'xh','xl','c','z'}, dimensions={0} | all-to-all | bytes 524288 | tf_op jit(solution)/shard_map/all_to_all | solution.py:294
  49.2 0.0 copy-start.3
  49.2 0.2 shard_map.94.refs_0_
  49.4 5.1 %collective-permute-start.1 = (bf16[113,8,128]{2,1,0:T(8,128)(2,1)S(1)}, bf16[113,8,128]{2,1,0:T(8,128)(2,1)S(1)}, u32[]{:S(2)}, u32[]{:S(2)}) collective-permute-start(bf16[113,8,128]{2,1,0:T(8,128)(2,1)S(1)} %shard_map.94.refs_0_), channel_id=1, source_target_pairs={{0,128},{16,912},{128,0},{144,272},{256,384},{272,144},{384,256},{... | collective-permute-start | bytes 694280 | tf_op jit(solution)/shard_map/ppermute | solution.py:275
  54.5 1.9 %collective-permute-start = (bf16[113,8,128]{2,1,0:T(8,128)(2,1)S(1)}, bf16[113,8,128]{2,1,0:T(8,128)(2,1)S(1)}, u32[]{:S(2)}, u32[]{:S(2)}) collective-permute-start(bf16[113,8,128]{2,1,0:T(8,128)(2,1)S(1)} %shard_map.94.refs_0_), channel_id=1, source_target_pairs={{0,896},{16,144},{128,256},{144,16},{256,128},{272,400},{384,512},... | collective-permute-start | bytes 694280 | tf_op jit(solution)/shard_map/ppermute | solution.py:275
  56.4 1.5 collective-permute-done.1.refs_1_
  57.9 1.9 %collective-permute-start.2 = (bf16[113,8,128]{2,1,0:T(8,128)(2,1)S(1)}, bf16[113,8,128]{2,1,0:T(8,128)(2,1)S(1)}, u32[]{:S(2)}, u32[]{:S(2)}) collective-permute-start(bf16[113,8,128]{2,1,0:T(8,128)(2,1)S(1)} %collective-permute-done.1.refs_1_), channel_id=1, source_target_pairs={{0,896},{16,144},{128,256},{144,16},{256,128},{272,400},{384,512},... | collective-permute-start | bytes 694280 | tf_op jit(solution)/shard_map/ppermute | solution.py:275
  59.8 1.5 collective-permute-done.refs_2_
  61.3 3.7 %collective-permute-done.2.refs_0_.refs_3_ = bf16[113,8,128]{2,1,0:T(8,128)(2,1)S(1)} collective-permute-done((bf16[113,8,128]{2,1,0:T(8,128)(2,1)S(1)}, bf16[113,8,128]{2,1,0:T(8,128)(2,1)S(1)}, u32[]{:S(2)}, u32[]{:S(2)}) %collective-permute-start.2) | collective-permute-done | bytes 231456 | tf_op jit(solution)/shard_map/ppermute | solution.py:275
  65.0 0.0 copy-start
  65.0 0.0 copy-start.1
  65.0 4.7 %collective-permute-start.3 = (bf16[2,113,8,128]{3,2,1,0:T(8,128)(2,1)S(1)}, bf16[2,113,8,128]{3,2,1,0:T(8,128)(2,1)S(1)}, u32[]{:S(2)}, u32[]{:S(2)}) collective-permute-start(bf16[2,113,8,128]{3,2,1,0:T(8,128)(2,1)S(1)} %pad_maximum_fusion), channel_id=1, source_target_pairs={{0,128},{16,912},{128,0},{144,272},{256,384},{272,144},{384,256},{... | collective-permute-start | bytes 1388552 | tf_op jit(solution)/shard_map/ppermute | solution.py:275
  69.7 0.0 copy-done.3
  69.7 0.0 copy-done
  69.7 0.0 copy-done.1
  69.8 0.8 shard_map.95
  70.6 5.4 %all-gather = bf16[384,384]{1,0:T(8,128)(2,1)S(1)} all-gather(bf16[96,384]{1,0:T(8,128)(2,1)S(1)} %get-tuple-element.17), channel_id=2, replica_groups=mesh['y'=8,'xh'=2,'xl'=2,'c'=2,'z'=16] {'xl','c'}, dimensions={0}, use_global_device_ids=true | all-gather | bytes 368640 | tf_op jit(solution)/shard_map/all_gather | solution.py:324
  76.0 0.0 collective-permute-done.3.refs_1_.refs_0_.refs_4_
  76.0 3.1 %collective-permute-start.4 = (bf16[2,113,8,128]{3,2,1,0:T(8,128)(2,1)S(1)}, bf16[2,113,8,128]{3,2,1,0:T(8,128)(2,1)S(1)}, u32[]{:S(2)}, u32[]{:S(2)}) collective-permute-start(bf16[2,113,8,128]{3,2,1,0:T(8,128)(2,1)S(1)} %collective-permute-done.3.refs_1_.refs_0_.refs_4_), channel_id=1, source_target_pairs={{0,896},{16,144},{128,256},{144,16},{256,128},{272,400},{384,512},... | collective-permute-start | bytes 1388552 | tf_op jit(solution)/shard_map/ppermute | solution.py:275
  79.0 0.6 shard_map.96
  79.7 8.4 %all-gather.1 = bf16[256,384]{1,0:T(8,128)(2,1)S(1)} all-gather(bf16[64,384]{1,0:T(8,128)(2,1)S(1)} %get-tuple-element.20), channel_id=3, replica_groups=mesh['y'=8,'xh'=2,'xl'=2,'c'=2,'z'=16] {'xl','c'}, dimensions={0}, use_global_device_ids=true | all-gather | bytes 245760 | tf_op jit(solution)/shard_map/all_gather | solution.py:324
  88.0 0.0 collective-permute-done.4.refs_1_.refs_5_
  88.1 0.8 shard_map.97
  88.9 6.6 %all-gather.2 = bf16[384,384]{1,0:T(8,128)(2,1)S(1)} all-gather(bf16[96,384]{1,0:T(8,128)(2,1)S(1)} %get-tuple-element.23), channel_id=4, replica_groups=mesh['y'=8,'xh'=2,'xl'=2,'c'=2,'z'=16] {'xl','c'}, dimensions={0}, use_global_device_ids=true | all-gather | bytes 368640 | tf_op jit(solution)/shard_map/all_gather | solution.py:324
  95.5 0.9 shard_map.98
  96.3 34.8 %all_to_all.16 = bf16[64,15,4,128]{3,2,1,0:T(4,128)(2,1)S(1)} all-to-all(bf16[64,15,4,128]{3,2,1,0:T(4,128)(2,1)S(1)} %get-tuple-element.27), channel_id=1, replica_groups=mesh['y'=8,'xh'=2,'xl'=2,'c'=2,'z'=16] {'y','xh','xl','c'}, dimensions={0} | all-to-all | bytes 1966080 | tf_op jit(solution)/shard_map/all_to_all | solution.py:351
  131.1 1.1 shard_map.99
  132.2 5.2 %all-to-all-start.2 = ((bf16[16,16,128]{2,1,0:T(8,128)(2,1)}), bf16[16,16,128]{2,1,0:T(8,128)(2,1)S(1)}, u32[]{:S(2)}, u32[]{:S(2)}) async-start(bf16[16,16,128]{2,1,0:T(8,128)(2,1)} %shard_map.99), calls=%async_computation.2 | async-start | bytes 131072 | tf_op jit(solution)/shard_map/all_to_all | solution.py:369
  137.4 1.7 %shard_map.101 = bf16[128,1792]{1,0:T(8,128)(2,1)} custom-call(bf16[113,8,128]{2,1,0:T(8,128)(2,1)S(1)} %shard_map.94.refs_0_, bf16[113,8,128]{2,1,0:T(8,128)(2,1)S(1)} %collective-permute-done.1.refs_1_, bf16[113,8,128]{2,1,0:T(8,128)(2,1)S(1)} %collective-permute-done.refs_2_, bf16[113,8,128]{2,1,0:T(8,128)(2,1)S(1)} %collective-permute-done.2.refs_0_.refs_3_, ...), custom_call_target="tpu_custom_call" | custom-call | flops 268435456 | bytes 4194304 | tf_op jit(solution)/shard_map/pallas_call | solution.py:353
  139.2 9.8 %all-to-all-done.2.final = bf16[16,16,128]{2,1,0:T(8,128)(2,1)S(1)} async-done(((bf16[16,16,128]{2,1,0:T(8,128)(2,1)}), bf16[16,16,128]{2,1,0:T(8,128)(2,1)S(1)}, u32[]{:S(2)}, u32[]{:S(2)}) %all-to-all-start.2) | async-done | bytes 65568 | tf_op jit(solution)/shard_map/all_to_all | solution.py:369
  149.0 0.7 shard_map.100
  (4 shorter events, 0.1 us)
Async XLA Ops:
  0.6 0.7 copy-start.2
  1.3 0.7 copy-start.5
  1.4 0.7 copy-start.4
  49.2 20.6 %copy-start.3 = (bf16[1,128,1792]{2,1,0:T(8,128)(2,1)S(1)}, bf16[1,128,1792]{2,1,0:T(8,128)(2,1)}, u32[]{:S(2)}) copy-start(bf16[1,128,1792]{2,1,0:T(8,128)(2,1)} %param.13) | copy-start | bytes 1376260
  49.4 8.5 %collective-permute-start.1 = (bf16[113,8,128]{2,1,0:T(8,128)(2,1)S(1)}, bf16[113,8,128]{2,1,0:T(8,128)(2,1)S(1)}, u32[]{:S(2)}, u32[]{:S(2)}) collective-permute-start(bf16[113,8,128]{2,1,0:T(8,128)(2,1)S(1)} %shard_map.94.refs_0_), channel_id=1, source_target_pairs={{0,128},{16,912},{128,0},{144,272},{256,384},{272,144},{384,256},{... | collective-permute-start | bytes 694280 | tf_op jit(solution)/shard_map/ppermute | solution.py:275
  54.5 6.8 %collective-permute-start = (bf16[113,8,128]{2,1,0:T(8,128)(2,1)S(1)}, bf16[113,8,128]{2,1,0:T(8,128)(2,1)S(1)}, u32[]{:S(2)}, u32[]{:S(2)}) collective-permute-start(bf16[113,8,128]{2,1,0:T(8,128)(2,1)S(1)} %shard_map.94.refs_0_), channel_id=1, source_target_pairs={{0,896},{16,144},{128,256},{144,16},{256,128},{272,400},{384,512},... | collective-permute-start | bytes 694280 | tf_op jit(solution)/shard_map/ppermute | solution.py:275
  57.9 7.1 %collective-permute-start.2 = (bf16[113,8,128]{2,1,0:T(8,128)(2,1)S(1)}, bf16[113,8,128]{2,1,0:T(8,128)(2,1)S(1)}, u32[]{:S(2)}, u32[]{:S(2)}) collective-permute-start(bf16[113,8,128]{2,1,0:T(8,128)(2,1)S(1)} %collective-permute-done.1.refs_1_), channel_id=1, source_target_pairs={{0,896},{16,144},{128,256},{144,16},{256,128},{272,400},{384,512},... | collective-permute-start | bytes 694280 | tf_op jit(solution)/shard_map/ppermute | solution.py:275
  65.0 4.8 %copy-start = (bf16[1,1792,128]{2,1,0:T(8,128)(2,1)S(1)}, bf16[1,1792,128]{2,1,0:T(8,128)(2,1)}, u32[]{:S(2)}) copy-start(bf16[1,1792,128]{2,1,0:T(8,128)(2,1)} %param.11) | copy-start | bytes 1376260
  65.0 4.8 %copy-start.1 = (bf16[1,1792,128]{2,1,0:T(8,128)(2,1)S(1)}, bf16[1,1792,128]{2,1,0:T(8,128)(2,1)}, u32[]{:S(2)}) copy-start(bf16[1,1792,128]{2,1,0:T(8,128)(2,1)} %param.12) | copy-start | bytes 1376260
  65.0 10.9 %collective-permute-start.3 = (bf16[2,113,8,128]{3,2,1,0:T(8,128)(2,1)S(1)}, bf16[2,113,8,128]{3,2,1,0:T(8,128)(2,1)S(1)}, u32[]{:S(2)}, u32[]{:S(2)}) collective-permute-start(bf16[2,113,8,128]{3,2,1,0:T(8,128)(2,1)S(1)} %pad_maximum_fusion), channel_id=1, source_target_pairs={{0,128},{16,912},{128,0},{144,272},{256,384},{272,144},{384,256},{... | collective-permute-start | bytes 1388552 | tf_op jit(solution)/shard_map/ppermute | solution.py:275
  76.0 12.1 %collective-permute-start.4 = (bf16[2,113,8,128]{3,2,1,0:T(8,128)(2,1)S(1)}, bf16[2,113,8,128]{3,2,1,0:T(8,128)(2,1)S(1)}, u32[]{:S(2)}, u32[]{:S(2)}) collective-permute-start(bf16[2,113,8,128]{3,2,1,0:T(8,128)(2,1)S(1)} %collective-permute-done.3.refs_1_.refs_0_.refs_4_), channel_id=1, source_target_pairs={{0,896},{16,144},{128,256},{144,16},{256,128},{272,400},{384,512},... | collective-permute-start | bytes 1388552 | tf_op jit(solution)/shard_map/ppermute | solution.py:275
  132.2 16.8 %all-to-all-start.2 = ((bf16[16,16,128]{2,1,0:T(8,128)(2,1)}), bf16[16,16,128]{2,1,0:T(8,128)(2,1)S(1)}, u32[]{:S(2)}, u32[]{:S(2)}) async-start(bf16[16,16,128]{2,1,0:T(8,128)(2,1)} %shard_map.99), calls=%async_computation.2 | async-start | bytes 131072 | tf_op jit(solution)/shard_map/all_to_all | solution.py:369
